TPU v7x, 256 devices: a whole 4x4x8 slice. The times are simulated.
256 devices in a mesh: sec: 32 (over x, y, core), tp: 8 (over z).
Axes of the slice: x: 4, y: 4, z: 8, core: 2. Of those that a mesh axis runs over, the one named last changes fastest.
Arguments:
- encoded: bfloat16 [16384, 4096], P('sec', 'tp'), may hold values from -9 to 9
- decoder_states: bfloat16 [512, 4096], P(None, 'tp'), may hold values from -10 to 10
- passage_counts: int32 [8], replicated, may hold values from 1 to 16, 64 in all
- enc_gain: float32 [4096], replicated, may hold values from 0.25 to 1.75
- dec_gain: float32 [4096], replicated, may hold values from 0.25 to 1.75
- w_key: bfloat16 [4096, 4096], P('sec', 'tp'), may hold values from -1 to 1
- w_value: bfloat16 [4096, 4096], P('sec', 'tp'), may hold values from -0.09375 to 0.09375
- w_query: bfloat16 [4096, 4096], P('sec', 'tp'), may hold values from -1 to 1
- w_out: bfloat16 [4096, 4096], P('tp', 'sec'), may hold values from -0.09375 to 0.09375
Outputs:
- decoded: bfloat16 [512, 4096], P(None, 'tp')
- passage_scores: float32 [64], P('sec')
Inputs may be any that keep to these rules, and one draw needn't show every extreme that they name: `passage_counts`: every question has at least one passage; the counts sum to 64, the largest is exactly 16.
All inputs are finite; a program needn't handle non-finite values.
Results may differ from a plain program's by a relative error of at most 0.015.
Values may be sent and summed in bfloat16 or wider, within the bound.
No kernel may reach another device: no remote copies, remote signals or barrier semaphores. Data moves between devices by JAX's collectives and lax.ppermute only.
A program may use at most 128 MiB of HBM per device.

v0:
```python
import jax
import jax.numpy as jnp
from jax import lax
from jax.sharding import PartitionSpec as P

HEADS = 64
HEAD_DIM = 64
PTOK = 256
QTOK = 64


def combined_all(x, axis, combine):
    everything = jax.tree.map(lambda part: lax.all_gather(part, axis), x)
    initial = jax.tree.map(lambda part: part[0], everything)

    def lap(k, so_far):
        return combine(so_far, jax.tree.map(lambda part: part[k], everything))

    return lax.fori_loop(1, lax.axis_size(axis), lap, initial)


def rms_norm(states, gain):
    values = states.astype(jnp.float32)
    scale = lax.rsqrt(jnp.mean(values * values, axis=-1, keepdims=True) + 1e-06)
    return (values * scale * gain).astype(jnp.bfloat16)


def on_device(
    encoded, decoder_states, passage_counts, enc_gain, dec_gain, w_key, w_value, w_query, w_out
):
    rows_local = encoded.shape[0]
    pass_local = rows_local // PTOK
    qrows = decoder_states.shape[0]
    local_heads = w_key.shape[1] // HEAD_DIM
    local_inner = local_heads * HEAD_DIM
    sec_index = lax.axis_index("sec")
    questions = qrows // QTOK
    window_questions = min(pass_local, questions)
    window_rows = window_questions * QTOK
    full_enc = lax.all_gather(encoded, "tp", axis=1, tiled=True)
    key_rows, value_rows, query_rows = (
        lax.all_gather(w_key, "sec", axis=0, tiled=True),
        lax.all_gather(w_value, "sec", axis=0, tiled=True),
        lax.all_gather(w_query, "sec", axis=0, tiled=True),
    )
    enc_normed = rms_norm(full_enc, enc_gain)
    keys = jnp.dot(enc_normed, key_rows, preferred_element_type=jnp.float32).astype(jnp.bfloat16)
    values = jnp.dot(enc_normed, value_rows, preferred_element_type=jnp.float32).astype(
        jnp.bfloat16
    )
    ends = jnp.cumsum(passage_counts)
    slot_ids = sec_index * pass_local + jnp.arange(pass_local, dtype=jnp.int32)
    slot_owner = jnp.sum((slot_ids[:, None] >= ends[None, :]).astype(jnp.int32), axis=1)
    first_question = jnp.minimum(slot_owner[0], questions - window_questions)
    first_row = first_question * QTOK
    own_rows = lax.dynamic_slice_in_dim(decoder_states, first_row, window_rows, 0)
    full_dec = lax.all_gather(own_rows, "tp", axis=1, tiled=True)
    queries = jnp.dot(
        rms_norm(full_dec, dec_gain), query_rows, preferred_element_type=jnp.float32
    ).astype(jnp.bfloat16)
    key_owner = jnp.repeat(slot_owner, PTOK)
    query_owner = first_question + jnp.arange(window_rows, dtype=jnp.int32) // QTOK
    mask = (query_owner[:, None] == key_owner[None, :])[None, :, :]
    query_heads = queries.reshape(window_rows, local_heads, HEAD_DIM)
    key_heads = keys.reshape(rows_local, local_heads, HEAD_DIM)
    value_heads = values.reshape(rows_local, local_heads, HEAD_DIM)
    scores = jnp.einsum("thd,khd->htk", query_heads, key_heads, preferred_element_type=jnp.float32)
    scores = jnp.where(mask, scores, jnp.float32(-1e30))
    local_top = jnp.max(scores, axis=2)
    weights = jnp.where(mask, jnp.exp(scores - local_top[:, :, None]), jnp.float32(0.0))
    local_total = jnp.sum(weights, axis=2)
    weighted = jnp.einsum(
        "htk,khd->thd",
        weights.astype(jnp.bfloat16),
        value_heads,
        preferred_element_type=jnp.float32,
    )
    weighted = weighted.reshape(window_rows, local_inner)
    top_rows = lax.dynamic_update_slice_in_dim(
        jnp.full((qrows, local_heads), -1e30, jnp.float32), local_top.T, first_row, 0
    )
    total_rows = lax.dynamic_update_slice_in_dim(
        jnp.zeros((qrows, local_heads), jnp.float32), local_total.T, first_row, 0
    )
    sum_rows = lax.dynamic_update_slice_in_dim(
        jnp.zeros((qrows, local_inner), jnp.float32), weighted, first_row, 0
    )

    def combine(first, second):
        top_a, total_a, sums_a = first
        top_b, total_b, sums_b = second
        upper = jnp.maximum(top_a, top_b)
        factor_a = jnp.exp(top_a - upper)
        factor_b = jnp.exp(top_b - upper)
        merged_sums = sums_a * jnp.repeat(factor_a, HEAD_DIM, axis=1) + sums_b * jnp.repeat(
            factor_b, HEAD_DIM, axis=1
        )
        return (upper, total_a * factor_a + total_b * factor_b, merged_sums)

    global_top, global_total, global_sums = combined_all(
        (top_rows, total_rows, sum_rows), "sec", combine
    )
    window_top = lax.dynamic_slice_in_dim(global_top, first_row, window_rows, 0)
    window_total = lax.dynamic_slice_in_dim(global_total, first_row, window_rows, 0)
    per_slot = jnp.sum(weights.reshape(local_heads, window_rows, pass_local, PTOK), axis=3)
    rescale = (jnp.exp(local_top.T - window_top) / window_total).T
    slot_sum = jnp.sum(per_slot * rescale[:, :, None], axis=(0, 1))
    passage_scores = lax.psum(slot_sum, "tp") / (HEADS * QTOK)
    context = (global_sums / jnp.repeat(global_total, HEAD_DIM, axis=1)).astype(jnp.bfloat16)
    terms = jnp.dot(
        context,
        lax.all_gather(w_out, "sec", axis=1, tiled=True),
        preferred_element_type=jnp.float32,
    )
    cross = lax.psum_scatter(
        terms.astype(jnp.bfloat16), "tp", scatter_dimension=1, tiled=True
    ).astype(jnp.float32)
    decoded = (decoder_states.astype(jnp.float32) + cross).astype(jnp.bfloat16)
    return (decoded, passage_scores)


def solution(mesh):
    placed = (
        P("sec", "tp"),
        P(None, "tp"),
        P(),
        P(),
        P(),
        P("sec", "tp"),
        P("sec", "tp"),
        P("sec", "tp"),
        P("tp", "sec"),
    )
    return jax.shard_map(
        on_device, mesh=mesh, in_specs=placed, out_specs=(P(None, "tp"), P("sec")), check_vma=False
    )
```

profile of v0, /device:TPU:1, one launch (start us, length us, event | category | flops | bytes accessed | tf_op | source)
XLA Modules:
  0.0 555.8 jit_solution(10406211442104568692)
XLA Ops:
  8.3 1.6 constant_dynamic-slice_fusion.1
  12.8 35.0 %all-gather.8.cloned.1.call-done = bf16[128,4096]{1,0:T(8,128)(2,1)} async-done(((bf16[128,512]{1,0:T(8,128)(2,1)}), bf16[128,4096]{1,0:T(8,128)(2,1)}) %all-gather.8.cloned.1.call-update) | async-done | bytes 1048592 | tf_op jit(solution)/shard_map/all_gather | solution.py:57
  47.8 1.6 fusion.6
  49.4 58.5 %all-gather.12.cloned.1.call-done = bf16[512,4096]{1,0:T(8,128)(2,1)} async-done(((bf16[512,512]{1,0:T(8,128)(2,1)}), bf16[512,4096]{1,0:T(8,128)(2,1)}) %all-gather.12.cloned.1.call-update) | async-done | bytes 4194320 | tf_op jit(solution)/shard_map/all_gather | solution.py:40
  107.9 3.1 fusion.3
  111.0 49.6 %all-gather.10.cloned.1.call-done = bf16[4096,512]{1,0:T(8,128)(2,1)} async-done(((bf16[128,512]{1,0:T(8,128)(2,1)}), bf16[4096,512]{1,0:T(8,128)(2,1)}) %all-gather.10.cloned.1.call-update) | async-done | bytes 4194320 | tf_op jit(solution)/shard_map/all_gather | solution.py:44
  160.6 2.9 convolution_convert_fusion.3
  163.7 49.9 %all-gather.14.cloned.1.call-done = bf16[4096,512]{1,0:T(8,128)(2,1)} async-done(((bf16[128,512]{1,0:T(8,128)(2,1)}), bf16[4096,512]{1,0:T(8,128)(2,1)}) %all-gather.14.cloned.1.call-update) | async-done | bytes 4194320 | tf_op jit(solution)/shard_map/all_gather | solution.py:42
  213.6 5.9 %convolution_convert_fusion.2 = bf16[512,512]{0,1:T(8,128)(2,1)S(1)} fusion(bf16[4096,512]{1,0:T(8,128)(2,1)} %all-gather.14.cloned.1.call-done, bf16[512,4096]{1,0:T(8,128)(2,1)} %all-gather.12.cloned.1.call-done, f32[4096]{0:T(1024)S(1)} %copy-done.6, f32[512]{0:T(512)S(1)} %add_rsqrt_fusion), kind=kOutput, calls=%fused_computation.24 | convolution fusion | flops 2156134400 | bytes 8931328 | tf_op jit(solution)/shard_map/dot_general | solution.py:47
  220.8 45.8 %all-gather.16.cloned.1.call-done = bf16[4096,512]{1,0:T(8,128)(2,1)} async-done(((bf16[128,512]{1,0:T(8,128)(2,1)}), bf16[4096,512]{1,0:T(8,128)(2,1)}) %all-gather.16.cloned.1.call-update) | async-done | bytes 4194320 | tf_op jit(solution)/shard_map/all_gather | solution.py:43
  266.5 5.9 %convolution_convert_fusion.1 = bf16[512,512]{0,1:T(8,128)(2,1)S(1)} fusion(bf16[4096,512]{1,0:T(8,128)(2,1)} %all-gather.16.cloned.1.call-done, bf16[512,4096]{1,0:T(8,128)(2,1)} %all-gather.12.cloned.1.call-done, f32[4096]{0:T(1024)S(1)} %copy-done.6, f32[512]{0:T(512)S(1)} %add_rsqrt_fusion), kind=kOutput, calls=%fused_computation.23 | convolution fusion | flops 2156134400 | bytes 8931328 | tf_op jit(solution)/shard_map/dot_general | solution.py:48
  275.4 26.7 %all_gather.43 = f32[32,512,8]{1,2,0:T(8,128)} all-gather(f32[1,512,8]{1,2,0:T(8,128)S(1)} %dynamic_update_slice.13), channel_id=1, replica_groups=mesh['sec'=32,'tp'=8] {'sec'}, dimensions={0}, use_global_device_ids=true | all-gather | bytes 540672 | tf_op jit(solution)/shard_map/all_gather | solution.py:13
  303.0 25.1 %all_gather.41 = f32[32,512,8]{1,2,0:T(8,128)} all-gather(f32[1,512,8]{1,2,0:T(8,128)S(1)} %dynamic_update_slice.12), channel_id=1, replica_groups=mesh['sec'=32,'tp'=8] {'sec'}, dimensions={0}, use_global_device_ids=true | all-gather | bytes 540672 | tf_op jit(solution)/shard_map/all_gather | solution.py:13
  328.8 65.4 %all-gather.18.cloned.1.call-done = f32[32,512,512]{2,1,0:T(8,128)} async-done(((f32[1,512,512]{2,1,0:T(8,128)}), f32[32,512,512]{2,1,0:T(8,128)}) %all-gather.18.cloned.1.call-update) | async-done | bytes 33554448 | tf_op jit(solution)/shard_map/all_gather | solution.py:13
  395.8 90.0 %while.19 = (s32[]{:T(128)}, f32[512,8]{0,1:T(8,128)S(1)}, f32[512,8]{0,1:T(8,128)S(1)}, f32[512,512]{0,1:T(8,128)S(1)}, f32[32,512,8]{1,2,0:T(8,128)}, /*index=...) while((s32[]{:T(128)}, f32[512,8]{0,1:T(8,128)S(1)}, ...), condition=%wide.region_7.8_spmd, body=%wide.region_6.7_spmd.sunk | while | flops 811013 | bytes 7504023 | solution.py:19
  437.2 1.5 constant_dynamic-slice_fusion.3
  443.1 1.4 constant_dynamic-slice_fusion.3
  486.0 6.5 %convolution_convert_fusion = bf16[512,4096]{1,0:T(8,128)(2,1)} fusion(bf16[512,512]{0,1:T(8,128)(2,1)S(1)} %fusion.12, bf16[512,4096]{1,0:T(8,128)(2,1)} %all-gather.20.cloned.1.call-done), kind=kOutput, calls=%fused_computation.15 | convolution fusion | flops 2149580800 | bytes 8912896 | tf_op jit(solution)/shard_map/dot_general | solution.py:110
  492.6 1.6 copy-done.1
  494.1 2.4 reshape.148
  496.5 2.8 reduce_sum.58
  499.6 15.6 %psum.7 = f32[2]{0:T(128)S(1)} all-reduce(f32[2]{0:T(128)S(1)} %multiply_reduce_fusion), channel_id=1, replica_groups=mesh['sec'=32,'tp'=8] {'tp'}, use_global_device_ids=true, to_apply=%region_11.12 | all-reduce | flops 2 | bytes 16 | tf_op jit(solution)/shard_map/psum | solution.py:108
  515.7 31.2 %reduce-scatter.2.cloned.1.call-done = bf16[512,512]{1,0:T(8,128)(2,1)} async-done(((bf16[512,4096]{1,0:T(8,128)(2,1)}), bf16[512,512]{1,0:T(8,128)(2,1)}) %reduce-scatter.2.cloned.1.call-update) | async-done | bytes 524304 | tf_op jit(solution)/shard_map/reduce_scatter | solution.py:115
  547.0 2.0 add_convert_fusion
  (180 shorter events, 98.5 us)
Async XLA Ops:
  7.2 153.4 %copy-start.5 = (f32[4096]{0:T(1024)S(1)}, f32[4096]{0:T(1024)}, u32[]{:S(2)}) copy-start(f32[4096]{0:T(1024)} %param.15) | copy-start | bytes 49156
  7.2 40.6 %all-gather.8.cloned.1.call-start = ((), (), s32[]{:S(2)}) async-start(), calls=%async_computation.1 | async-start | bytes 1179648 | tf_op jit(solution)/shard_map/all_gather | solution.py:57
  9.9 98.0 %all-gather.12.cloned.1.call-start = ((), (), s32[]{:S(2)}) async-start(), calls=%async_computation.3 | async-start | bytes 4718592 | tf_op jit(solution)/shard_map/all_gather | solution.py:40
  10.7 150.0 %all-gather.10.cloned.1.call-start = ((), (), s32[]{:S(2)}) async-start(), calls=%async_computation.2 | async-start | bytes 4325376 | tf_op jit(solution)/shard_map/all_gather | solution.py:44
  11.4 202.2 %all-gather.14.cloned.1.call-start = ((), (), s32[]{:S(2)}) async-start(), calls=%async_computation.4 | async-start | bytes 4325376 | tf_op jit(solution)/shard_map/all_gather | solution.py:42
  12.0 254.6 %all-gather.16.cloned.1.call-start = ((), (), s32[]{:S(2)}) async-start(), calls=%async_computation.5 | async-start | bytes 4325376 | tf_op jit(solution)/shard_map/all_gather | solution.py:43
  12.6 381.6 %all-gather.18.cloned.1.call-start = ((), (), s32[]{:S(2)}) async-start(), calls=%async_computation.6 | async-start | bytes 34603008 | tf_op jit(solution)/shard_map/all_gather | solution.py:13
  47.8 112.8 %copy-start.3 = (bf16[128,4096]{1,0:T(8,128)(2,1)S(1)}, bf16[128,4096]{1,0:T(8,128)(2,1)}, u32[]{:S(2)}) copy-start(bf16[128,4096]{1,0:T(8,128)(2,1)} %all-gather.8.cloned.1.call-done) | copy-start | bytes 3145732
  49.4 164.2 %copy-start.6 = (f32[4096]{0:T(1024)S(1)}, f32[4096]{0:T(1024)}, u32[]{:S(2)}) copy-start(f32[4096]{0:T(1024)} %param.14) | copy-start | bytes 49156
  220.8 51.7 %copy-start = (f32[8,128,512]{2,1,0:T(8,128)}, f32[8,128,512]{2,1,0:T(8,128)S(1)}, u32[]{:S(2)}) copy-start(f32[8,128,512]{2,1,0:T(8,128)S(1)} %get-tuple-element.223) | copy-start | bytes 6291460
  273.3 1.0 copy-start.2
  274.3 211.7 %all-gather.20.cloned.1.call-start = ((), (), s32[]{:S(2)}) async-start(), calls=%async_computation.7 | async-start | bytes 4325376 | tf_op jit(solution)/shard_map/all_gather | solution.py:112
  275.1 271.9 %reduce-scatter.2.cloned.1.call-start = ((), (), s32[]{:S(2)}) async-start(), calls=%async_computation.8 | async-start | bytes 4718592 | tf_op jit(solution)/shard_map/reduce_scatter | solution.py:115
  492.5 1.6 copy-start.1
  494.1 52.8 %copy-start.4 = (bf16[512,512]{1,0:T(8,128)(2,1)S(1)}, bf16[512,512]{1,0:T(8,128)(2,1)}, u32[]{:S(2)}) copy-start(bf16[512,512]{1,0:T(8,128)(2,1)} %param.12) | copy-start | bytes 1572868
Sparse Core Ops, SparseCore 0:
  10.4 37.3 all-gather.7
  49.6 58.2 all-gather.11
  110.5 50.0 all-gather.9
  163.0 50.5 all-gather.13
  216.0 50.5 all-gather.15
  274.4 119.7 all-gather.17
  396.6 53.2 all-gather.19
  492.7 54.2 reduce-scatter.1
where the time goes:
time: 562 us; the launch traced here: 556 us
  waiting for transfers between devices  339 us (60%)
  blocking collectives  67.4 us (12%)
  local copies, waits for them, and re-layouts  61.4 us (11%)
  other arithmetic  50.3 us (9%)
  matrix products  22.4 us (4%)
  between operations  14.4 us (3%)
    all_gather x1, waiting for transfers between devices, combined_all(): everything = jax.tree.map(lambda part: lax.all_gather(part, axis), x)  65.4 us
    all_gather x1, waiting for transfers between devices, on_device(): full_enc = lax.all_gather(encoded, 'tp', axis=1, tiled=True)  58.5 us
    all_gather x2, blocking collectives, combined_all(): everything = jax.tree.map(lambda part: lax.all_gather(part, axis), x)  51.8 us
    dynamic_slice x62, local copies, waits for them, and re-layouts, lap(): return combine(so_far, jax.tree.map(lambda part: part[k], everything))  50.9 us
    all_gather x1, waiting for transfers between devices, on_device(): lax.all_gather(w_key, 'sec', axis=0, tiled=True)  49.9 us
    all_gather x1, waiting for transfers between devices, on_device(): lax.all_gather(w_query, 'sec', axis=0, tiled=True)  49.6 us
    all_gather x1, waiting for transfers between devices, on_device(): lax.all_gather(w_value, 'sec', axis=0, tiled=True)  45.8 us
    all_gather x1, waiting for transfers between devices, on_device(): full_dec = lax.all_gather(own_rows, 'tp', axis=1, tiled=True)  35 us
  transfers between devices with their start and end apart: 8, of which 7 were waited for; matrix products, arithmetic and copies ran while one was open for 20% of the time, Pallas kernels for 0%

commit v1 on v0

v1 whole, which is shorter than its diff:
```python
import jax
import jax.numpy as jnp
from jax import lax
from jax.experimental import pallas as pl
from jax.experimental.pallas import tpu as pltpu
from jax.sharding import PartitionSpec as P

HEADS = 64
HEAD_DIM = 64
PTOK = 256
QTOK = 64
SIDE = 4
CORES = 2
ABSENT = -1e30
BF16 = jnp.bfloat16
F32 = jnp.float32
REACH = (0, -1, 1, 2)


def sec_id(x, y, c):
    return ((x % SIDE) * SIDE + y % SIDE) * CORES + c


def along_tp(v, step):
    n = lax.axis_size("tp")
    return lax.ppermute(v, "tp", [(i, (i + step) % n) for i in range(n)])


def along_tp_by_core(v):
    n = lax.axis_size("tp")
    s = lax.axis_size("sec")
    pairs = [
        (i * n + z, i * n + (z + (1 if i % CORES == 0 else -1)) % n)
        for i in range(s)
        for z in range(n)
    ]
    return lax.ppermute(v, ("sec", "tp"), pairs)


def other_core(v):
    s = lax.axis_size("sec")
    return lax.ppermute(v, "sec", [(i, i ^ 1) for i in range(s)])


def in_plane(v, step, swap):
    pairs = []
    for x in range(SIDE):
        for y in range(SIDE):
            for c in range(CORES):
                on_x = (c == 0) != swap
                to = sec_id(x + step, y, c) if on_x else sec_id(x, y + step, c)
                pairs.append((sec_id(x, y, c), to))
    return lax.ppermute(v, "sec", pairs)


def ring_gather(piece):
    core = lax.axis_index("sec") % CORES
    up = down = piece
    held = [piece]
    for _ in range(3):
        up, down = along_tp(up, 1), along_tp(down, -1)
        held += [up, down]
    held.append(along_tp_by_core(jnp.where(core == 0, up, down)))
    return held


def plane_gather(shard):
    half = shard.shape[0] // 2
    a, b = in_plane(shard, 1, False), in_plane(shard, -1, False)
    c, d = in_plane(a[:half], 1, False), in_plane(b[half:], -1, False)
    g = jnp.concatenate([shard, a, b, c, d], 0)
    ga, gb = in_plane(g, 1, True), in_plane(g, -1, True)
    half = g.shape[0] // 2
    gc, gd = in_plane(ga[:half], 1, True), in_plane(gb[half:], -1, True)
    own = [g, ga, gb, gc, gd]
    return own + [other_core(v) for v in own]


def high_low(v):
    high = v.astype(BF16).astype(F32)
    return high, (v - high).astype(BF16).astype(F32)


def attend_kernel(
    info, gains, *refs
):
    x_parts, w_parts = refs[:8], refs[8:18]
    out, wo = refs[18:20]
    xs, ws, ks, vs, qs, scale, sems = refs[20:]
    sec, tp, first, own_a, own_b = info[0], info[1], info[2], info[3], info[4]
    core = sec % CORES
    px = sec // (SIDE * CORES)
    py = (sec // CORES) % SIDE
    for part, off in zip(x_parts, (0, -1, 1, -2, 2, -3, 3, 4)):
        at = pl.multiple_of(((tp + off + 8) % 8) * 512, 512)
        pltpu.make_async_copy(part, xs.at[:, pl.ds(at, 512)], sems.at[0]).start()
    shards = []
    for mine in (True, False):
        group = w_parts[:5] if mine else w_parts[5:]
        col = core if mine else 1 - core
        for r2 in REACH:
            for at, r1 in enumerate(REACH):
                if r2 == 2:
                    ref, row = (group[3], at) if at < 2 else (group[4], at - 2)
                else:
                    ref, row = group[REACH.index(r2)], at
                dx = jnp.where(col == 0, r1, r2)
                dy = jnp.where(col == 0, r2, r1)
                s = (((px + dx + SIDE) % SIDE) * SIDE + (py + dy + SIDE) % SIDE) * CORES + col
                shards.append((ref, row, s))
    for ref, row, s in shards:
        pltpu.make_async_copy(ref.at[pl.ds(row * 512, 384)], ws.at[s], sems.at[1]).start()
    for ref, row, s in shards:
        pltpu.make_async_copy(
            ref.at[pl.ds(row * 512 + 384, 128)],
            wo.at[pl.ds(pl.multiple_of(s * 128, 128), 128)],
            sems.at[2],
        ).start()

    lane = lax.broadcasted_iota(jnp.int32, (1, 128), 1)
    rest = jnp.where(lane < 8, ABSENT, 0.0)
    out[:, :512] = jnp.zeros((512, 512), BF16)
    out[:, 512:] = jnp.broadcast_to(rest, (512, 128)).astype(BF16)

    pltpu.make_async_copy(xs, xs, sems.at[0]).wait()

    @pl.loop(0, 5)
    def _(i):
        rows = pl.ds(pl.multiple_of(i * 128, 128), 128)
        which = pl.ds((i == 4).astype(jnp.int32), 1)
        total = jnp.zeros((128, 1), F32)
        for j in range(8):
            cols = slice(512 * j, 512 * (j + 1))
            v = xs[rows, cols].astype(F32)
            total = total + jnp.sum(v * v, axis=1, keepdims=True)
            xs[rows, cols] = (v * gains[which, cols]).astype(BF16)
        scale[rows, :] = jnp.broadcast_to(lax.rsqrt(total / 4096.0 + 1e-06), (128, 128))

    pltpu.make_async_copy(ws, ws, sems.at[1]).wait()

    @pl.loop(0, 2)
    def _(n):
        cols = pl.ds(pl.multiple_of(n * 256, 256), 256)
        wq = ws[:, 256:384, cols].reshape(4096, 256)
        q = jnp.dot(xs[512:640, :], wq, preferred_element_type=F32)
        qs[:, cols] = (q * scale[512:640, 0:1]).astype(BF16)
        wk = ws[:, 0:128, cols].reshape(4096, 256)
        k = jnp.dot(xs[0:512, :], wk, preferred_element_type=F32)
        ks[:, cols] = (k * scale[0:512, 0:1]).astype(BF16)
        wv = ws[:, 128:256, cols].reshape(4096, 256)
        v = jnp.dot(xs[0:512, :], wv, preferred_element_type=F32)
        vs[:, cols] = (v * scale[0:512, 0:1]).astype(BF16)

    row_owner = first + lax.broadcasted_iota(jnp.int32, (128, 512), 0) // QTOK
    key_owner = jnp.where(lax.broadcasted_iota(jnp.int32, (128, 512), 1) < PTOK, own_a, own_b)
    keep = row_owner == key_owner
    window = pl.ds(pl.multiple_of(first * QTOK, QTOK), 128)
    lane = lax.broadcasted_iota(jnp.int32, (128, 128), 1)
    stats = jnp.zeros((128, 128), F32)
    for pair in range(4):
        cols = slice(128 * pair, 128 * (pair + 1))
        q2, k2, v2 = qs[:, cols], ks[:, cols], vs[:, cols]
        sums = []
        for side in range(2):
            h = 2 * pair + side
            mine = (lane < 64) if side == 0 else (lane >= 64)
            qh = jnp.where(mine, q2.astype(F32), 0.0).astype(BF16)
            scores = lax.dot_general(qh, k2, (((1,), (1,)), ((), ())), preferred_element_type=F32)
            scores = jnp.where(keep, scores, ABSENT)
            top_hi, top_lo = high_low(jnp.max(scores, axis=1, keepdims=True))
            weights = jnp.where(keep, jnp.exp(scores - (top_hi + top_lo)), 0.0)
            a_hi, a_lo = high_low(jnp.sum(weights[:, :PTOK], axis=1, keepdims=True))
            b_hi, b_lo = high_low(jnp.sum(weights[:, PTOK:], axis=1, keepdims=True))
            for at, value in enumerate((top_hi, top_lo, a_hi, a_lo, b_hi, b_lo)):
                stats = jnp.where(lane == 8 * at + h, value, stats)
            sums.append(jnp.dot(weights.astype(BF16), v2, preferred_element_type=F32))
        out[window, cols] = jnp.where(lane < 64, sums[0], sums[1]).astype(BF16)
    out[window, 512:640] = stats.astype(BF16)
    pltpu.make_async_copy(wo, wo, sems.at[2]).wait()


def attend(info, gains, x_parts, w_parts):
    anywhere = pl.BlockSpec(memory_space=pl.ANY)
    inside = pl.BlockSpec(memory_space=pltpu.VMEM)
    return pl.pallas_call(
        attend_kernel,
        in_specs=[pl.BlockSpec(memory_space=pltpu.SMEM), inside] + [anywhere] * 18,
        out_specs=[inside, anywhere],
        out_shape=[
            jax.ShapeDtypeStruct((512, 640), BF16),
            jax.ShapeDtypeStruct((4096, 512), BF16),
        ],
        scratch_shapes=[
            pltpu.VMEM((640, 4096), BF16),
            pltpu.VMEM((32, 384, 512), BF16),
            pltpu.VMEM((512, 512), BF16),
            pltpu.VMEM((512, 512), BF16),
            pltpu.VMEM((128, 512), BF16),
            pltpu.VMEM((640, 128), F32),
            pltpu.SemaphoreType.DMA((3,)),
        ],
        compiler_params=pltpu.CompilerParams(vmem_limit_bytes=40 * 2**20),
        cost_estimate=pl.CostEstimate(
            flops=5 * 10**9, bytes_accessed=30 * 2**20, transcendentals=2**19
        ),
        name="project_attend",
    )(info, gains, *x_parts, *w_parts)


def merge_kernel(got, wo, out):
    st = got[:, 512:640].astype(F32)
    both = st + pltpu.roll(st, 120, 1)
    sum_a = pltpu.roll(both, 112, 1).reshape(32, 16, 128)
    sum_b = pltpu.roll(both, 96, 1).reshape(32, 16, 128)
    both = both.reshape(32, 16, 128)
    lane3 = lax.broadcasted_iota(jnp.int32, (32, 16, 128), 2)
    head = lane3 < 8
    tops = jnp.where(head, both, 0.0)
    top = jnp.max(tops, axis=0, keepdims=True)
    factor = jnp.exp(tops - top)
    sum_a = jnp.where(head, sum_a * factor, 0.0)
    sum_b = jnp.where(head, sum_b * factor, 0.0)
    total = jnp.sum(sum_a + sum_b, axis=0, keepdims=True)
    inverse = jnp.where(head[:1], 1.0 / total, 0.0)
    share_a = jnp.sum((sum_a * inverse).reshape(512, 128), axis=1, keepdims=True)
    share_b = jnp.sum((sum_b * inverse).reshape(512, 128), axis=1, keepdims=True)
    lane = lax.broadcasted_iota(jnp.int32, (512, 128), 1)
    slot = (lax.broadcasted_iota(jnp.int32, (512, 128), 0) // 16) * 2
    pooled = jnp.sum(
        jnp.where(lane == slot, share_a, 0.0) + jnp.where(lane == slot + 1, share_b, 0.0),
        axis=0,
        keepdims=True,
    )
    ratio_hi, ratio_lo = high_low((factor * inverse).reshape(512, 128))
    spread = (
        lax.broadcasted_iota(jnp.int32, (128, 512), 1) // HEAD_DIM
        == lax.broadcasted_iota(jnp.int32, (128, 512), 0)
    )
    spread = jnp.where(spread, 1.0, 0.0).astype(BF16)
    ratio = jnp.dot(ratio_hi.astype(BF16), spread, preferred_element_type=F32) + jnp.dot(
        ratio_lo.astype(BF16), spread, preferred_element_type=F32
    )
    context = jnp.sum((got[:, 0:512].astype(F32) * ratio).reshape(32, 16, 512), axis=0)
    context = context.astype(BF16)
    pool_hi, pool_lo = high_low(pooled)
    row = lax.broadcasted_iota(jnp.int32, (16, 128), 0)
    extra = jnp.where(row == 0, pool_hi, jnp.where(row == 1, pool_lo, 0.0)).astype(BF16)
    for z in range(8):
        term = lax.dot_general(
            context,
            wo[512 * z : 512 * (z + 1), :],
            (((1,), (1,)), ((), ())),
            preferred_element_type=F32,
        )
        out[z, :, 0:512] = term.astype(BF16)
        out[z, :, 512:640] = extra


def merge(got, wo):
    return pl.pallas_call(
        merge_kernel,
        out_shape=jax.ShapeDtypeStruct((8, 16, 640), BF16),
        compiler_params=pltpu.CompilerParams(vmem_limit_bytes=40 * 2**20),
        name="merge_project",
    )(got, wo)


def add_kernel(got, rows, out):
    sums = jnp.sum(got[...].astype(F32), axis=0)
    done = (rows[...].astype(F32) + sums[:, 0:512]).astype(BF16)
    pool_hi, pool_lo = high_low(jnp.sum(sums[:, 512:640], axis=0, keepdims=True))
    row = lax.broadcasted_iota(jnp.int32, (16, 128), 0)
    extra = jnp.where(row == 0, pool_hi, jnp.where(row == 1, pool_lo, 0.0)).astype(BF16)
    for s in range(32):
        out[s, :, 0:512] = done
        out[s, :, 512:640] = extra


def add_rows(got, rows):
    return pl.pallas_call(
        add_kernel,
        out_shape=jax.ShapeDtypeStruct((32, 16, 640), BF16),
        name="add_rows",
    )(got, rows)


def on_device(
    encoded, decoder_states, passage_counts, enc_gain, dec_gain, w_key, w_value, w_query, w_out
):
    sec = lax.axis_index("sec")
    tp = lax.axis_index("tp")
    questions = decoder_states.shape[0] // QTOK
    ends = jnp.cumsum(passage_counts)
    slots = sec * 2 + jnp.arange(2, dtype=jnp.int32)
    owner = jnp.sum((slots[:, None] >= ends[None, :]).astype(jnp.int32), axis=1)
    first = jnp.minimum(owner[0], questions - 2)
    info = jnp.stack([sec, tp, first, owner[0], owner[1]]).astype(jnp.int32)
    window = lax.dynamic_slice_in_dim(decoder_states, first * QTOK, 2 * QTOK, 0)
    x_parts = ring_gather(jnp.concatenate([encoded, window], 0))
    w_parts = plane_gather(jnp.concatenate([w_key, w_value, w_query, w_out.T], 0))
    gains = jnp.stack([enc_gain, dec_gain])
    partial, wo = attend(info, gains, x_parts, w_parts)
    got = lax.all_to_all(partial, "sec", 0, 0, tiled=True)
    terms = merge(got, wo)
    terms = lax.all_to_all(terms, "tp", 0, 0, tiled=True)
    rows = lax.dynamic_slice_in_dim(decoder_states, sec * 16, 16, 0)
    finished = lax.all_to_all(add_rows(terms, rows), "sec", 0, 0, tiled=True)
    decoded = finished[:, :, 0:512].reshape(512, 512)
    pooled = jnp.sum(finished[:, 0:2, 512:640].astype(F32), axis=(0, 1))
    passage_scores = lax.dynamic_slice_in_dim(pooled, sec * 2, 2, 0) / (HEADS * QTOK)
    return (decoded, passage_scores)


def solution(mesh):
    placed = (
        P("sec", "tp"),
        P(None, "tp"),
        P(),
        P(),
        P(),
        P("sec", "tp"),
        P("sec", "tp"),
        P("sec", "tp"),
        P("tp", "sec"),
    )
    return jax.shard_map(
        on_device, mesh=mesh, in_specs=placed, out_specs=(P(None, "tp"), P("sec")), check_vma=False
    )
```

time: 562 us -> 266 us (0.47); the launches traced: 556 us -> 265 us
  waiting for transfers between devices: 339 us -> 57.2 us
  Pallas kernels: 0 us -> 119 us
  blocking collectives: 67.4 us -> 21.5 us
  other arithmetic: 50.3 us -> 5.08 us
  starting transfers between devices: 0.31 us -> 44.5 us
  local copies, waits for them, and re-layouts: 61.4 us -> 17.6 us
  matrix products: 22.4 us -> 0 us
  between operations: 14.4 us -> 0.86 us
    all_gather x7 -> x0, waiting for transfers between devices: 304 us -> none  [the longest x1 65.4 us: combined_all(): everything = jax.tree.map(lambda part: lax.all_gather(part, axis), x)]
    pallas_call x0 -> x3, Pallas kernels: none -> 119 us  [the longest x1 114 us: attend(): pl.pallas_call(attend_kernel, in_specs=[pl.BlockSpec(memory_space=pltpu.S...]
    dynamic_slice x63 -> x2, local copies, waits for them, and re-layouts: 52.5 us -> 0.62 us  [the longest x1 0.6 us: on_device(): rows = lax.dynamic_slice_in_dim(decoder_states, sec * 16, 16, 0)]
    all_gather x2 -> x0, blocking collectives: 51.8 us -> none  [combined_all(): everything = jax.tree.map(lambda part: lax.all_gather(part, axis), x)]
    add x64 -> x1, other arithmetic: 38.1 us -> 0.01 us  [on_device(): slots = sec * 2 + jnp.arange(2, dtype=jnp.int32)]
    ppermute x0 -> x20, starting transfers between devices: none -> 35.6 us  [the longest x8 15.6 us: in_plane(): return lax.ppermute(v, 'sec', pairs)]
    ppermute x0 -> x20, waiting for transfers between devices: none -> 34.5 us  [the longest x6 21.1 us: along_tp(): return lax.ppermute(v, 'tp', [(i, (i + step) % n) for i in range(n)])]
    reduce_scatter x1 -> x0, waiting for transfers between devices: 31.2 us -> none  [on_device(): lax.psum_scatter(terms.astype(jnp.bfloat16), 'tp', scatter_dimension=1, t...]
  transfers between devices with their start and end apart: 8 -> 22, of which waited for: 7 -> 11; matrix products, arithmetic and copies ran while one was open for 20% -> 4% of each run, Pallas kernels for 0% -> 0%
where the time goes in v1:
time: 266 us; the launch traced here: 265 us
  Pallas kernels  119 us (45%)
  waiting for transfers between devices  57.2 us (22%)
  starting transfers between devices  44.5 us (17%)
  blocking collectives  21.5 us (8%)
  local copies, waits for them, and re-layouts  17.6 us (7%)
  other arithmetic  5.08 us (2%)
    pallas_call x1, Pallas kernels, attend(): pl.pallas_call(attend_kernel, in_specs=[pl.BlockSpec(memory_space=pltpu.S...  114 us
    all_to_all x1, blocking collectives, on_device(): got = lax.all_to_all(partial, 'sec', 0, 0, tiled=True)  21.5 us
    ppermute x6, waiting for transfers between devices, along_tp(): return lax.ppermute(v, 'tp', [(i, (i + step) % n) for i in range(n)])  21.1 us
    ppermute x8, starting transfers between devices, in_plane(): return lax.ppermute(v, 'sec', pairs)  15.6 us
    unnamed x36, local copies, waits for them, and re-layouts  14 us
    all_to_all x1, waiting for transfers between devices, on_device(): finished = lax.all_to_all(add_rows(terms, rows), 'sec', 0, 0, tiled=True)  13.1 us
    ppermute x6, starting transfers between devices, along_tp(): return lax.ppermute(v, 'tp', [(i, (i + step) % n) for i in range(n)])  11.7 us
    ppermute x8, waiting for transfers between devices, in_plane(): return lax.ppermute(v, 'sec', pairs)  9.89 us
  transfers between devices with their start and end apart: 22, of which 11 were waited for; matrix products, arithmetic and copies ran while one was open for 4% of the time, Pallas kernels for 0%

profile of v1, /device:TPU:1, one launch (start us, length us, event | category | flops | bytes accessed | tf_op | source)
XLA Modules:
  0.0 265.4 jit_solution(6639542281776338000)
XLA Ops:
  2.8 2.2 collective-permute-start.7
  7.2 1.7 collective-permute-start
  9.0 4.0 %collective-permute-start.1 = (bf16[640,512]{1,0:T(8,128)(2,1)S(1)}, bf16[640,512]{1,0:T(8,128)(2,1)S(1)}, u32[]{:S(2)}, u32[]{:S(2)}) collective-permute-start(bf16[640,512]{1,0:T(8,128)(2,1)S(1)} %pad_maximum_fusion.refs_0_), channel_id=1, source_target_pairs={{0,7},{1,0},{2,1},{3,2},{4,3},{5,4},{6,5},{7,6},{8,15},{9,8},{10,9... | collective-permute-start | bytes 1966088 | tf_op jit(solution)/shard_map/ppermute | solution.py:26
  17.3 4.0 %collective-permute-done.8 = bf16[512,512]{1,0:T(8,128)(2,1)S(1)} collective-permute-done((bf16[512,512]{1,0:T(8,128)(2,1)S(1)}, bf16[512,512]{1,0:T(8,128)(2,1)S(1)}, u32[]{:S(2)}, u32[]{:S(2)}) %collective-permute-start.8) | collective-permute-done | bytes 524320 | tf_op jit(solution)/shard_map/ppermute | solution.py:53
  21.3 2.8 %collective-permute-start.10 = (bf16[256,512]{1,0:T(8,128)(2,1)S(1)}, bf16[256,512]{1,0:T(8,128)(2,1)S(1)}, u32[]{:S(2)}, u32[]{:S(2)}) collective-permute-start(bf16[256,512]{1,0:T(8,128)(2,1)S(1)} %slice.32), channel_id=1, source_target_pairs={{0,192},{8,56},{16,208},{24,8},{32,224},{40,24},{48,240},{56,40},{... | collective-permute-start | bytes 786440 | tf_op jit(solution)/shard_map/ppermute | solution.py:53
  28.0 2.7 %collective-permute-start.3 = (bf16[640,512]{1,0:T(8,128)(2,1)S(1)}, bf16[640,512]{1,0:T(8,128)(2,1)}, u32[]{:S(2)}, u32[]{:S(2)}) collective-permute-start(bf16[640,512]{1,0:T(8,128)(2,1)S(1)} %collective-permute-done.1.refs_2_), channel_id=1, source_target_pairs={{0,7},{1,0},{2,1},{3,2},{4,3},{5,4},{6,5},{7,6},{8,15},{9,8},{10,9... | collective-permute-start | bytes 1966088 | tf_op jit(solution)/shard_map/ppermute | solution.py:26
  33.3 2.3 collective-permute-start.12
  35.6 7.6 %collective-permute-done.2.refs_3_ = bf16[640,512]{1,0:T(8,128)(2,1)} collective-permute-done((bf16[640,512]{1,0:T(8,128)(2,1)S(1)}, bf16[640,512]{1,0:T(8,128)(2,1)}, u32[]{:S(2)}, u32[]{:S(2)}) %collective-permute-start.2) | collective-permute-done | bytes 655392 | tf_op jit(solution)/shard_map/ppermute | solution.py:26
  43.2 3.2 %collective-permute-start.5 = (bf16[640,512]{1,0:T(8,128)(2,1)}, bf16[640,512]{1,0:T(8,128)(2,1)}, u32[]{:S(2)}, u32[]{:S(2)}) collective-permute-start(bf16[640,512]{1,0:T(8,128)(2,1)} %collective-permute-done.3.refs_4_), channel_id=1, source_target_pairs={{0,7},{1,0},{2,1},{3,2},{4,3},{5,4},{6,5},{7,6},{8,15},{9,8},{10,9... | collective-permute-start | bytes 1966088 | tf_op jit(solution)/shard_map/ppermute | solution.py:26
  46.5 12.1 %collective-permute-done.4.refs_5_ = bf16[640,512]{1,0:T(8,128)(2,1)} collective-permute-done((bf16[640,512]{1,0:T(8,128)(2,1)}, bf16[640,512]{1,0:T(8,128)(2,1)}, u32[]{:S(2)}, u32[]{:S(2)}) %collective-permute-start.4) | collective-permute-done | bytes 655392 | tf_op jit(solution)/shard_map/ppermute | solution.py:26
  59.8 3.0 %collective-permute-start.6 = (bf16[640,512]{1,0:T(8,128)(2,1)S(1)}, bf16[640,512]{1,0:T(8,128)(2,1)S(1)}, u32[]{:S(2)}, u32[]{:S(2)}) collective-permute-start(bf16[640,512]{1,0:T(8,128)(2,1)S(1)} %broadcast_select_fusion), channel_id=1, source_target_pairs={{0,1},{1,2},{2,3},{3,4},{4,5},{5,6},{6,7},{7,0},{8,15},{9,8},{10,9... | collective-permute-start | bytes 1966088 | tf_op jit(solution)/shard_map/ppermute | solution.py:37
  65.9 4.3 %collective-permute-start.14 = (bf16[1024,512]{1,0:T(8,128)(2,1)S(1)}, bf16[1024,512]{1,0:T(8,128)(2,1)}, u32[]{:S(2)}, u32[]{:S(2)}) collective-permute-start(bf16[1024,512]{1,0:T(8,128)(2,1)S(1)} %slice.34), channel_id=1, source_target_pairs={{0,48},{8,200},{16,0},{24,216},{32,16},{40,232},{48,32},{56,248},{... | collective-permute-start | bytes 3145736 | tf_op jit(solution)/shard_map/ppermute | solution.py:53
  71.2 4.9 %collective-permute-start.17 = (bf16[2048,512]{1,0:T(8,128)(2,1)}, bf16[2048,512]{1,0:T(8,128)(2,1)}, u32[]{:S(2)}, u32[]{:S(2)}) collective-permute-start(bf16[2048,512]{1,0:T(8,128)(2,1)} %collective-permute-done.12.refs_10_), channel_id=1, source_target_pairs={{0,8},{8,0},{16,24},{24,16},{32,40},{40,32},{48,56},{56,48},{64,72... | collective-permute-start | bytes 6291464 | tf_op jit(solution)/shard_map/ppermute | solution.py:42
  76.1 4.8 %collective-permute-done.13.refs_11_ = bf16[1024,512]{1,0:T(8,128)(2,1)} collective-permute-done((bf16[1024,512]{1,0:T(8,128)(2,1)S(1)}, bf16[1024,512]{1,0:T(8,128)(2,1)}, u32[]{:S(2)}, u32[]{:S(2)}) %collective-permute-start.13) | collective-permute-done | bytes 1048608 | tf_op jit(solution)/shard_map/ppermute | solution.py:53
  82.1 1.8 collective-permute-done.18.refs_16_
  88.7 114.3 %project_attend.1 = (bf16[512,640]{1,0:T(8,128)(2,1)S(1)}, bf16[4096,512]{1,0:T(8,128)(2,1)}) custom-call(s32[5]{0:T(128)S(1)} %pad_add_fusion.info, f32[2,4096]{1,0:T(2,128)S(1)} %pad_maximum_fusion.2.gains, bf16[640,512]{1,0:T(8,128)(2,1)S(1)} %pad_maximum_fusion.refs_0_, bf16[640,512]{1,0:T(8,128)(2,1)S(1)} %copy-done.3, bf16[640,512]{1,0:T(8,128)(2,1)S(1)} %copy-done.5, ...), custom_call_target="tpu_custom_call" | custom-call | flops 5000000000 | bytes 31457280 | tf_op jit(solution)/shard_map/project_attend/pallas_call | solution.py:185
  203.0 21.5 %all_to_all.21 = bf16[32,16,640]{2,1,0:T(8,128)(2,1)S(1)} all-to-all(bf16[32,16,640]{2,1,0:T(8,128)(2,1)S(1)} %bitcast.14), channel_id=1, replica_groups=mesh['sec'=32,'tp'=8] {'sec'}, dimensions={0} | all-to-all | bytes 1310720 | tf_op jit(solution)/shard_map/all_to_all | solution.py:303
  224.5 2.2 copy-done.1
  226.7 2.5 merge_project.1
  229.2 4.9 %all-to-all-start.1 = ((bf16[8,16,640]{2,1,0:T(8,128)(2,1)}), bf16[8,16,640]{2,1,0:T(8,128)(2,1)S(1)}, u32[]{:S(2)}, u32[]{:S(2)}) async-start(bf16[8,16,640]{2,1,0:T(8,128)(2,1)} %merge_project.1), calls=%async_computation.1 | async-start | bytes 327680 | tf_op jit(solution)/shard_map/all_to_all | solution.py:305
  234.7 9.6 %all-to-all-done.1.got = bf16[8,16,640]{2,1,0:T(8,128)(2,1)S(1)} async-done(((bf16[8,16,640]{2,1,0:T(8,128)(2,1)}), bf16[8,16,640]{2,1,0:T(8,128)(2,1)S(1)}, u32[]{:S(2)}, u32[]{:S(2)}) %all-to-all-start.1) | async-done | bytes 163872 | tf_op jit(solution)/shard_map/all_to_all | solution.py:305
  245.0 1.8 add_rows.1
  246.8 4.1 %all-to-all-start.2 = ((bf16[32,16,640]{2,1,0:T(8,128)(2,1)}), bf16[32,16,640]{2,1,0:T(8,128)(2,1)S(1)}, u32[]{:S(2)}, u32[]{:S(2)}) async-start(bf16[32,16,640]{2,1,0:T(8,128)(2,1)} %add_rows.1), calls=%async_computation.2 | async-start | bytes 1310720 | tf_op jit(solution)/shard_map/all_to_all | solution.py:307
  250.9 13.1 %all-to-all-done.2 = bf16[32,16,640]{2,1,0:T(8,128)(2,1)S(1)} async-done(((bf16[32,16,640]{2,1,0:T(8,128)(2,1)}), bf16[32,16,640]{2,1,0:T(8,128)(2,1)S(1)}, u32[]{:S(2)}, u32[]{:S(2)}) %all-to-all-start.2) | async-done | bytes 655392 | tf_op jit(solution)/shard_map/all_to_all | solution.py:307
  (78 shorter events, 29.1 us)
Async XLA Ops:
  2.8 13.6 %collective-permute-start.7 = (bf16[512,512]{1,0:T(8,128)(2,1)S(1)}, bf16[512,512]{1,0:T(8,128)(2,1)S(1)}, u32[]{:S(2)}, u32[]{:S(2)}) collective-permute-start(bf16[512,512]{1,0:T(8,128)(2,1)S(1)} %pad_maximum_fusion.1), channel_id=1, source_target_pairs={{0,64},{8,24},{16,80},{24,40},{32,96},{40,56},{48,112},{56,8},{64,... | collective-permute-start | bytes 1572872 | tf_op jit(solution)/shard_map/ppermute | solution.py:53
  7.2 19.9 %collective-permute-start = (bf16[640,512]{1,0:T(8,128)(2,1)S(1)}, bf16[640,512]{1,0:T(8,128)(2,1)S(1)}, u32[]{:S(2)}, u32[]{:S(2)}) collective-permute-start(bf16[640,512]{1,0:T(8,128)(2,1)S(1)} %pad_maximum_fusion.refs_0_), channel_id=1, source_target_pairs={{0,1},{1,2},{2,3},{3,4},{4,5},{5,6},{6,7},{7,0},{8,9},{9,10},{10,1... | collective-permute-start | bytes 1966088 | tf_op jit(solution)/shard_map/ppermute | solution.py:26
  9.0 19.0 %collective-permute-start.1 = (bf16[640,512]{1,0:T(8,128)(2,1)S(1)}, bf16[640,512]{1,0:T(8,128)(2,1)S(1)}, u32[]{:S(2)}, u32[]{:S(2)}) collective-permute-start(bf16[640,512]{1,0:T(8,128)(2,1)S(1)} %pad_maximum_fusion.refs_0_), channel_id=1, source_target_pairs={{0,7},{1,0},{2,1},{3,2},{4,3},{5,4},{6,5},{7,6},{8,15},{9,8},{10,9... | collective-permute-start | bytes 1966088 | tf_op jit(solution)/shard_map/ppermute | solution.py:26
  13.0 8.3 %collective-permute-start.8 = (bf16[512,512]{1,0:T(8,128)(2,1)S(1)}, bf16[512,512]{1,0:T(8,128)(2,1)S(1)}, u32[]{:S(2)}, u32[]{:S(2)}) collective-permute-start(bf16[512,512]{1,0:T(8,128)(2,1)S(1)} %pad_maximum_fusion.1), channel_id=1, source_target_pairs={{0,192},{8,56},{16,208},{24,8},{32,224},{40,24},{48,240},{56,40},{... | collective-permute-start | bytes 1572872 | tf_op jit(solution)/shard_map/ppermute | solution.py:53
  16.5 14.2 %collective-permute-start.9 = (bf16[256,512]{1,0:T(8,128)(2,1)S(1)}, bf16[256,512]{1,0:T(8,128)(2,1)S(1)}, u32[]{:S(2)}, u32[]{:S(2)}) collective-permute-start(bf16[256,512]{1,0:T(8,128)(2,1)S(1)} %slice.31), channel_id=1, source_target_pairs={{0,64},{8,24},{16,80},{24,40},{32,96},{40,56},{48,112},{56,8},{64,... | collective-permute-start | bytes 786440 | tf_op jit(solution)/shard_map/ppermute | solution.py:53
  21.3 10.1 %collective-permute-start.10 = (bf16[256,512]{1,0:T(8,128)(2,1)S(1)}, bf16[256,512]{1,0:T(8,128)(2,1)S(1)}, u32[]{:S(2)}, u32[]{:S(2)}) collective-permute-start(bf16[256,512]{1,0:T(8,128)(2,1)S(1)} %slice.32), channel_id=1, source_target_pairs={{0,192},{8,56},{16,208},{24,8},{32,224},{40,24},{48,240},{56,40},{... | collective-permute-start | bytes 786440 | tf_op jit(solution)/shard_map/ppermute | solution.py:53
  27.1 16.1 %collective-permute-start.2 = (bf16[640,512]{1,0:T(8,128)(2,1)S(1)}, bf16[640,512]{1,0:T(8,128)(2,1)}, u32[]{:S(2)}, u32[]{:S(2)}) collective-permute-start(bf16[640,512]{1,0:T(8,128)(2,1)S(1)} %collective-permute-done.refs_1_), channel_id=1, source_target_pairs={{0,1},{1,2},{2,3},{3,4},{4,5},{5,6},{6,7},{7,0},{8,9},{9,10},{10,1... | collective-permute-start | bytes 1966088 | tf_op jit(solution)/shard_map/ppermute | solution.py:26
  28.0 15.2 %collective-permute-start.3 = (bf16[640,512]{1,0:T(8,128)(2,1)S(1)}, bf16[640,512]{1,0:T(8,128)(2,1)}, u32[]{:S(2)}, u32[]{:S(2)}) collective-permute-start(bf16[640,512]{1,0:T(8,128)(2,1)S(1)} %collective-permute-done.1.refs_2_), channel_id=1, source_target_pairs={{0,7},{1,0},{2,1},{3,2},{4,3},{5,4},{6,5},{7,6},{8,15},{9,8},{10,9... | collective-permute-start | bytes 1966088 | tf_op jit(solution)/shard_map/ppermute | solution.py:26
  32.1 31.1 %collective-permute-start.11 = (bf16[2048,512]{1,0:T(8,128)(2,1)}, bf16[2048,512]{1,0:T(8,128)(2,1)S(1)}, u32[]{:S(2)}, u32[]{:S(2)}) collective-permute-start(bf16[2048,512]{1,0:T(8,128)(2,1)} %constant_dynamic-update-slice_fusion.refs_8_), channel_id=1, source_target_pairs={{0,16},{8,72},{16,32},{24,88},{32,48},{40,104},{48,0},{56,120},{64... | collective-permute-start | bytes 6291464 | tf_op jit(solution)/shard_map/ppermute | solution.py:53
  33.3 31.3 %collective-permute-start.12 = (bf16[2048,512]{1,0:T(8,128)(2,1)}, bf16[2048,512]{1,0:T(8,128)(2,1)}, u32[]{:S(2)}, u32[]{:S(2)}) collective-permute-start(bf16[2048,512]{1,0:T(8,128)(2,1)} %constant_dynamic-update-slice_fusion.refs_8_), channel_id=1, source_target_pairs={{0,48},{8,200},{16,0},{24,216},{32,16},{40,232},{48,32},{56,248},{... | collective-permute-start | bytes 6291464 | tf_op jit(solution)/shard_map/ppermute | solution.py:53
  43.2 15.4 %collective-permute-start.4 = (bf16[640,512]{1,0:T(8,128)(2,1)}, bf16[640,512]{1,0:T(8,128)(2,1)}, u32[]{:S(2)}, u32[]{:S(2)}) collective-permute-start(bf16[640,512]{1,0:T(8,128)(2,1)} %collective-permute-done.2.refs_3_), channel_id=1, source_target_pairs={{0,1},{1,2},{2,3},{3,4},{4,5},{5,6},{6,7},{7,0},{8,9},{9,10},{10,1... | collective-permute-start | bytes 1966088 | tf_op jit(solution)/shard_map/ppermute | solution.py:26
  43.2 15.4 %collective-permute-start.5 = (bf16[640,512]{1,0:T(8,128)(2,1)}, bf16[640,512]{1,0:T(8,128)(2,1)}, u32[]{:S(2)}, u32[]{:S(2)}) collective-permute-start(bf16[640,512]{1,0:T(8,128)(2,1)} %collective-permute-done.3.refs_4_), channel_id=1, source_target_pairs={{0,7},{1,0},{2,1},{3,2},{4,3},{5,4},{6,5},{7,6},{8,15},{9,8},{10,9... | collective-permute-start | bytes 1966088 | tf_op jit(solution)/shard_map/ppermute | solution.py:26
  59.8 22.3 %copy-start.12 = (f32[4096]{0:T(1024)S(1)}, f32[4096]{0:T(1024)}, u32[]{:S(2)}) copy-start(f32[4096]{0:T(1024)} %param.13) | copy-start | bytes 49156
  59.8 22.2 %copy-start.13 = (f32[4096]{0:T(1024)S(1)}, f32[4096]{0:T(1024)}, u32[]{:S(2)}) copy-start(f32[4096]{0:T(1024)} %param.12) | copy-start | bytes 49156
  59.8 10.6 %collective-permute-start.6 = (bf16[640,512]{1,0:T(8,128)(2,1)S(1)}, bf16[640,512]{1,0:T(8,128)(2,1)S(1)}, u32[]{:S(2)}, u32[]{:S(2)}) collective-permute-start(bf16[640,512]{1,0:T(8,128)(2,1)S(1)} %broadcast_select_fusion), channel_id=1, source_target_pairs={{0,1},{1,2},{2,3},{3,4},{4,5},{5,6},{6,7},{7,0},{8,15},{9,8},{10,9... | collective-permute-start | bytes 1966088 | tf_op jit(solution)/shard_map/ppermute | solution.py:37
  62.8 19.2 %collective-permute-start.15 = (bf16[2048,512]{1,0:T(8,128)(2,1)}, bf16[2048,512]{1,0:T(8,128)(2,1)}, u32[]{:S(2)}, u32[]{:S(2)}) collective-permute-start(bf16[2048,512]{1,0:T(8,128)(2,1)} %constant_dynamic-update-slice_fusion.refs_8_), channel_id=1, source_target_pairs={{0,8},{8,0},{16,24},{24,16},{32,40},{40,32},{48,56},{56,48},{64,72... | collective-permute-start | bytes 6291464 | tf_op jit(solution)/shard_map/ppermute | solution.py:42
  63.3 17.6 %collective-permute-start.13 = (bf16[1024,512]{1,0:T(8,128)(2,1)S(1)}, bf16[1024,512]{1,0:T(8,128)(2,1)}, u32[]{:S(2)}, u32[]{:S(2)}) collective-permute-start(bf16[1024,512]{1,0:T(8,128)(2,1)S(1)} %slice.33), channel_id=1, source_target_pairs={{0,16},{8,72},{16,32},{24,88},{32,48},{40,104},{48,0},{56,120},{64... | collective-permute-start | bytes 3145736 | tf_op jit(solution)/shard_map/ppermute | solution.py:53
  65.9 16.0 %collective-permute-start.14 = (bf16[1024,512]{1,0:T(8,128)(2,1)S(1)}, bf16[1024,512]{1,0:T(8,128)(2,1)}, u32[]{:S(2)}, u32[]{:S(2)}) collective-permute-start(bf16[1024,512]{1,0:T(8,128)(2,1)S(1)} %slice.34), channel_id=1, source_target_pairs={{0,48},{8,200},{16,0},{24,216},{32,16},{40,232},{48,32},{56,248},{... | collective-permute-start | bytes 3145736 | tf_op jit(solution)/shard_map/ppermute | solution.py:53
  70.2 15.2 %collective-permute-start.16 = (bf16[2048,512]{1,0:T(8,128)(2,1)S(1)}, bf16[2048,512]{1,0:T(8,128)(2,1)}, u32[]{:S(2)}, u32[]{:S(2)}) collective-permute-start(bf16[2048,512]{1,0:T(8,128)(2,1)S(1)} %collective-permute-done.11.refs_9_), channel_id=1, source_target_pairs={{0,8},{8,0},{16,24},{24,16},{32,40},{40,32},{48,56},{56,48},{64,72... | collective-permute-start | bytes 6291464 | tf_op jit(solution)/shard_map/ppermute | solution.py:42
  71.2 14.2 %collective-permute-start.17 = (bf16[2048,512]{1,0:T(8,128)(2,1)}, bf16[2048,512]{1,0:T(8,128)(2,1)}, u32[]{:S(2)}, u32[]{:S(2)}) collective-permute-start(bf16[2048,512]{1,0:T(8,128)(2,1)} %collective-permute-done.12.refs_10_), channel_id=1, source_target_pairs={{0,8},{8,0},{16,24},{24,16},{32,40},{40,32},{48,56},{56,48},{64,72... | collective-permute-start | bytes 6291464 | tf_op jit(solution)/shard_map/ppermute | solution.py:42
  80.9 3.0 %collective-permute-start.18 = (bf16[1024,512]{1,0:T(8,128)(2,1)}, bf16[1024,512]{1,0:T(8,128)(2,1)}, u32[]{:S(2)}, u32[]{:S(2)}) collective-permute-start(bf16[1024,512]{1,0:T(8,128)(2,1)} %collective-permute-done.13.refs_11_), channel_id=1, source_target_pairs={{0,8},{8,0},{16,24},{24,16},{32,40},{40,32},{48,56},{56,48},{64,72... | collective-permute-start | bytes 3145736 | tf_op jit(solution)/shard_map/ppermute | solution.py:42
  81.9 3.5 %collective-permute-start.19 = (bf16[1024,512]{1,0:T(8,128)(2,1)}, bf16[1024,512]{1,0:T(8,128)(2,1)}, u32[]{:S(2)}, u32[]{:S(2)}) collective-permute-start(bf16[1024,512]{1,0:T(8,128)(2,1)} %collective-permute-done.14.refs_12_), channel_id=1, source_target_pairs={{0,8},{8,0},{16,24},{24,16},{32,40},{40,32},{48,56},{56,48},{64,72... | collective-permute-start | bytes 3145736 | tf_op jit(solution)/shard_map/ppermute | solution.py:42
  229.2 15.1 %all-to-all-start.1 = ((bf16[8,16,640]{2,1,0:T(8,128)(2,1)}), bf16[8,16,640]{2,1,0:T(8,128)(2,1)S(1)}, u32[]{:S(2)}, u32[]{:S(2)}) async-start(bf16[8,16,640]{2,1,0:T(8,128)(2,1)} %merge_project.1), calls=%async_computation.1 | async-start | bytes 327680 | tf_op jit(solution)/shard_map/all_to_all | solution.py:305
  246.8 17.1 %all-to-all-start.2 = ((bf16[32,16,640]{2,1,0:T(8,128)(2,1)}), bf16[32,16,640]{2,1,0:T(8,128)(2,1)S(1)}, u32[]{:S(2)}, u32[]{:S(2)}) async-start(bf16[32,16,640]{2,1,0:T(8,128)(2,1)} %add_rows.1), calls=%async_computation.2 | async-start | bytes 1310720 | tf_op jit(solution)/shard_map/all_to_all | solution.py:307
  (12 other events, 72.0 us)

commit v2 on v1

--- a/solution.py
+++ b/solution.py
@@ -81,19 +81,10 @@
     return high, (v - high).astype(BF16).astype(F32)
 
 
-def attend_kernel(
-    info, gains, *refs
-):
-    x_parts, w_parts = refs[:8], refs[8:18]
-    out, wo = refs[18:20]
-    xs, ws, ks, vs, qs, scale, sems = refs[20:]
-    sec, tp, first, own_a, own_b = info[0], info[1], info[2], info[3], info[4]
+def shard_places(w_parts, sec):
     core = sec % CORES
     px = sec // (SIDE * CORES)
     py = (sec // CORES) % SIDE
-    for part, off in zip(x_parts, (0, -1, 1, -2, 2, -3, 3, 4)):
-        at = pl.multiple_of(((tp + off + 8) % 8) * 512, 512)
-        pltpu.make_async_copy(part, xs.at[:, pl.ds(at, 512)], sems.at[0]).start()
     shards = []
     for mine in (True, False):
         group = w_parts[:5] if mine else w_parts[5:]
@@ -108,15 +99,19 @@
                 dy = jnp.where(col == 0, r2, r1)
                 s = (((px + dx + SIDE) % SIDE) * SIDE + (py + dy + SIDE) % SIDE) * CORES + col
                 shards.append((ref, row, s))
+    return shards
+
+
+def attend_kernel(info, gains, *refs):
+    x_parts, w_parts = refs[:8], refs[8:18]
+    out, xs, ws, ks, vs, qs, scale, sems = refs[18:]
+    sec, tp, first, own_a, own_b = (info[i] for i in range(5))
+    for part, off in zip(x_parts, (0, -1, 1, -2, 2, -3, 3, 4)):
+        at = pl.multiple_of(((tp + off + 8) % 8) * 512, 512)
+        pltpu.make_async_copy(part, xs.at[:, pl.ds(at, 512)], sems.at[0]).start()
+    shards = shard_places(w_parts, sec)
     for ref, row, s in shards:
         pltpu.make_async_copy(ref.at[pl.ds(row * 512, 384)], ws.at[s], sems.at[1]).start()
-    for ref, row, s in shards:
-        pltpu.make_async_copy(
-            ref.at[pl.ds(row * 512 + 384, 128)],
-            wo.at[pl.ds(pl.multiple_of(s * 128, 128), 128)],
-            sems.at[2],
-        ).start()
-
     lane = lax.broadcasted_iota(jnp.int32, (1, 128), 1)
     rest = jnp.where(lane < 8, ABSENT, 0.0)
     out[:, :512] = jnp.zeros((512, 512), BF16)
@@ -176,7 +171,6 @@
             sums.append(jnp.dot(weights.astype(BF16), v2, preferred_element_type=F32))
         out[window, cols] = jnp.where(lane < 64, sums[0], sums[1]).astype(BF16)
     out[window, 512:640] = stats.astype(BF16)
-    pltpu.make_async_copy(wo, wo, sems.at[2]).wait()
 
 
 def attend(info, gains, x_parts, w_parts):
@@ -185,11 +179,8 @@
     return pl.pallas_call(
         attend_kernel,
         in_specs=[pl.BlockSpec(memory_space=pltpu.SMEM), inside] + [anywhere] * 18,
-        out_specs=[inside, anywhere],
-        out_shape=[
-            jax.ShapeDtypeStruct((512, 640), BF16),
-            jax.ShapeDtypeStruct((4096, 512), BF16),
-        ],
+        out_specs=inside,
+        out_shape=jax.ShapeDtypeStruct((512, 640), BF16),
         scratch_shapes=[
             pltpu.VMEM((640, 4096), BF16),
             pltpu.VMEM((32, 384, 512), BF16),
@@ -197,7 +188,7 @@
             pltpu.VMEM((512, 512), BF16),
             pltpu.VMEM((128, 512), BF16),
             pltpu.VMEM((640, 128), F32),
-            pltpu.SemaphoreType.DMA((3,)),
+            pltpu.SemaphoreType.DMA((2,)),
         ],
         compiler_params=pltpu.CompilerParams(vmem_limit_bytes=40 * 2**20),
         cost_estimate=pl.CostEstimate(
@@ -207,7 +198,15 @@
     )(info, gains, *x_parts, *w_parts)
 
 
-def merge_kernel(got, wo, out):
+def merge_kernel(info, got, *refs):
+    w_parts = refs[:10]
+    out, wo, sem = refs[10:]
+    for ref, row, s in shard_places(w_parts, info[0]):
+        pltpu.make_async_copy(
+            ref.at[pl.ds(row * 512 + 384, 128)],
+            wo.at[pl.ds(pl.multiple_of(s * 128, 128), 128)],
+            sem,
+        ).start()
     st = got[:, 512:640].astype(F32)
     both = st + pltpu.roll(st, 120, 1)
     sum_a = pltpu.roll(both, 112, 1).reshape(32, 16, 128)
@@ -245,6 +244,7 @@
     pool_hi, pool_lo = high_low(pooled)
     row = lax.broadcasted_iota(jnp.int32, (16, 128), 0)
     extra = jnp.where(row == 0, pool_hi, jnp.where(row == 1, pool_lo, 0.0)).astype(BF16)
+    pltpu.make_async_copy(wo, wo, sem).wait()
     for z in range(8):
         term = lax.dot_general(
             context,
@@ -256,13 +256,18 @@
         out[z, :, 512:640] = extra
 
 
-def merge(got, wo):
+def merge(info, got, w_parts):
+    anywhere = pl.BlockSpec(memory_space=pl.ANY)
+    inside = pl.BlockSpec(memory_space=pltpu.VMEM)
     return pl.pallas_call(
         merge_kernel,
+        in_specs=[pl.BlockSpec(memory_space=pltpu.SMEM), inside] + [anywhere] * 10,
+        out_specs=inside,
         out_shape=jax.ShapeDtypeStruct((8, 16, 640), BF16),
+        scratch_shapes=[pltpu.VMEM((4096, 512), BF16), pltpu.SemaphoreType.DMA(())],
         compiler_params=pltpu.CompilerParams(vmem_limit_bytes=40 * 2**20),
         name="merge_project",
-    )(got, wo)
+    )(info, got, *w_parts)
 
 
 def add_kernel(got, rows, out):
@@ -299,9 +304,9 @@
     x_parts = ring_gather(jnp.concatenate([encoded, window], 0))
     w_parts = plane_gather(jnp.concatenate([w_key, w_value, w_query, w_out.T], 0))
     gains = jnp.stack([enc_gain, dec_gain])
-    partial, wo = attend(info, gains, x_parts, w_parts)
+    partial = attend(info, gains, x_parts, w_parts)
     got = lax.all_to_all(partial, "sec", 0, 0, tiled=True)
-    terms = merge(got, wo)
+    terms = merge(info, got, w_parts)
     terms = lax.all_to_all(terms, "tp", 0, 0, tiled=True)
     rows = lax.dynamic_slice_in_dim(decoder_states, sec * 16, 16, 0)
     finished = lax.all_to_all(add_rows(terms, rows), "sec", 0, 0, tiled=True)

time: 266 us -> 166 us (0.62)
  Pallas kernels: 119 us -> 20.7 us
    pallas_call x1, Pallas kernels: 114 us -> 13.6 us  [attend(): pl.pallas_call(attend_kernel, in_specs=[pl.BlockSpec(memory_space=pltpu.S...]
    pallas_call x1, Pallas kernels: 2.52 us -> 5.36 us  [merge(): pl.pallas_call(merge_kernel, in_specs=[pl.BlockSpec(memory_space=pltpu.SM...]
    unnamed x36 -> x34, local copies, waits for them, and re-layouts: 14 us -> 11.8 us
  transfers between devices with their start and end apart: 22 -> 22, of which waited for: 11 -> 11; matrix products, arithmetic and copies ran while one was open for 4% -> 7% of each run, Pallas kernels for 0% -> 0%
where the time goes in v2:
time: 166 us; the launch traced here: 165 us
  waiting for transfers between devices  57.2 us (34%)
  starting transfers between devices  44.5 us (27%)
  blocking collectives  21.5 us (13%)
  Pallas kernels  20.7 us (12%)
  local copies, waits for them, and re-layouts  15.4 us (9%)
  other arithmetic  5.08 us (3%)
    all_to_all x1, blocking collectives, on_device(): got = lax.all_to_all(partial, 'sec', 0, 0, tiled=True)  21.5 us
    ppermute x6, waiting for transfers between devices, along_tp(): return lax.ppermute(v, 'tp', [(i, (i + step) % n) for i in range(n)])  21.1 us
    ppermute x8, starting transfers between devices, in_plane(): return lax.ppermute(v, 'sec', pairs)  15.6 us
    pallas_call x1, Pallas kernels, attend(): pl.pallas_call(attend_kernel, in_specs=[pl.BlockSpec(memory_space=pltpu.S...  13.6 us
    all_to_all x1, waiting for transfers between devices, on_device(): finished = lax.all_to_all(add_rows(terms, rows), 'sec', 0, 0, tiled=True)  13.1 us
    unnamed x34, local copies, waits for them, and re-layouts  11.8 us
    ppermute x6, starting transfers between devices, along_tp(): return lax.ppermute(v, 'tp', [(i, (i + step) % n) for i in range(n)])  11.7 us
    ppermute x8, waiting for transfers between devices, in_plane(): return lax.ppermute(v, 'sec', pairs)  9.92 us
  transfers between devices with their start and end apart: 22, of which 11 were waited for; matrix products, arithmetic and copies ran while one was open for 7% of the time, Pallas kernels for 0%

profile of v2, /device:TPU:1, one launch (start us, length us, event | category | flops | bytes accessed | tf_op | source)
XLA Modules:
  0.0 165.4 jit_solution(11616390129871105260)
XLA Ops:
  2.8 2.2 %collective-permute-start.7 = (bf16[512,512]{1,0:T(8,128)(2,1)S(1)}, bf16[512,512]{1,0:T(8,128)(2,1)S(1)}, u32[]{:S(2)}, u32[]{:S(2)}) collective-permute-start(bf16[512,512]{1,0:T(8,128)(2,1)S(1)} %pad_maximum_fusion.1), channel_id=1, source_target_pairs={{0,64},{8,24},{16,80},{24,40},{32,96},{40,56},{48,112},{56,8},{64,... | collective-permute-start | bytes 1572872 | tf_op jit(solution)/shard_map/ppermute | solution.py:53
  7.2 1.7 %collective-permute-start = (bf16[640,512]{1,0:T(8,128)(2,1)S(1)}, bf16[640,512]{1,0:T(8,128)(2,1)S(1)}, u32[]{:S(2)}, u32[]{:S(2)}) collective-permute-start(bf16[640,512]{1,0:T(8,128)(2,1)S(1)} %pad_maximum_fusion.refs_0_), channel_id=1, source_target_pairs={{0,1},{1,2},{2,3},{3,4},{4,5},{5,6},{6,7},{7,0},{8,9},{9,10},{10,1... | collective-permute-start | bytes 1966088 | tf_op jit(solution)/shard_map/ppermute | solution.py:26
  9.0 4.0 %collective-permute-start.1 = (bf16[640,512]{1,0:T(8,128)(2,1)S(1)}, bf16[640,512]{1,0:T(8,128)(2,1)S(1)}, u32[]{:S(2)}, u32[]{:S(2)}) collective-permute-start(bf16[640,512]{1,0:T(8,128)(2,1)S(1)} %pad_maximum_fusion.refs_0_), channel_id=1, source_target_pairs={{0,7},{1,0},{2,1},{3,2},{4,3},{5,4},{6,5},{7,6},{8,15},{9,8},{10,9... | collective-permute-start | bytes 1966088 | tf_op jit(solution)/shard_map/ppermute | solution.py:26
  17.2 4.1 %collective-permute-done.8 = bf16[512,512]{1,0:T(8,128)(2,1)S(1)} collective-permute-done((bf16[512,512]{1,0:T(8,128)(2,1)S(1)}, bf16[512,512]{1,0:T(8,128)(2,1)S(1)}, u32[]{:S(2)}, u32[]{:S(2)}) %collective-permute-start.8) | collective-permute-done | bytes 524320 | tf_op jit(solution)/shard_map/ppermute | solution.py:53
  21.3 2.8 %collective-permute-start.10 = (bf16[256,512]{1,0:T(8,128)(2,1)S(1)}, bf16[256,512]{1,0:T(8,128)(2,1)S(1)}, u32[]{:S(2)}, u32[]{:S(2)}) collective-permute-start(bf16[256,512]{1,0:T(8,128)(2,1)S(1)} %slice.32), channel_id=1, source_target_pairs={{0,192},{8,56},{16,208},{24,8},{32,224},{40,24},{48,240},{56,40},{... | collective-permute-start | bytes 786440 | tf_op jit(solution)/shard_map/ppermute | solution.py:53
  28.0 2.7 %collective-permute-start.3 = (bf16[640,512]{1,0:T(8,128)(2,1)S(1)}, bf16[640,512]{1,0:T(8,128)(2,1)}, u32[]{:S(2)}, u32[]{:S(2)}) collective-permute-start(bf16[640,512]{1,0:T(8,128)(2,1)S(1)} %collective-permute-done.1.refs_2_), channel_id=1, source_target_pairs={{0,7},{1,0},{2,1},{3,2},{4,3},{5,4},{6,5},{7,6},{8,15},{9,8},{10,9... | collective-permute-start | bytes 1966088 | tf_op jit(solution)/shard_map/ppermute | solution.py:26
  33.4 2.3 %collective-permute-start.12 = (bf16[2048,512]{1,0:T(8,128)(2,1)}, bf16[2048,512]{1,0:T(8,128)(2,1)}, u32[]{:S(2)}, u32[]{:S(2)}) collective-permute-start(bf16[2048,512]{1,0:T(8,128)(2,1)} %constant_dynamic-update-slice_fusion.refs_8_.refs_0_), channel_id=1, source_target_pairs={{0,48},{8,200},{16,0},{24,216},{32,16},{40,232},{48,32},{56,248},{... | collective-permute-start | bytes 6291464 | tf_op jit(solution)/shard_map/ppermute | solution.py:53
  35.7 7.6 %collective-permute-done.2.refs_3_ = bf16[640,512]{1,0:T(8,128)(2,1)} collective-permute-done((bf16[640,512]{1,0:T(8,128)(2,1)S(1)}, bf16[640,512]{1,0:T(8,128)(2,1)}, u32[]{:S(2)}, u32[]{:S(2)}) %collective-permute-start.2) | collective-permute-done | bytes 655392 | tf_op jit(solution)/shard_map/ppermute | solution.py:26
  43.2 3.2 %collective-permute-start.5 = (bf16[640,512]{1,0:T(8,128)(2,1)}, bf16[640,512]{1,0:T(8,128)(2,1)}, u32[]{:S(2)}, u32[]{:S(2)}) collective-permute-start(bf16[640,512]{1,0:T(8,128)(2,1)} %collective-permute-done.3.refs_4_), channel_id=1, source_target_pairs={{0,7},{1,0},{2,1},{3,2},{4,3},{5,4},{6,5},{7,6},{8,15},{9,8},{10,9... | collective-permute-start | bytes 1966088 | tf_op jit(solution)/shard_map/ppermute | solution.py:26
  46.5 12.1 %collective-permute-done.4.refs_5_ = bf16[640,512]{1,0:T(8,128)(2,1)} collective-permute-done((bf16[640,512]{1,0:T(8,128)(2,1)}, bf16[640,512]{1,0:T(8,128)(2,1)}, u32[]{:S(2)}, u32[]{:S(2)}) %collective-permute-start.4) | collective-permute-done | bytes 655392 | tf_op jit(solution)/shard_map/ppermute | solution.py:26
  59.8 3.0 %collective-permute-start.6 = (bf16[640,512]{1,0:T(8,128)(2,1)S(1)}, bf16[640,512]{1,0:T(8,128)(2,1)S(1)}, u32[]{:S(2)}, u32[]{:S(2)}) collective-permute-start(bf16[640,512]{1,0:T(8,128)(2,1)S(1)} %broadcast_select_fusion), channel_id=1, source_target_pairs={{0,1},{1,2},{2,3},{3,4},{4,5},{5,6},{6,7},{7,0},{8,15},{9,8},{10,9... | collective-permute-start | bytes 1966088 | tf_op jit(solution)/shard_map/ppermute | solution.py:37
  65.9 4.3 %collective-permute-start.14 = (bf16[1024,512]{1,0:T(8,128)(2,1)S(1)}, bf16[1024,512]{1,0:T(8,128)(2,1)}, u32[]{:S(2)}, u32[]{:S(2)}) collective-permute-start(bf16[1024,512]{1,0:T(8,128)(2,1)S(1)} %slice.34), channel_id=1, source_target_pairs={{0,48},{8,200},{16,0},{24,216},{32,16},{40,232},{48,32},{56,248},{... | collective-permute-start | bytes 3145736 | tf_op jit(solution)/shard_map/ppermute | solution.py:53
  71.2 4.9 %collective-permute-start.17 = (bf16[2048,512]{1,0:T(8,128)(2,1)}, bf16[2048,512]{1,0:T(8,128)(2,1)}, u32[]{:S(2)}, u32[]{:S(2)}) collective-permute-start(bf16[2048,512]{1,0:T(8,128)(2,1)} %collective-permute-done.12.refs_10_.refs_2_), channel_id=1, source_target_pairs={{0,8},{8,0},{16,24},{24,16},{32,40},{40,32},{48,56},{56,48},{64,72... | collective-permute-start | bytes 6291464 | tf_op jit(solution)/shard_map/ppermute | solution.py:42
  76.1 4.8 %collective-permute-done.13.refs_11_.refs_3_ = bf16[1024,512]{1,0:T(8,128)(2,1)} collective-permute-done((bf16[1024,512]{1,0:T(8,128)(2,1)S(1)}, bf16[1024,512]{1,0:T(8,128)(2,1)}, u32[]{:S(2)}, u32[]{:S(2)}) %collective-permute-start.13) | collective-permute-done | bytes 1048608 | tf_op jit(solution)/shard_map/ppermute | solution.py:53
  82.1 1.8 %collective-permute-done.18.refs_16_.refs_8_ = bf16[1024,512]{1,0:T(8,128)(2,1)} collective-permute-done((bf16[1024,512]{1,0:T(8,128)(2,1)}, bf16[1024,512]{1,0:T(8,128)(2,1)}, u32[]{:S(2)}, u32[]{:S(2)}) %collective-permute-start.18) | collective-permute-done | bytes 1048608 | tf_op jit(solution)/shard_map/ppermute | solution.py:42
  83.9 1.5 collective-permute-done.19.refs_17_.refs_9_
  88.7 13.6 %project_attend.1 = bf16[512,640]{1,0:T(8,128)(2,1)S(1)} custom-call(s32[5]{0:T(128)S(1)} %pad_add_fusion.info, f32[2,4096]{1,0:T(2,128)S(1)} %pad_maximum_fusion.2.gains, bf16[640,512]{1,0:T(8,128)(2,1)S(1)} %pad_maximum_fusion.refs_0_, bf16[640,512]{1,0:T(8,128)(2,1)S(1)} %copy-done.2, bf16[640,512]{1,0:T(8,128)(2,1)S(1)} %copy-done.4, ...), custom_call_target="tpu_custom_call" | custom-call | flops 5000000000 | bytes 31457280 | tf_op jit(solution)/shard_map/project_attend/pallas_call | solution.py:179
  102.3 21.5 %all_to_all.21 = bf16[32,16,640]{2,1,0:T(8,128)(2,1)S(1)} all-to-all(bf16[32,16,640]{2,1,0:T(8,128)(2,1)S(1)} %bitcast.14), channel_id=1, replica_groups=mesh['sec'=32,'tp'=8] {'sec'}, dimensions={0} | all-to-all | bytes 1310720 | tf_op jit(solution)/shard_map/all_to_all | solution.py:308
  123.8 5.4 %merge_project.1 = bf16[8,16,640]{2,1,0:T(8,128)(2,1)} custom-call(s32[5]{0:T(128)S(1)} %pad_add_fusion.info, bf16[512,640]{1,0:T(8,128)(2,1)S(1)} %bitcast.13, bf16[2048,512]{1,0:T(8,128)(2,1)} %constant_dynamic-update-slice_fusion.refs_8_.refs_0_, bf16[2048,512]{1,0:T(8,128)(2,1)S(1)} %collective-permute-done.11.refs_9_.refs_1_, ...), custom_call_target="tpu_custom_call" | custom-call | tf_op jit(solution)/shard_map/merge_project/pallas_call | solution.py:262
  129.1 4.9 %all-to-all-start.1 = ((bf16[8,16,640]{2,1,0:T(8,128)(2,1)}), bf16[8,16,640]{2,1,0:T(8,128)(2,1)S(1)}, u32[]{:S(2)}, u32[]{:S(2)}) async-start(bf16[8,16,640]{2,1,0:T(8,128)(2,1)} %merge_project.1), calls=%async_computation.1 | async-start | bytes 327680 | tf_op jit(solution)/shard_map/all_to_all | solution.py:310
  134.6 9.6 %all-to-all-done.1.got = bf16[8,16,640]{2,1,0:T(8,128)(2,1)S(1)} async-done(((bf16[8,16,640]{2,1,0:T(8,128)(2,1)}), bf16[8,16,640]{2,1,0:T(8,128)(2,1)S(1)}, u32[]{:S(2)}, u32[]{:S(2)}) %all-to-all-start.1) | async-done | bytes 163872 | tf_op jit(solution)/shard_map/all_to_all | solution.py:310
  144.9 1.8 %add_rows.1 = bf16[32,16,640]{2,1,0:T(8,128)(2,1)} custom-call(bf16[8,16,640]{2,1,0:T(8,128)(2,1)} %copy-done.7, bf16[16,512]{1,0:T(8,128)(2,1)} %constant_dynamic-slice_fusion.rows), custom_call_target="tpu_custom_call" | custom-call | tf_op jit(solution)/shard_map/add_rows/pallas_call | solution.py:285
  146.7 4.1 %all-to-all-start.2 = ((bf16[32,16,640]{2,1,0:T(8,128)(2,1)}), bf16[32,16,640]{2,1,0:T(8,128)(2,1)S(1)}, u32[]{:S(2)}, u32[]{:S(2)}) async-start(bf16[32,16,640]{2,1,0:T(8,128)(2,1)} %add_rows.1), calls=%async_computation.2 | async-start | bytes 1310720 | tf_op jit(solution)/shard_map/all_to_all | solution.py:312
  150.8 13.1 %all-to-all-done.2 = bf16[32,16,640]{2,1,0:T(8,128)(2,1)S(1)} async-done(((bf16[32,16,640]{2,1,0:T(8,128)(2,1)}), bf16[32,16,640]{2,1,0:T(8,128)(2,1)S(1)}, u32[]{:S(2)}, u32[]{:S(2)}) %all-to-all-start.2) | async-done | bytes 655392 | tf_op jit(solution)/shard_map/all_to_all | solution.py:312
  (76 shorter events, 27.6 us)
Async XLA Ops:
  2.8 13.6 %collective-permute-start.7 = (bf16[512,512]{1,0:T(8,128)(2,1)S(1)}, bf16[512,512]{1,0:T(8,128)(2,1)S(1)}, u32[]{:S(2)}, u32[]{:S(2)}) collective-permute-start(bf16[512,512]{1,0:T(8,128)(2,1)S(1)} %pad_maximum_fusion.1), channel_id=1, source_target_pairs={{0,64},{8,24},{16,80},{24,40},{32,96},{40,56},{48,112},{56,8},{64,... | collective-permute-start | bytes 1572872 | tf_op jit(solution)/shard_map/ppermute | solution.py:53
  7.2 19.9 %collective-permute-start = (bf16[640,512]{1,0:T(8,128)(2,1)S(1)}, bf16[640,512]{1,0:T(8,128)(2,1)S(1)}, u32[]{:S(2)}, u32[]{:S(2)}) collective-permute-start(bf16[640,512]{1,0:T(8,128)(2,1)S(1)} %pad_maximum_fusion.refs_0_), channel_id=1, source_target_pairs={{0,1},{1,2},{2,3},{3,4},{4,5},{5,6},{6,7},{7,0},{8,9},{9,10},{10,1... | collective-permute-start | bytes 1966088 | tf_op jit(solution)/shard_map/ppermute | solution.py:26
  9.0 19.0 %collective-permute-start.1 = (bf16[640,512]{1,0:T(8,128)(2,1)S(1)}, bf16[640,512]{1,0:T(8,128)(2,1)S(1)}, u32[]{:S(2)}, u32[]{:S(2)}) collective-permute-start(bf16[640,512]{1,0:T(8,128)(2,1)S(1)} %pad_maximum_fusion.refs_0_), channel_id=1, source_target_pairs={{0,7},{1,0},{2,1},{3,2},{4,3},{5,4},{6,5},{7,6},{8,15},{9,8},{10,9... | collective-permute-start | bytes 1966088 | tf_op jit(solution)/shard_map/ppermute | solution.py:26
  13.0 8.3 %collective-permute-start.8 = (bf16[512,512]{1,0:T(8,128)(2,1)S(1)}, bf16[512,512]{1,0:T(8,128)(2,1)S(1)}, u32[]{:S(2)}, u32[]{:S(2)}) collective-permute-start(bf16[512,512]{1,0:T(8,128)(2,1)S(1)} %pad_maximum_fusion.1), channel_id=1, source_target_pairs={{0,192},{8,56},{16,208},{24,8},{32,224},{40,24},{48,240},{56,40},{... | collective-permute-start | bytes 1572872 | tf_op jit(solution)/shard_map/ppermute | solution.py:53
  16.5 14.2 %collective-permute-start.9 = (bf16[256,512]{1,0:T(8,128)(2,1)S(1)}, bf16[256,512]{1,0:T(8,128)(2,1)S(1)}, u32[]{:S(2)}, u32[]{:S(2)}) collective-permute-start(bf16[256,512]{1,0:T(8,128)(2,1)S(1)} %slice.31), channel_id=1, source_target_pairs={{0,64},{8,24},{16,80},{24,40},{32,96},{40,56},{48,112},{56,8},{64,... | collective-permute-start | bytes 786440 | tf_op jit(solution)/shard_map/ppermute | solution.py:53
  21.3 10.1 %collective-permute-start.10 = (bf16[256,512]{1,0:T(8,128)(2,1)S(1)}, bf16[256,512]{1,0:T(8,128)(2,1)S(1)}, u32[]{:S(2)}, u32[]{:S(2)}) collective-permute-start(bf16[256,512]{1,0:T(8,128)(2,1)S(1)} %slice.32), channel_id=1, source_target_pairs={{0,192},{8,56},{16,208},{24,8},{32,224},{40,24},{48,240},{56,40},{... | collective-permute-start | bytes 786440 | tf_op jit(solution)/shard_map/ppermute | solution.py:53
  27.1 16.1 %collective-permute-start.2 = (bf16[640,512]{1,0:T(8,128)(2,1)S(1)}, bf16[640,512]{1,0:T(8,128)(2,1)}, u32[]{:S(2)}, u32[]{:S(2)}) collective-permute-start(bf16[640,512]{1,0:T(8,128)(2,1)S(1)} %collective-permute-done.refs_1_), channel_id=1, source_target_pairs={{0,1},{1,2},{2,3},{3,4},{4,5},{5,6},{6,7},{7,0},{8,9},{9,10},{10,1... | collective-permute-start | bytes 1966088 | tf_op jit(solution)/shard_map/ppermute | solution.py:26
  28.0 15.2 %collective-permute-start.3 = (bf16[640,512]{1,0:T(8,128)(2,1)S(1)}, bf16[640,512]{1,0:T(8,128)(2,1)}, u32[]{:S(2)}, u32[]{:S(2)}) collective-permute-start(bf16[640,512]{1,0:T(8,128)(2,1)S(1)} %collective-permute-done.1.refs_2_), channel_id=1, source_target_pairs={{0,7},{1,0},{2,1},{3,2},{4,3},{5,4},{6,5},{7,6},{8,15},{9,8},{10,9... | collective-permute-start | bytes 1966088 | tf_op jit(solution)/shard_map/ppermute | solution.py:26
  32.1 31.1 %collective-permute-start.11 = (bf16[2048,512]{1,0:T(8,128)(2,1)}, bf16[2048,512]{1,0:T(8,128)(2,1)S(1)}, u32[]{:S(2)}, u32[]{:S(2)}) collective-permute-start(bf16[2048,512]{1,0:T(8,128)(2,1)} %constant_dynamic-update-slice_fusion.refs_8_.refs_0_), channel_id=1, source_target_pairs={{0,16},{8,72},{16,32},{24,88},{32,48},{40,104},{48,0},{56,120},{64... | collective-permute-start | bytes 6291464 | tf_op jit(solution)/shard_map/ppermute | solution.py:53
  33.4 31.3 %collective-permute-start.12 = (bf16[2048,512]{1,0:T(8,128)(2,1)}, bf16[2048,512]{1,0:T(8,128)(2,1)}, u32[]{:S(2)}, u32[]{:S(2)}) collective-permute-start(bf16[2048,512]{1,0:T(8,128)(2,1)} %constant_dynamic-update-slice_fusion.refs_8_.refs_0_), channel_id=1, source_target_pairs={{0,48},{8,200},{16,0},{24,216},{32,16},{40,232},{48,32},{56,248},{... | collective-permute-start | bytes 6291464 | tf_op jit(solution)/shard_map/ppermute | solution.py:53
  43.2 15.4 %collective-permute-start.4 = (bf16[640,512]{1,0:T(8,128)(2,1)}, bf16[640,512]{1,0:T(8,128)(2,1)}, u32[]{:S(2)}, u32[]{:S(2)}) collective-permute-start(bf16[640,512]{1,0:T(8,128)(2,1)} %collective-permute-done.2.refs_3_), channel_id=1, source_target_pairs={{0,1},{1,2},{2,3},{3,4},{4,5},{5,6},{6,7},{7,0},{8,9},{9,10},{10,1... | collective-permute-start | bytes 1966088 | tf_op jit(solution)/shard_map/ppermute | solution.py:26
  43.2 15.4 %collective-permute-start.5 = (bf16[640,512]{1,0:T(8,128)(2,1)}, bf16[640,512]{1,0:T(8,128)(2,1)}, u32[]{:S(2)}, u32[]{:S(2)}) collective-permute-start(bf16[640,512]{1,0:T(8,128)(2,1)} %collective-permute-done.3.refs_4_), channel_id=1, source_target_pairs={{0,7},{1,0},{2,1},{3,2},{4,3},{5,4},{6,5},{7,6},{8,15},{9,8},{10,9... | collective-permute-start | bytes 1966088 | tf_op jit(solution)/shard_map/ppermute | solution.py:26
  59.8 22.3 %copy-start.11 = (f32[4096]{0:T(1024)S(1)}, f32[4096]{0:T(1024)}, u32[]{:S(2)}) copy-start(f32[4096]{0:T(1024)} %param.13) | copy-start | bytes 49156
  59.8 22.3 %copy-start.12 = (f32[4096]{0:T(1024)S(1)}, f32[4096]{0:T(1024)}, u32[]{:S(2)}) copy-start(f32[4096]{0:T(1024)} %param.12) | copy-start | bytes 49156
  59.8 10.6 %collective-permute-start.6 = (bf16[640,512]{1,0:T(8,128)(2,1)S(1)}, bf16[640,512]{1,0:T(8,128)(2,1)S(1)}, u32[]{:S(2)}, u32[]{:S(2)}) collective-permute-start(bf16[640,512]{1,0:T(8,128)(2,1)S(1)} %broadcast_select_fusion), channel_id=1, source_target_pairs={{0,1},{1,2},{2,3},{3,4},{4,5},{5,6},{6,7},{7,0},{8,15},{9,8},{10,9... | collective-permute-start | bytes 1966088 | tf_op jit(solution)/shard_map/ppermute | solution.py:37
  62.8 19.2 %collective-permute-start.15 = (bf16[2048,512]{1,0:T(8,128)(2,1)}, bf16[2048,512]{1,0:T(8,128)(2,1)}, u32[]{:S(2)}, u32[]{:S(2)}) collective-permute-start(bf16[2048,512]{1,0:T(8,128)(2,1)} %constant_dynamic-update-slice_fusion.refs_8_.refs_0_), channel_id=1, source_target_pairs={{0,8},{8,0},{16,24},{24,16},{32,40},{40,32},{48,56},{56,48},{64,72... | collective-permute-start | bytes 6291464 | tf_op jit(solution)/shard_map/ppermute | solution.py:42
  63.3 17.6 %collective-permute-start.13 = (bf16[1024,512]{1,0:T(8,128)(2,1)S(1)}, bf16[1024,512]{1,0:T(8,128)(2,1)}, u32[]{:S(2)}, u32[]{:S(2)}) collective-permute-start(bf16[1024,512]{1,0:T(8,128)(2,1)S(1)} %slice.33), channel_id=1, source_target_pairs={{0,16},{8,72},{16,32},{24,88},{32,48},{40,104},{48,0},{56,120},{64... | collective-permute-start | bytes 3145736 | tf_op jit(solution)/shard_map/ppermute | solution.py:53
  65.9 16.0 %collective-permute-start.14 = (bf16[1024,512]{1,0:T(8,128)(2,1)S(1)}, bf16[1024,512]{1,0:T(8,128)(2,1)}, u32[]{:S(2)}, u32[]{:S(2)}) collective-permute-start(bf16[1024,512]{1,0:T(8,128)(2,1)S(1)} %slice.34), channel_id=1, source_target_pairs={{0,48},{8,200},{16,0},{24,216},{32,16},{40,232},{48,32},{56,248},{... | collective-permute-start | bytes 3145736 | tf_op jit(solution)/shard_map/ppermute | solution.py:53
  70.2 15.2 %collective-permute-start.16 = (bf16[2048,512]{1,0:T(8,128)(2,1)S(1)}, bf16[2048,512]{1,0:T(8,128)(2,1)}, u32[]{:S(2)}, u32[]{:S(2)}) collective-permute-start(bf16[2048,512]{1,0:T(8,128)(2,1)S(1)} %collective-permute-done.11.refs_9_.refs_1_), channel_id=1, source_target_pairs={{0,8},{8,0},{16,24},{24,16},{32,40},{40,32},{48,56},{56,48},{64,72... | collective-permute-start | bytes 6291464 | tf_op jit(solution)/shard_map/ppermute | solution.py:42
  71.2 14.2 %collective-permute-start.17 = (bf16[2048,512]{1,0:T(8,128)(2,1)}, bf16[2048,512]{1,0:T(8,128)(2,1)}, u32[]{:S(2)}, u32[]{:S(2)}) collective-permute-start(bf16[2048,512]{1,0:T(8,128)(2,1)} %collective-permute-done.12.refs_10_.refs_2_), channel_id=1, source_target_pairs={{0,8},{8,0},{16,24},{24,16},{32,40},{40,32},{48,56},{56,48},{64,72... | collective-permute-start | bytes 6291464 | tf_op jit(solution)/shard_map/ppermute | solution.py:42
  80.9 3.0 %collective-permute-start.18 = (bf16[1024,512]{1,0:T(8,128)(2,1)}, bf16[1024,512]{1,0:T(8,128)(2,1)}, u32[]{:S(2)}, u32[]{:S(2)}) collective-permute-start(bf16[1024,512]{1,0:T(8,128)(2,1)} %collective-permute-done.13.refs_11_.refs_3_), channel_id=1, source_target_pairs={{0,8},{8,0},{16,24},{24,16},{32,40},{40,32},{48,56},{56,48},{64,72... | collective-permute-start | bytes 3145736 | tf_op jit(solution)/shard_map/ppermute | solution.py:42
  81.9 3.5 %collective-permute-start.19 = (bf16[1024,512]{1,0:T(8,128)(2,1)}, bf16[1024,512]{1,0:T(8,128)(2,1)}, u32[]{:S(2)}, u32[]{:S(2)}) collective-permute-start(bf16[1024,512]{1,0:T(8,128)(2,1)} %collective-permute-done.14.refs_12_.refs_4_), channel_id=1, source_target_pairs={{0,8},{8,0},{16,24},{24,16},{32,40},{40,32},{48,56},{56,48},{64,72... | collective-permute-start | bytes 3145736 | tf_op jit(solution)/shard_map/ppermute | solution.py:42
  129.1 15.1 %all-to-all-start.1 = ((bf16[8,16,640]{2,1,0:T(8,128)(2,1)}), bf16[8,16,640]{2,1,0:T(8,128)(2,1)S(1)}, u32[]{:S(2)}, u32[]{:S(2)}) async-start(bf16[8,16,640]{2,1,0:T(8,128)(2,1)} %merge_project.1), calls=%async_computation.1 | async-start | bytes 327680 | tf_op jit(solution)/shard_map/all_to_all | solution.py:310
  146.7 17.1 %all-to-all-start.2 = ((bf16[32,16,640]{2,1,0:T(8,128)(2,1)}), bf16[32,16,640]{2,1,0:T(8,128)(2,1)S(1)}, u32[]{:S(2)}, u32[]{:S(2)}) async-start(bf16[32,16,640]{2,1,0:T(8,128)(2,1)} %add_rows.1), calls=%async_computation.2 | async-start | bytes 1310720 | tf_op jit(solution)/shard_map/all_to_all | solution.py:312
  (11 other events, 69.8 us)

commit v3 on v2

--- a/solution.py
+++ b/solution.py
@@ -53,27 +53,33 @@
     return lax.ppermute(v, "sec", pairs)
 
 
-def ring_gather(piece):
-    core = lax.axis_index("sec") % CORES
-    up = down = piece
-    held = [piece]
-    for _ in range(3):
-        up, down = along_tp(up, 1), along_tp(down, -1)
-        held += [up, down]
-    held.append(along_tp_by_core(jnp.where(core == 0, up, down)))
-    return held
-
-
-def plane_gather(shard):
+def gather(tokens, shard):
+    together = lax.optimization_barrier
     half = shard.shape[0] // 2
+    theirs = other_core(tokens)
+    mine1, theirs1 = along_tp_by_core(tokens), along_tp_by_core(theirs)
     a, b = in_plane(shard, 1, False), in_plane(shard, -1, False)
+    a, b, mine1 = together((a, b, mine1))
     c, d = in_plane(a[:half], 1, False), in_plane(b[half:], -1, False)
+    mine2 = along_tp_by_core(mine1)
+    c, d, theirs1 = together((c, d, theirs1))
+    theirs2 = along_tp_by_core(theirs1)
     g = jnp.concatenate([shard, a, b, c, d], 0)
-    ga, gb = in_plane(g, 1, True), in_plane(g, -1, True)
+    g2, mine2 = together((g, mine2))
+    ga, gb = in_plane(g, 1, True), in_plane(g2, -1, True)
+    mine3 = along_tp_by_core(mine2)
+    passed1 = other_core(theirs1)
+    theirs3 = along_tp_by_core(theirs2)
+    mine4 = along_tp_by_core(mine3)
+    passed2, go = other_core(theirs2), other_core(g2)
+    ga, mine3, passed1 = together((ga, mine3, passed1))
     half = g.shape[0] // 2
     gc, gd = in_plane(ga[:half], 1, True), in_plane(gb[half:], -1, True)
-    own = [g, ga, gb, gc, gd]
-    return own + [other_core(v) for v in own]
+    theirs3, ga2, gb2, mine4, passed2 = together((theirs3, ga, gb, mine4, passed2))
+    passed3, gao, gbo = other_core(theirs3), other_core(ga2), other_core(gb2)
+    gc, gd, mine4 = together((gc, gd, mine4))
+    held = [tokens, mine1, mine2, mine3, mine4, passed1, passed2, passed3]
+    return held, [g, ga, gb, gc, gd, go, gao, gbo, other_core(gc), other_core(gd)]
 
 
 def high_low(v):
@@ -106,12 +112,16 @@
     x_parts, w_parts = refs[:8], refs[8:18]
     out, xs, ws, ks, vs, qs, scale, sems = refs[18:]
     sec, tp, first, own_a, own_b = (info[i] for i in range(5))
-    for part, off in zip(x_parts, (0, -1, 1, -2, 2, -3, 3, 4)):
-        at = pl.multiple_of(((tp + off + 8) % 8) * 512, 512)
+    turn = 2 * (sec % CORES) - 1
+    for part, off in zip(x_parts, (0, 1, 2, 3, 4, -1, -2, -3)):
+        at = pl.multiple_of(((tp + turn * off + 8) % 8) * 512, 512)
         pltpu.make_async_copy(part, xs.at[:, pl.ds(at, 512)], sems.at[0]).start()
     shards = shard_places(w_parts, sec)
-    for ref, row, s in shards:
-        pltpu.make_async_copy(ref.at[pl.ds(row * 512, 384)], ws.at[s], sems.at[1]).start()
+    for kind in (2, 0, 1):
+        for ref, row, s in shards:
+            pltpu.make_async_copy(
+                ref.at[pl.ds(row * 512 + kind * 128, 128)], ws.at[kind, s], sems.at[1 + kind]
+            ).start()
     lane = lax.broadcasted_iota(jnp.int32, (1, 128), 1)
     rest = jnp.where(lane < 8, ABSENT, 0.0)
     out[:, :512] = jnp.zeros((512, 512), BF16)
@@ -131,20 +141,15 @@
             xs[rows, cols] = (v * gains[which, cols]).astype(BF16)
         scale[rows, :] = jnp.broadcast_to(lax.rsqrt(total / 4096.0 + 1e-06), (128, 128))
 
-    pltpu.make_async_copy(ws, ws, sems.at[1]).wait()
-
-    @pl.loop(0, 2)
-    def _(n):
-        cols = pl.ds(pl.multiple_of(n * 256, 256), 256)
-        wq = ws[:, 256:384, cols].reshape(4096, 256)
-        q = jnp.dot(xs[512:640, :], wq, preferred_element_type=F32)
-        qs[:, cols] = (q * scale[512:640, 0:1]).astype(BF16)
-        wk = ws[:, 0:128, cols].reshape(4096, 256)
-        k = jnp.dot(xs[0:512, :], wk, preferred_element_type=F32)
-        ks[:, cols] = (k * scale[0:512, 0:1]).astype(BF16)
-        wv = ws[:, 128:256, cols].reshape(4096, 256)
-        v = jnp.dot(xs[0:512, :], wv, preferred_element_type=F32)
-        vs[:, cols] = (v * scale[0:512, 0:1]).astype(BF16)
+    for kind, rows, held in ((2, slice(512, 640), qs), (0, slice(0, 512), ks), (1, slice(0, 512), vs)):
+        pltpu.make_async_copy(ws.at[kind], ws.at[kind], sems.at[1 + kind]).wait()
+
+        @pl.loop(0, 2)
+        def _(n):
+            cols = pl.ds(pl.multiple_of(n * 256, 256), 256)
+            part = ws[kind, :, :, cols].reshape(4096, 256)
+            product = jnp.dot(xs[rows, :], part, preferred_element_type=F32)
+            held[:, cols] = (product * scale[rows, 0:1]).astype(BF16)
 
     row_owner = first + lax.broadcasted_iota(jnp.int32, (128, 512), 0) // QTOK
     key_owner = jnp.where(lax.broadcasted_iota(jnp.int32, (128, 512), 1) < PTOK, own_a, own_b)
@@ -183,14 +188,14 @@
         out_shape=jax.ShapeDtypeStruct((512, 640), BF16),
         scratch_shapes=[
             pltpu.VMEM((640, 4096), BF16),
-            pltpu.VMEM((32, 384, 512), BF16),
+            pltpu.VMEM((3, 32, 128, 512), BF16),
             pltpu.VMEM((512, 512), BF16),
             pltpu.VMEM((512, 512), BF16),
             pltpu.VMEM((128, 512), BF16),
             pltpu.VMEM((640, 128), F32),
-            pltpu.SemaphoreType.DMA((2,)),
+            pltpu.SemaphoreType.DMA((4,)),
         ],
-        compiler_params=pltpu.CompilerParams(vmem_limit_bytes=40 * 2**20),
+        compiler_params=pltpu.CompilerParams(vmem_limit_bytes=54 * 2**20),
         cost_estimate=pl.CostEstimate(
             flops=5 * 10**9, bytes_accessed=30 * 2**20, transcendentals=2**19
         ),
@@ -198,15 +203,33 @@
     )(info, gains, *x_parts, *w_parts)
 
 
-def merge_kernel(info, got, *refs):
+def assemble_kernel(info, *refs):
     w_parts = refs[:10]
-    out, wo, sem = refs[10:]
+    wo, sem = refs[10:]
     for ref, row, s in shard_places(w_parts, info[0]):
         pltpu.make_async_copy(
             ref.at[pl.ds(row * 512 + 384, 128)],
             wo.at[pl.ds(pl.multiple_of(s * 128, 128), 128)],
             sem,
         ).start()
+    pltpu.make_async_copy(wo, wo, sem).wait()
+
+
+def assemble(info, w_parts):
+    anywhere = pl.BlockSpec(memory_space=pl.ANY)
+    return pl.pallas_call(
+        assemble_kernel,
+        in_specs=[pl.BlockSpec(memory_space=pltpu.SMEM)] + [anywhere] * 10,
+        out_specs=pl.BlockSpec(memory_space=pltpu.VMEM),
+        out_shape=jax.ShapeDtypeStruct((4096, 512), BF16),
+        scratch_shapes=[pltpu.SemaphoreType.DMA(())],
+        compiler_params=pltpu.CompilerParams(vmem_limit_bytes=58 * 2**20),
+        cost_estimate=pl.CostEstimate(flops=0, bytes_accessed=8 * 2**20, transcendentals=0),
+        name="assemble_out",
+    )(info, *w_parts)
+
+
+def merge_kernel(got, wo, out):
     st = got[:, 512:640].astype(F32)
     both = st + pltpu.roll(st, 120, 1)
     sum_a = pltpu.roll(both, 112, 1).reshape(32, 16, 128)
@@ -244,7 +267,6 @@
     pool_hi, pool_lo = high_low(pooled)
     row = lax.broadcasted_iota(jnp.int32, (16, 128), 0)
     extra = jnp.where(row == 0, pool_hi, jnp.where(row == 1, pool_lo, 0.0)).astype(BF16)
-    pltpu.make_async_copy(wo, wo, sem).wait()
     for z in range(8):
         term = lax.dot_general(
             context,
@@ -256,18 +278,13 @@
         out[z, :, 512:640] = extra
 
 
-def merge(info, got, w_parts):
-    anywhere = pl.BlockSpec(memory_space=pl.ANY)
-    inside = pl.BlockSpec(memory_space=pltpu.VMEM)
+def merge(got, wo):
     return pl.pallas_call(
         merge_kernel,
-        in_specs=[pl.BlockSpec(memory_space=pltpu.SMEM), inside] + [anywhere] * 10,
-        out_specs=inside,
         out_shape=jax.ShapeDtypeStruct((8, 16, 640), BF16),
-        scratch_shapes=[pltpu.VMEM((4096, 512), BF16), pltpu.SemaphoreType.DMA(())],
-        compiler_params=pltpu.CompilerParams(vmem_limit_bytes=40 * 2**20),
+        compiler_params=pltpu.CompilerParams(vmem_limit_bytes=58 * 2**20),
         name="merge_project",
-    )(info, got, *w_parts)
+    )(got, wo)
 
 
 def add_kernel(got, rows, out):
@@ -289,24 +306,61 @@
     )(got, rows)
 
 
+def pack_kernel(
+    info, encoded, states, w_key, w_value, w_query, w_out, gain_a, gain_b, tokens, shard, gains
+):
+    gains[0:1, :] = gain_a[...]
+    gains[1:2, :] = gain_b[...]
+    tokens[0:512, :] = encoded[...]
+    tokens[512:640, :] = states[pl.ds(pl.multiple_of(info[2] * QTOK, QTOK), 2 * QTOK), :]
+    shard[0:128, :] = w_key[...]
+    shard[128:256, :] = w_value[...]
+    shard[256:384, :] = w_query[...]
+    shard[384:512, :] = w_out[...].T
+
+
+def pack(info, *arrays):
+    inside = pl.BlockSpec(memory_space=pltpu.VMEM)
+    return pl.pallas_call(
+        pack_kernel,
+        in_specs=[pl.BlockSpec(memory_space=pltpu.SMEM)] + [inside] * 8,
+        out_specs=[inside] * 3,
+        out_shape=[
+            jax.ShapeDtypeStruct((640, 512), BF16),
+            jax.ShapeDtypeStruct((512, 512), BF16),
+            jax.ShapeDtypeStruct((2, 4096), F32),
+        ],
+        name="pack",
+    )(info, *arrays)
+
+
 def on_device(
     encoded, decoder_states, passage_counts, enc_gain, dec_gain, w_key, w_value, w_query, w_out
 ):
     sec = lax.axis_index("sec")
     tp = lax.axis_index("tp")
     questions = decoder_states.shape[0] // QTOK
-    ends = jnp.cumsum(passage_counts)
+    order = jnp.arange(questions, dtype=jnp.int32)
+    ends = jnp.sum(jnp.where(order[:, None] <= order[None, :], passage_counts[:, None], 0), axis=0)
     slots = sec * 2 + jnp.arange(2, dtype=jnp.int32)
     owner = jnp.sum((slots[:, None] >= ends[None, :]).astype(jnp.int32), axis=1)
     first = jnp.minimum(owner[0], questions - 2)
     info = jnp.stack([sec, tp, first, owner[0], owner[1]]).astype(jnp.int32)
-    window = lax.dynamic_slice_in_dim(decoder_states, first * QTOK, 2 * QTOK, 0)
-    x_parts = ring_gather(jnp.concatenate([encoded, window], 0))
-    w_parts = plane_gather(jnp.concatenate([w_key, w_value, w_query, w_out.T], 0))
-    gains = jnp.stack([enc_gain, dec_gain])
+    tokens, shard, gains = pack(
+        info,
+        encoded,
+        decoder_states,
+        w_key,
+        w_value,
+        w_query,
+        w_out,
+        enc_gain.reshape(1, -1),
+        dec_gain.reshape(1, -1),
+    )
+    x_parts, w_parts = gather(tokens, shard)
     partial = attend(info, gains, x_parts, w_parts)
     got = lax.all_to_all(partial, "sec", 0, 0, tiled=True)
-    terms = merge(info, got, w_parts)
+    terms = merge(got, assemble(info, w_parts))
     terms = lax.all_to_all(terms, "tp", 0, 0, tiled=True)
     rows = lax.dynamic_slice_in_dim(decoder_states, sec * 16, 16, 0)
     finished = lax.all_to_all(add_rows(terms, rows), "sec", 0, 0, tiled=True)

time: 166 us -> 167 us (level)
  blocking collectives: 21.5 us -> 0 us
  starting transfers between devices: 44.5 us -> 58.8 us
  waiting for transfers between devices: 57.2 us -> 66.3 us
  Pallas kernels: 20.7 us -> 28.6 us
  local copies, waits for them, and re-layouts: 15.4 us -> 9.77 us
  other arithmetic: 5.08 us -> 2.18 us
    all_to_all x1 -> x0, blocking collectives: 21.5 us -> none  [on_device(): got = lax.all_to_all(partial, 'sec', 0, 0, tiled=True)]
    ppermute x6 -> x0, waiting for transfers between devices: 21.1 us -> none  [along_tp(): return lax.ppermute(v, 'tp', [(i, (i + step) % n) for i in range(n)])]
    ppermute x1 -> x7, waiting for transfers between devices: 0.16 us -> 19.3 us  [along_tp_by_core(): return lax.ppermute(v, ('sec', 'tp'), pairs)]
    ppermute x6 -> x0, starting transfers between devices: 11.7 us -> none  [along_tp(): return lax.ppermute(v, 'tp', [(i, (i + step) % n) for i in range(n)])]
    ppermute x1 -> x7, starting transfers between devices: 3.05 us -> 14.6 us  [along_tp_by_core(): return lax.ppermute(v, ('sec', 'tp'), pairs)]
    ppermute x5 -> x9, starting transfers between devices: 5.33 us -> 15.6 us  [other_core(): return lax.ppermute(v, 'sec', [(i, i ^ 1) for i in range(s)])]
    all_to_all x0 -> x1, waiting for transfers between devices: none -> 7.96 us  [on_device(): got = lax.all_to_all(partial, 'sec', 0, 0, tiled=True)]
    pallas_call x1 -> x3, Pallas kernels: 5.36 us -> 12.3 us  [the longest x1 4.97 us: assemble(): pl.pallas_call(assemble_kernel, in_specs=[pl.BlockSpec(memory_space=pltpu...]
  transfers between devices with their start and end apart: 22 -> 27, of which waited for: 11 -> 13; matrix products, arithmetic and copies ran while one was open for 7% -> 2% of each run, Pallas kernels for 0% -> 3%
where the time goes in v3:
time: 167 us
  waiting for transfers between devices  66.3 us (40%)
  starting transfers between devices  58.8 us (35%)
  Pallas kernels  28.6 us (17%)
  local copies, waits for them, and re-layouts  9.77 us (6%)
  other arithmetic  2.18 us (1%)
    ppermute x7, waiting for transfers between devices, along_tp_by_core(): return lax.ppermute(v, ('sec', 'tp'), pairs)  19.3 us
    ppermute x9, starting transfers between devices, other_core(): return lax.ppermute(v, 'sec', [(i, i ^ 1) for i in range(s)])  15.6 us
    ppermute x7, starting transfers between devices, along_tp_by_core(): return lax.ppermute(v, ('sec', 'tp'), pairs)  14.6 us
    pallas_call x1, Pallas kernels, attend(): pl.pallas_call(attend_kernel, in_specs=[pl.BlockSpec(memory_space=pltpu.S...  14.4 us
    all_to_all x1, waiting for transfers between devices, on_device(): finished = lax.all_to_all(add_rows(terms, rows), 'sec', 0, 0, tiled=True)  13.1 us
    ppermute x8, starting transfers between devices, in_plane(): return lax.ppermute(v, 'sec', pairs)  12.9 us
    ppermute x8, waiting for transfers between devices, in_plane(): return lax.ppermute(v, 'sec', pairs)  12.8 us
    all_to_all x1, waiting for transfers between devices, on_device(): terms = lax.all_to_all(terms, 'tp', 0, 0, tiled=True)  8.91 us
  transfers between devices with their start and end apart: 27, of which 13 were waited for; matrix products, arithmetic and copies ran while one was open for 2% of the time, Pallas kernels for 3%

profile of v3, /device:TPU:1, one launch (start us, length us, event | category | flops | bytes accessed | tf_op | source)
XLA Modules:
  0.0 166.5 jit_solution(12032906298323465023)
XLA Ops:
  4.7 3.2 %collective-permute-start.5 = (bf16[640,512]{1,0:T(8,128)(2,1)}, bf16[640,512]{1,0:T(8,128)(2,1)S(1)}, u32[]{:S(2)}, u32[]{:S(2)}) collective-permute-start(bf16[640,512]{1,0:T(8,128)(2,1)} %get-tuple-element.25.refs_0_), channel_id=1, source_target_pairs={{0,8},{8,0},{16,24},{24,16},{32,40},{40,32},{48,56},{56,48},{64,72... | collective-permute-start | bytes 1966088 | tf_op jit(solution)/shard_map/ppermute | solution.py:42
  7.9 3.8 %collective-permute-start.2 = (bf16[640,512]{1,0:T(8,128)(2,1)}, bf16[640,512]{1,0:T(8,128)(2,1)S(1)}, u32[]{:S(2)}, u32[]{:S(2)}) collective-permute-start(bf16[640,512]{1,0:T(8,128)(2,1)} %get-tuple-element.25.refs_0_), channel_id=1, source_target_pairs={{0,1},{1,2},{2,3},{3,4},{4,5},{5,6},{6,7},{7,0},{8,15},{9,8},{10,9... | collective-permute-start | bytes 1966088 | tf_op jit(solution)/shard_map/ppermute | solution.py:37
  15.2 6.3 %collective-permute-done = bf16[512,512]{1,0:T(8,128)(2,1)S(1)} collective-permute-done((bf16[512,512]{1,0:T(8,128)(2,1)}, bf16[512,512]{1,0:T(8,128)(2,1)S(1)}, u32[]{:S(2)}, u32[]{:S(2)}) %collective-permute-start) | collective-permute-done | bytes 524320 | tf_op jit(solution)/shard_map/ppermute | solution.py:53
  30.0 5.4 %collective-permute-done.7.refs_2_ = bf16[640,512]{1,0:T(8,128)(2,1)S(1)} collective-permute-done((bf16[640,512]{1,0:T(8,128)(2,1)S(1)}, bf16[640,512]{1,0:T(8,128)(2,1)S(1)}, u32[]{:S(2)}, u32[]{:S(2)}) %collective-permute-start.7) | collective-permute-done | bytes 655392 | tf_op jit(solution)/shard_map/ppermute | solution.py:37
  35.4 2.5 %collective-permute-start.12 = (bf16[2048,512]{1,0:T(8,128)(2,1)S(1)}, bf16[2048,512]{1,0:T(8,128)(2,1)S(1)}, u32[]{:S(2)}, u32[]{:S(2)}) collective-permute-start(bf16[2048,512]{1,0:T(8,128)(2,1)S(1)} %constant_dynamic-update-slice_fusion.refs_8_.refs_0_), channel_id=1, source_target_pairs={{0,48},{8,200},{16,0},{24,216},{32,16},{40,232},{48,32},{56,248},{... | collective-permute-start | bytes 6291464 | tf_op jit(solution)/shard_map/ppermute | solution.py:53
  41.7 6.0 %collective-permute-done.14 = bf16[640,512]{1,0:T(8,128)(2,1)S(1)} collective-permute-done((bf16[640,512]{1,0:T(8,128)(2,1)S(1)}, bf16[640,512]{1,0:T(8,128)(2,1)S(1)}, u32[]{:S(2)}, u32[]{:S(2)}) %collective-permute-start.14) | collective-permute-done | bytes 655392 | tf_op jit(solution)/shard_map/ppermute | solution.py:37
  47.7 3.4 %collective-permute-start.15 = (bf16[640,512]{1,0:T(8,128)(2,1)S(1)}, bf16[640,512]{1,0:T(8,128)(2,1)S(1)}, u32[]{:S(2)}, u32[]{:S(2)}) collective-permute-start(bf16[640,512]{1,0:T(8,128)(2,1)S(1)} %collective-permute-done.14), channel_id=1, source_target_pairs={{0,1},{1,2},{2,3},{3,4},{4,5},{5,6},{6,7},{7,0},{8,15},{9,8},{10,9... | collective-permute-start | bytes 1966088 | tf_op jit(solution)/shard_map/ppermute | solution.py:37
  51.1 3.6 %collective-permute-done.9.refs_3_ = bf16[640,512]{1,0:T(8,128)(2,1)S(1)} collective-permute-done((bf16[640,512]{1,0:T(8,128)(2,1)S(1)}, bf16[640,512]{1,0:T(8,128)(2,1)S(1)}, u32[]{:S(2)}, u32[]{:S(2)}) %collective-permute-start.9) | collective-permute-done | bytes 655392 | tf_op jit(solution)/shard_map/ppermute | solution.py:37
  54.7 3.1 %collective-permute-start.16 = (bf16[640,512]{1,0:T(8,128)(2,1)S(1)}, bf16[640,512]{1,0:T(8,128)(2,1)S(1)}, u32[]{:S(2)}, u32[]{:S(2)}) collective-permute-start(bf16[640,512]{1,0:T(8,128)(2,1)S(1)} %collective-permute-done.9.refs_3_), channel_id=1, source_target_pairs={{0,1},{1,2},{2,3},{3,4},{4,5},{5,6},{6,7},{7,0},{8,15},{9,8},{10,9... | collective-permute-start | bytes 1966088 | tf_op jit(solution)/shard_map/ppermute | solution.py:37
  61.8 2.6 %collective-permute-start.13 = (bf16[1024,512]{1,0:T(8,128)(2,1)S(1)}, bf16[1024,512]{1,0:T(8,128)(2,1)S(1)}, u32[]{:S(2)}, u32[]{:S(2)}) collective-permute-start(bf16[1024,512]{1,0:T(8,128)(2,1)S(1)} %slice.31), channel_id=1, source_target_pairs={{0,48},{8,200},{16,0},{24,216},{32,16},{40,232},{48,32},{56,248},{... | collective-permute-start | bytes 3145736 | tf_op jit(solution)/shard_map/ppermute | solution.py:53
  64.4 4.3 %collective-permute-done.16.refs_4_ = bf16[640,512]{1,0:T(8,128)(2,1)S(1)} collective-permute-done((bf16[640,512]{1,0:T(8,128)(2,1)S(1)}, bf16[640,512]{1,0:T(8,128)(2,1)S(1)}, u32[]{:S(2)}, u32[]{:S(2)}) %collective-permute-start.16) | collective-permute-done | bytes 655392 | tf_op jit(solution)/shard_map/ppermute | solution.py:37
  68.7 4.4 %collective-permute-start.20 = (bf16[2048,512]{1,0:T(8,128)(2,1)S(1)}, bf16[2048,512]{1,0:T(8,128)(2,1)S(1)}, u32[]{:S(2)}, u32[]{:S(2)}) collective-permute-start(bf16[2048,512]{1,0:T(8,128)(2,1)S(1)} %collective-permute-done.8.refs_9_.refs_1_), channel_id=1, source_target_pairs={{0,8},{8,0},{16,24},{24,16},{32,40},{40,32},{48,56},{56,48},{64,72... | collective-permute-start | bytes 6291464 | tf_op jit(solution)/shard_map/ppermute | solution.py:42
  73.3 3.4 %collective-permute-done.11.refs_11_.refs_3_ = bf16[1024,512]{1,0:T(8,128)(2,1)S(1)} collective-permute-done((bf16[1024,512]{1,0:T(8,128)(2,1)S(1)}, bf16[1024,512]{1,0:T(8,128)(2,1)S(1)}, u32[]{:S(2)}, u32[]{:S(2)}) %collective-permute-start.11) | collective-permute-done | bytes 1048608 | tf_op jit(solution)/shard_map/ppermute | solution.py:53
  76.7 4.2 %collective-permute-start.22 = (bf16[1024,512]{1,0:T(8,128)(2,1)S(1)}, bf16[1024,512]{1,0:T(8,128)(2,1)S(1)}, u32[]{:S(2)}, u32[]{:S(2)}) collective-permute-start(bf16[1024,512]{1,0:T(8,128)(2,1)S(1)} %collective-permute-done.11.refs_11_.refs_3_), channel_id=1, source_target_pairs={{0,8},{8,0},{16,24},{24,16},{32,40},{40,32},{48,56},{56,48},{64,72... | collective-permute-start | bytes 3145736 | tf_op jit(solution)/shard_map/ppermute | solution.py:42
  81.4 4.2 %collective-permute-done.18.refs_7_ = bf16[640,512]{1,0:T(8,128)(2,1)S(1)} collective-permute-done((bf16[640,512]{1,0:T(8,128)(2,1)S(1)}, bf16[640,512]{1,0:T(8,128)(2,1)S(1)}, u32[]{:S(2)}, u32[]{:S(2)}) %collective-permute-start.18) | collective-permute-done | bytes 655392 | tf_op jit(solution)/shard_map/ppermute | solution.py:42
  90.4 14.4 %project_attend.1 = bf16[512,640]{1,0:T(8,128)(2,1)} custom-call(s32[5]{0:T(128)} %pad_add_fusion.info, f32[2,4096]{1,0:T(2,128)} %get-tuple-element.24.gains, bf16[640,512]{1,0:T(8,128)(2,1)} %get-tuple-element.25.refs_0_, bf16[640,512]{1,0:T(8,128)(2,1)} %copy-done.11, bf16[640,512]{1,0:T(8,128)(2,1)} %copy-done.12, bf16[640,512]{1,0:T(8,128)(2,1)} %copy-done.13, ...), custom_call_target="tpu_custom_call" | custom-call | flops 5000000000 | bytes 31457280 | tf_op jit(solution)/shard_map/project_attend/pallas_call | solution.py:184
  104.8 6.1 %all-to-all-start = ((bf16[32,16,640]{2,1,0:T(8,128)(2,1)}), bf16[32,16,640]{2,1,0:T(8,128)(2,1)S(1)}, u32[]{:S(2)}, u32[]{:S(2)}) async-start(bf16[32,16,640]{2,1,0:T(8,128)(2,1)} %bitcast.8), calls=%async_computation | async-start | bytes 1310720 | tf_op jit(solution)/shard_map/all_to_all | solution.py:362
  110.9 5.0 %assemble_out.1.wo = bf16[4096,512]{1,0:T(8,128)(2,1)} custom-call(s32[5]{0:T(128)} %pad_add_fusion.info, bf16[2048,512]{1,0:T(8,128)(2,1)} %copy-done.2, bf16[2048,512]{1,0:T(8,128)(2,1)} %copy-done, bf16[2048,512]{1,0:T(8,128)(2,1)} %copy-done.1, bf16[1024,512]{1,0:T(8,128)(2,1)} %copy-done.6, bf16[1024,512]{1,0:T(8,128)(2,1)} %copy-done.7, ...), custom_call_target="tpu_custom_call" | custom-call | bytes 8388608 | tf_op jit(solution)/shard_map/assemble_out/pallas_call | solution.py:220
  115.9 8.0 %all-to-all-done = bf16[32,16,640]{2,1,0:T(8,128)(2,1)S(1)} async-done(((bf16[32,16,640]{2,1,0:T(8,128)(2,1)}), bf16[32,16,640]{2,1,0:T(8,128)(2,1)S(1)}, u32[]{:S(2)}, u32[]{:S(2)}) %all-to-all-start) | async-done | bytes 655392 | tf_op jit(solution)/shard_map/all_to_all | solution.py:362
  124.7 4.9 %merge_project.1 = bf16[8,16,640]{2,1,0:T(8,128)(2,1)} custom-call(bf16[512,640]{1,0:T(8,128)(2,1)} %bitcast.9, bf16[4096,512]{1,0:T(8,128)(2,1)} %assemble_out.1.wo), custom_call_target="tpu_custom_call" | custom-call | tf_op jit(solution)/shard_map/merge_project/pallas_call | solution.py:282
  129.6 5.6 %all-to-all-start.1 = ((bf16[8,16,640]{2,1,0:T(8,128)(2,1)}), bf16[8,16,640]{2,1,0:T(8,128)(2,1)S(1)}, u32[]{:S(2)}, u32[]{:S(2)}) async-start(bf16[8,16,640]{2,1,0:T(8,128)(2,1)} %merge_project.1), calls=%async_computation.1 | async-start | bytes 327680 | tf_op jit(solution)/shard_map/all_to_all | solution.py:364
  136.5 8.9 %all-to-all-done.1.got = bf16[8,16,640]{2,1,0:T(8,128)(2,1)S(1)} async-done(((bf16[8,16,640]{2,1,0:T(8,128)(2,1)}), bf16[8,16,640]{2,1,0:T(8,128)(2,1)S(1)}, u32[]{:S(2)}, u32[]{:S(2)}) %all-to-all-start.1) | async-done | bytes 163872 | tf_op jit(solution)/shard_map/all_to_all | solution.py:364
  147.9 4.1 %all-to-all-start.2 = ((bf16[32,16,640]{2,1,0:T(8,128)(2,1)}), bf16[32,16,640]{2,1,0:T(8,128)(2,1)S(1)}, u32[]{:S(2)}, u32[]{:S(2)}) async-start(bf16[32,16,640]{2,1,0:T(8,128)(2,1)} %add_rows.1), calls=%async_computation.2 | async-start | bytes 1310720 | tf_op jit(solution)/shard_map/all_to_all | solution.py:366
  152.0 13.1 %all-to-all-done.2 = bf16[32,16,640]{2,1,0:T(8,128)(2,1)S(1)} async-done(((bf16[32,16,640]{2,1,0:T(8,128)(2,1)}), bf16[32,16,640]{2,1,0:T(8,128)(2,1)S(1)}, u32[]{:S(2)}, u32[]{:S(2)}) %all-to-all-start.2) | async-done | bytes 655392 | tf_op jit(solution)/shard_map/all_to_all | solution.py:366
  (90 shorter events, 35.1 us)
Async XLA Ops:
  4.7 9.8 %collective-permute-start.5 = (bf16[640,512]{1,0:T(8,128)(2,1)}, bf16[640,512]{1,0:T(8,128)(2,1)S(1)}, u32[]{:S(2)}, u32[]{:S(2)}) collective-permute-start(bf16[640,512]{1,0:T(8,128)(2,1)} %get-tuple-element.25.refs_0_), channel_id=1, source_target_pairs={{0,8},{8,0},{16,24},{24,16},{32,40},{40,32},{48,56},{56,48},{64,72... | collective-permute-start | bytes 1966088 | tf_op jit(solution)/shard_map/ppermute | solution.py:42
  7.9 13.7 %collective-permute-start.2 = (bf16[640,512]{1,0:T(8,128)(2,1)}, bf16[640,512]{1,0:T(8,128)(2,1)S(1)}, u32[]{:S(2)}, u32[]{:S(2)}) collective-permute-start(bf16[640,512]{1,0:T(8,128)(2,1)} %get-tuple-element.25.refs_0_), channel_id=1, source_target_pairs={{0,1},{1,2},{2,3},{3,4},{4,5},{5,6},{6,7},{7,0},{8,15},{9,8},{10,9... | collective-permute-start | bytes 1966088 | tf_op jit(solution)/shard_map/ppermute | solution.py:37
  11.7 9.8 %collective-permute-start = (bf16[512,512]{1,0:T(8,128)(2,1)}, bf16[512,512]{1,0:T(8,128)(2,1)S(1)}, u32[]{:S(2)}, u32[]{:S(2)}) collective-permute-start(bf16[512,512]{1,0:T(8,128)(2,1)} %get-tuple-element.26), channel_id=1, source_target_pairs={{0,64},{8,24},{16,80},{24,40},{32,96},{40,56},{48,112},{56,8},{64,... | collective-permute-start | bytes 1572872 | tf_op jit(solution)/shard_map/ppermute | solution.py:53
  13.0 8.5 %collective-permute-start.1 = (bf16[512,512]{1,0:T(8,128)(2,1)}, bf16[512,512]{1,0:T(8,128)(2,1)S(1)}, u32[]{:S(2)}, u32[]{:S(2)}) collective-permute-start(bf16[512,512]{1,0:T(8,128)(2,1)} %get-tuple-element.26), channel_id=1, source_target_pairs={{0,192},{8,56},{16,208},{24,8},{32,224},{40,24},{48,240},{56,40},{... | collective-permute-start | bytes 1572872 | tf_op jit(solution)/shard_map/ppermute | solution.py:53
  14.5 14.0 %collective-permute-start.6 = (bf16[640,512]{1,0:T(8,128)(2,1)S(1)}, bf16[640,512]{1,0:T(8,128)(2,1)S(1)}, u32[]{:S(2)}, u32[]{:S(2)}) collective-permute-start(bf16[640,512]{1,0:T(8,128)(2,1)S(1)} %collective-permute-done.5), channel_id=1, source_target_pairs={{0,1},{1,2},{2,3},{3,4},{4,5},{5,6},{6,7},{7,0},{8,15},{9,8},{10,9... | collective-permute-start | bytes 1966088 | tf_op jit(solution)/shard_map/ppermute | solution.py:37
  25.5 9.8 %collective-permute-start.7 = (bf16[640,512]{1,0:T(8,128)(2,1)S(1)}, bf16[640,512]{1,0:T(8,128)(2,1)S(1)}, u32[]{:S(2)}, u32[]{:S(2)}) collective-permute-start(bf16[640,512]{1,0:T(8,128)(2,1)S(1)} %collective-permute-done.2.refs_1_), channel_id=1, source_target_pairs={{0,1},{1,2},{2,3},{3,4},{4,5},{5,6},{6,7},{7,0},{8,15},{9,8},{10,9... | collective-permute-start | bytes 1966088 | tf_op jit(solution)/shard_map/ppermute | solution.py:37
  28.6 30.6 %collective-permute-start.8 = (bf16[2048,512]{1,0:T(8,128)(2,1)S(1)}, bf16[2048,512]{1,0:T(8,128)(2,1)S(1)}, u32[]{:S(2)}, u32[]{:S(2)}) collective-permute-start(bf16[2048,512]{1,0:T(8,128)(2,1)S(1)} %constant_dynamic-update-slice_fusion.refs_8_.refs_0_), channel_id=1, source_target_pairs={{0,16},{8,72},{16,32},{24,88},{32,48},{40,104},{48,0},{56,120},{64... | collective-permute-start | bytes 6291464 | tf_op jit(solution)/shard_map/ppermute | solution.py:53
  35.4 25.5 %collective-permute-start.12 = (bf16[2048,512]{1,0:T(8,128)(2,1)S(1)}, bf16[2048,512]{1,0:T(8,128)(2,1)S(1)}, u32[]{:S(2)}, u32[]{:S(2)}) collective-permute-start(bf16[2048,512]{1,0:T(8,128)(2,1)S(1)} %constant_dynamic-update-slice_fusion.refs_8_.refs_0_), channel_id=1, source_target_pairs={{0,48},{8,200},{16,0},{24,216},{32,16},{40,232},{48,32},{56,248},{... | collective-permute-start | bytes 6291464 | tf_op jit(solution)/shard_map/ppermute | solution.py:53
  37.8 9.8 %collective-permute-start.14 = (bf16[640,512]{1,0:T(8,128)(2,1)S(1)}, bf16[640,512]{1,0:T(8,128)(2,1)S(1)}, u32[]{:S(2)}, u32[]{:S(2)}) collective-permute-start(bf16[640,512]{1,0:T(8,128)(2,1)S(1)} %collective-permute-done.6), channel_id=1, source_target_pairs={{0,1},{1,2},{2,3},{3,4},{4,5},{5,6},{6,7},{7,0},{8,15},{9,8},{10,9... | collective-permute-start | bytes 1966088 | tf_op jit(solution)/shard_map/ppermute | solution.py:37
  40.1 14.6 %collective-permute-start.9 = (bf16[640,512]{1,0:T(8,128)(2,1)S(1)}, bf16[640,512]{1,0:T(8,128)(2,1)S(1)}, u32[]{:S(2)}, u32[]{:S(2)}) collective-permute-start(bf16[640,512]{1,0:T(8,128)(2,1)S(1)} %collective-permute-done.7.refs_2_), channel_id=1, source_target_pairs={{0,1},{1,2},{2,3},{3,4},{4,5},{5,6},{6,7},{7,0},{8,15},{9,8},{10,9... | collective-permute-start | bytes 1966088 | tf_op jit(solution)/shard_map/ppermute | solution.py:37
  40.2 17.6 %collective-permute-start.10 = (bf16[640,512]{1,0:T(8,128)(2,1)S(1)}, bf16[640,512]{1,0:T(8,128)(2,1)S(1)}, u32[]{:S(2)}, u32[]{:S(2)}) collective-permute-start(bf16[640,512]{1,0:T(8,128)(2,1)S(1)} %collective-permute-done.6), channel_id=1, source_target_pairs={{0,8},{8,0},{16,24},{24,16},{32,40},{40,32},{48,56},{56,48},{64,72... | collective-permute-start | bytes 1966088 | tf_op jit(solution)/shard_map/ppermute | solution.py:42
  47.7 14.2 %collective-permute-start.15 = (bf16[640,512]{1,0:T(8,128)(2,1)S(1)}, bf16[640,512]{1,0:T(8,128)(2,1)S(1)}, u32[]{:S(2)}, u32[]{:S(2)}) collective-permute-start(bf16[640,512]{1,0:T(8,128)(2,1)S(1)} %collective-permute-done.14), channel_id=1, source_target_pairs={{0,1},{1,2},{2,3},{3,4},{4,5},{5,6},{6,7},{7,0},{8,15},{9,8},{10,9... | collective-permute-start | bytes 1966088 | tf_op jit(solution)/shard_map/ppermute | solution.py:37
  54.7 14.0 %collective-permute-start.16 = (bf16[640,512]{1,0:T(8,128)(2,1)S(1)}, bf16[640,512]{1,0:T(8,128)(2,1)S(1)}, u32[]{:S(2)}, u32[]{:S(2)}) collective-permute-start(bf16[640,512]{1,0:T(8,128)(2,1)S(1)} %collective-permute-done.9.refs_3_), channel_id=1, source_target_pairs={{0,1},{1,2},{2,3},{3,4},{4,5},{5,6},{6,7},{7,0},{8,15},{9,8},{10,9... | collective-permute-start | bytes 1966088 | tf_op jit(solution)/shard_map/ppermute | solution.py:37
  57.8 10.9 %collective-permute-start.17 = (bf16[640,512]{1,0:T(8,128)(2,1)S(1)}, bf16[640,512]{1,0:T(8,128)(2,1)S(1)}, u32[]{:S(2)}, u32[]{:S(2)}) collective-permute-start(bf16[640,512]{1,0:T(8,128)(2,1)S(1)} %collective-permute-done.14), channel_id=1, source_target_pairs={{0,8},{8,0},{16,24},{24,16},{32,40},{40,32},{48,56},{56,48},{64,72... | collective-permute-start | bytes 1966088 | tf_op jit(solution)/shard_map/ppermute | solution.py:42
  59.2 21.7 %collective-permute-start.19 = (bf16[2048,512]{1,0:T(8,128)(2,1)S(1)}, bf16[2048,512]{1,0:T(8,128)(2,1)S(1)}, u32[]{:S(2)}, u32[]{:S(2)}) collective-permute-start(bf16[2048,512]{1,0:T(8,128)(2,1)S(1)} %constant_dynamic-update-slice_fusion.refs_8_.refs_0_), channel_id=1, source_target_pairs={{0,8},{8,0},{16,24},{24,16},{32,40},{40,32},{48,56},{56,48},{64,72... | collective-permute-start | bytes 6291464 | tf_op jit(solution)/shard_map/ppermute | solution.py:42
  60.8 15.9 %collective-permute-start.11 = (bf16[1024,512]{1,0:T(8,128)(2,1)S(1)}, bf16[1024,512]{1,0:T(8,128)(2,1)S(1)}, u32[]{:S(2)}, u32[]{:S(2)}) collective-permute-start(bf16[1024,512]{1,0:T(8,128)(2,1)S(1)} %slice.27), channel_id=1, source_target_pairs={{0,16},{8,72},{16,32},{24,88},{32,48},{40,104},{48,0},{56,120},{64... | collective-permute-start | bytes 3145736 | tf_op jit(solution)/shard_map/ppermute | solution.py:53
  61.8 14.9 %collective-permute-start.13 = (bf16[1024,512]{1,0:T(8,128)(2,1)S(1)}, bf16[1024,512]{1,0:T(8,128)(2,1)S(1)}, u32[]{:S(2)}, u32[]{:S(2)}) collective-permute-start(bf16[1024,512]{1,0:T(8,128)(2,1)S(1)} %slice.31), channel_id=1, source_target_pairs={{0,48},{8,200},{16,0},{24,216},{32,16},{40,232},{48,32},{56,248},{... | collective-permute-start | bytes 3145736 | tf_op jit(solution)/shard_map/ppermute | solution.py:53
  68.7 16.8 %collective-permute-start.20 = (bf16[2048,512]{1,0:T(8,128)(2,1)S(1)}, bf16[2048,512]{1,0:T(8,128)(2,1)S(1)}, u32[]{:S(2)}, u32[]{:S(2)}) collective-permute-start(bf16[2048,512]{1,0:T(8,128)(2,1)S(1)} %collective-permute-done.8.refs_9_.refs_1_), channel_id=1, source_target_pairs={{0,8},{8,0},{16,24},{24,16},{32,40},{40,32},{48,56},{56,48},{64,72... | collective-permute-start | bytes 6291464 | tf_op jit(solution)/shard_map/ppermute | solution.py:42
  73.2 12.4 %collective-permute-start.21 = (bf16[2048,512]{1,0:T(8,128)(2,1)S(1)}, bf16[2048,512]{1,0:T(8,128)(2,1)S(1)}, u32[]{:S(2)}, u32[]{:S(2)}) collective-permute-start(bf16[2048,512]{1,0:T(8,128)(2,1)S(1)} %collective-permute-done.12.refs_10_.refs_2_), channel_id=1, source_target_pairs={{0,8},{8,0},{16,24},{24,16},{32,40},{40,32},{48,56},{56,48},{64,72... | collective-permute-start | bytes 6291464 | tf_op jit(solution)/shard_map/ppermute | solution.py:42
  76.7 10.3 %collective-permute-start.22 = (bf16[1024,512]{1,0:T(8,128)(2,1)S(1)}, bf16[1024,512]{1,0:T(8,128)(2,1)S(1)}, u32[]{:S(2)}, u32[]{:S(2)}) collective-permute-start(bf16[1024,512]{1,0:T(8,128)(2,1)S(1)} %collective-permute-done.11.refs_11_.refs_3_), channel_id=1, source_target_pairs={{0,8},{8,0},{16,24},{24,16},{32,40},{40,32},{48,56},{56,48},{64,72... | collective-permute-start | bytes 3145736 | tf_op jit(solution)/shard_map/ppermute | solution.py:42
  80.9 7.5 %collective-permute-start.23 = (bf16[1024,512]{1,0:T(8,128)(2,1)S(1)}, bf16[1024,512]{1,0:T(8,128)(2,1)S(1)}, u32[]{:S(2)}, u32[]{:S(2)}) collective-permute-start(bf16[1024,512]{1,0:T(8,128)(2,1)S(1)} %collective-permute-done.13.refs_12_.refs_4_), channel_id=1, source_target_pairs={{0,8},{8,0},{16,24},{24,16},{32,40},{40,32},{48,56},{56,48},{64,72... | collective-permute-start | bytes 3145736 | tf_op jit(solution)/shard_map/ppermute | solution.py:42
  104.8 19.0 %all-to-all-start = ((bf16[32,16,640]{2,1,0:T(8,128)(2,1)}), bf16[32,16,640]{2,1,0:T(8,128)(2,1)S(1)}, u32[]{:S(2)}, u32[]{:S(2)}) async-start(bf16[32,16,640]{2,1,0:T(8,128)(2,1)} %bitcast.8), calls=%async_computation | async-start | bytes 1310720 | tf_op jit(solution)/shard_map/all_to_all | solution.py:362
  129.6 15.8 %all-to-all-start.1 = ((bf16[8,16,640]{2,1,0:T(8,128)(2,1)}), bf16[8,16,640]{2,1,0:T(8,128)(2,1)S(1)}, u32[]{:S(2)}, u32[]{:S(2)}) async-start(bf16[8,16,640]{2,1,0:T(8,128)(2,1)} %merge_project.1), calls=%async_computation.1 | async-start | bytes 327680 | tf_op jit(solution)/shard_map/all_to_all | solution.py:364
  147.9 17.1 %all-to-all-start.2 = ((bf16[32,16,640]{2,1,0:T(8,128)(2,1)}), bf16[32,16,640]{2,1,0:T(8,128)(2,1)S(1)}, u32[]{:S(2)}, u32[]{:S(2)}) async-start(bf16[32,16,640]{2,1,0:T(8,128)(2,1)} %add_rows.1), calls=%async_computation.2 | async-start | bytes 1310720 | tf_op jit(solution)/shard_map/all_to_all | solution.py:366
  (22 other events, 332.4 us)

commit v4 on v2

--- a/solution.py
+++ b/solution.py
@@ -198,15 +198,33 @@
     )(info, gains, *x_parts, *w_parts)
 
 
-def merge_kernel(info, got, *refs):
+def assemble_kernel(info, *refs):
     w_parts = refs[:10]
-    out, wo, sem = refs[10:]
+    wo, sem = refs[10:]
     for ref, row, s in shard_places(w_parts, info[0]):
         pltpu.make_async_copy(
             ref.at[pl.ds(row * 512 + 384, 128)],
             wo.at[pl.ds(pl.multiple_of(s * 128, 128), 128)],
             sem,
         ).start()
+    pltpu.make_async_copy(wo, wo, sem).wait()
+
+
+def assemble(info, w_parts):
+    anywhere = pl.BlockSpec(memory_space=pl.ANY)
+    return pl.pallas_call(
+        assemble_kernel,
+        in_specs=[pl.BlockSpec(memory_space=pltpu.SMEM)] + [anywhere] * 10,
+        out_specs=pl.BlockSpec(memory_space=pltpu.VMEM),
+        out_shape=jax.ShapeDtypeStruct((4096, 512), BF16),
+        scratch_shapes=[pltpu.SemaphoreType.DMA(())],
+        compiler_params=pltpu.CompilerParams(vmem_limit_bytes=40 * 2**20),
+        cost_estimate=pl.CostEstimate(flops=0, bytes_accessed=8 * 2**20, transcendentals=0),
+        name="assemble_out",
+    )(info, *w_parts)
+
+
+def merge_kernel(got, wo, out):
     st = got[:, 512:640].astype(F32)
     both = st + pltpu.roll(st, 120, 1)
     sum_a = pltpu.roll(both, 112, 1).reshape(32, 16, 128)
@@ -244,7 +262,6 @@
     pool_hi, pool_lo = high_low(pooled)
     row = lax.broadcasted_iota(jnp.int32, (16, 128), 0)
     extra = jnp.where(row == 0, pool_hi, jnp.where(row == 1, pool_lo, 0.0)).astype(BF16)
-    pltpu.make_async_copy(wo, wo, sem).wait()
     for z in range(8):
         term = lax.dot_general(
             context,
@@ -256,18 +273,13 @@
         out[z, :, 512:640] = extra
 
 
-def merge(info, got, w_parts):
-    anywhere = pl.BlockSpec(memory_space=pl.ANY)
-    inside = pl.BlockSpec(memory_space=pltpu.VMEM)
+def merge(got, wo):
     return pl.pallas_call(
         merge_kernel,
-        in_specs=[pl.BlockSpec(memory_space=pltpu.SMEM), inside] + [anywhere] * 10,
-        out_specs=inside,
         out_shape=jax.ShapeDtypeStruct((8, 16, 640), BF16),
-        scratch_shapes=[pltpu.VMEM((4096, 512), BF16), pltpu.SemaphoreType.DMA(())],
         compiler_params=pltpu.CompilerParams(vmem_limit_bytes=40 * 2**20),
         name="merge_project",
-    )(info, got, *w_parts)
+    )(got, wo)
 
 
 def add_kernel(got, rows, out):
@@ -289,24 +301,50 @@
     )(got, rows)
 
 
+def pack_kernel(
+    info, encoded, states, w_key, w_value, w_query, w_out, tokens, shard
+):
+    tokens[0:512, :] = encoded[...]
+    tokens[512:640, :] = states[pl.ds(pl.multiple_of(info[2] * QTOK, QTOK), 2 * QTOK), :]
+    shard[0:128, :] = w_key[...]
+    shard[128:256, :] = w_value[...]
+    shard[256:384, :] = w_query[...]
+    shard[384:512, :] = w_out[...].T
+
+
+def pack(info, *arrays):
+    inside = pl.BlockSpec(memory_space=pltpu.VMEM)
+    return pl.pallas_call(
+        pack_kernel,
+        in_specs=[pl.BlockSpec(memory_space=pltpu.SMEM)] + [inside] * 6,
+        out_specs=[inside] * 2,
+        out_shape=[
+            jax.ShapeDtypeStruct((640, 512), BF16),
+            jax.ShapeDtypeStruct((512, 512), BF16),
+        ],
+        name="pack",
+    )(info, *arrays)
+
+
 def on_device(
     encoded, decoder_states, passage_counts, enc_gain, dec_gain, w_key, w_value, w_query, w_out
 ):
     sec = lax.axis_index("sec")
     tp = lax.axis_index("tp")
     questions = decoder_states.shape[0] // QTOK
-    ends = jnp.cumsum(passage_counts)
+    order = jnp.arange(questions, dtype=jnp.int32)
+    ends = jnp.sum(jnp.where(order[:, None] <= order[None, :], passage_counts[:, None], 0), axis=0)
     slots = sec * 2 + jnp.arange(2, dtype=jnp.int32)
     owner = jnp.sum((slots[:, None] >= ends[None, :]).astype(jnp.int32), axis=1)
     first = jnp.minimum(owner[0], questions - 2)
     info = jnp.stack([sec, tp, first, owner[0], owner[1]]).astype(jnp.int32)
-    window = lax.dynamic_slice_in_dim(decoder_states, first * QTOK, 2 * QTOK, 0)
-    x_parts = ring_gather(jnp.concatenate([encoded, window], 0))
-    w_parts = plane_gather(jnp.concatenate([w_key, w_value, w_query, w_out.T], 0))
+    tokens, shard = pack(info, encoded, decoder_states, w_key, w_value, w_query, w_out)
+    x_parts = ring_gather(tokens)
+    w_parts = plane_gather(shard)
     gains = jnp.stack([enc_gain, dec_gain])
     partial = attend(info, gains, x_parts, w_parts)
     got = lax.all_to_all(partial, "sec", 0, 0, tiled=True)
-    terms = merge(info, got, w_parts)
+    terms = merge(got, assemble(info, w_parts))
     terms = lax.all_to_all(terms, "tp", 0, 0, tiled=True)
     rows = lax.dynamic_slice_in_dim(decoder_states, sec * 16, 16, 0)
     finished = lax.all_to_all(add_rows(terms, rows), "sec", 0, 0, tiled=True)

time: 166 us -> 173 us (1.042)
  blocking collectives: 21.5 us -> 0 us
  starting transfers between devices: 44.5 us -> 56.9 us
  Pallas kernels: 20.7 us -> 28 us
  waiting for transfers between devices: 57.2 us -> 64.3 us
  local copies, waits for them, and re-layouts: 15.4 us -> 19.8 us
  other arithmetic: 5.08 us -> 2.29 us
    all_to_all x1 -> x0, blocking collectives: 21.5 us -> none  [on_device(): got = lax.all_to_all(partial, 'sec', 0, 0, tiled=True)]
    all_to_all x0 -> x1, starting transfers between devices: none -> 7.84 us  [on_device(): got = lax.all_to_all(partial, 'sec', 0, 0, tiled=True)]
    pallas_call x1 -> x3, Pallas kernels: 5.36 us -> 12.5 us  [the longest x1 6.5 us: assemble(): pl.pallas_call(assemble_kernel, in_specs=[pl.BlockSpec(memory_space=pltpu...]
    ppermute x8, starting transfers between devices: 15.6 us -> 20.4 us  [in_plane(): return lax.ppermute(v, 'sec', pairs)]
    ppermute x6, waiting for transfers between devices: 21.1 us -> 25.5 us  [along_tp(): return lax.ppermute(v, 'tp', [(i, (i + step) % n) for i in range(n)])]
    unnamed x34 -> x54, local copies, waits for them, and re-layouts: 11.8 us -> 15.5 us
    ppermute x8, waiting for transfers between devices: 9.92 us -> 13.2 us  [in_plane(): return lax.ppermute(v, 'sec', pairs)]
    all_to_all x1, starting transfers between devices: 4.07 us -> 6.31 us  [on_device(): finished = lax.all_to_all(add_rows(terms, rows), 'sec', 0, 0, tiled=True)]
  transfers between devices with their start and end apart: 22 -> 23, of which waited for: 11 -> 11; matrix products, arithmetic and copies ran while one was open for 7% -> 5% of each run, Pallas kernels for 0% -> 4%
where the time goes in v4:
time: 173 us; the launch traced here: 172 us
  waiting for transfers between devices  64.3 us (37%)
  starting transfers between devices  56.9 us (33%)
  Pallas kernels  28 us (16%)
  local copies, waits for them, and re-layouts  19.8 us (11%)
  other arithmetic  2.29 us (1%)
    ppermute x6, waiting for transfers between devices, along_tp(): return lax.ppermute(v, 'tp', [(i, (i + step) % n) for i in range(n)])  25.5 us
    ppermute x8, starting transfers between devices, in_plane(): return lax.ppermute(v, 'sec', pairs)  20.4 us
    unnamed x54, local copies, waits for them, and re-layouts  15.5 us
    pallas_call x1, Pallas kernels, attend(): pl.pallas_call(attend_kernel, in_specs=[pl.BlockSpec(memory_space=pltpu.S...  13.7 us
    ppermute x8, waiting for transfers between devices, in_plane(): return lax.ppermute(v, 'sec', pairs)  13.2 us
    all_to_all x1, waiting for transfers between devices, on_device(): finished = lax.all_to_all(add_rows(terms, rows), 'sec', 0, 0, tiled=True)  12.9 us
    ppermute x6, starting transfers between devices, along_tp(): return lax.ppermute(v, 'tp', [(i, (i + step) % n) for i in range(n)])  10.9 us
    all_to_all x1, waiting for transfers between devices, on_device(): terms = lax.all_to_all(terms, 'tp', 0, 0, tiled=True)  8.91 us
  transfers between devices with their start and end apart: 23, of which 11 were waited for; matrix products, arithmetic and copies ran while one was open for 5% of the time, Pallas kernels for 4%

profile of v4, /device:TPU:1, one launch (start us, length us, event | category | flops | bytes accessed | tf_op | source)
XLA Modules:
  0.0 172.3 jit_solution(10198622828669632849)
XLA Ops:
  2.2 2.4 %pack.1 = (bf16[640,512]{1,0:T(8,128)(2,1)}, bf16[512,512]{1,0:T(8,128)(2,1)}) custom-call(s32[5]{0:T(128)} %pad_add_fusion.info, bf16[512,512]{1,0:T(8,128)(2,1)} %encoded.1, bf16[512,512]{1,0:T(8,128)(2,1)} %states.1, bf16[128,512]{1,0:T(8,128)(2,1)} %w_key.1, bf16[128,512]{1,0:T(8,128)(2,1)} %w_value.1, bf16[128,512]{1,0:T(8,128)(2,1)} %w_query.1, ...), custom_call_target="tpu_custom_call" | custom-call | tf_op jit(solution)/shard_map/pack/pallas_call | solution.py:317
  9.8 3.9 %collective-permute-start.1 = (bf16[640,512]{1,0:T(8,128)(2,1)}, bf16[640,512]{1,0:T(8,128)(2,1)S(1)}, u32[]{:S(2)}, u32[]{:S(2)}) collective-permute-start(bf16[640,512]{1,0:T(8,128)(2,1)} %get-tuple-element.4.refs_0_), channel_id=1, source_target_pairs={{0,7},{1,0},{2,1},{3,2},{4,3},{5,4},{6,5},{7,6},{8,15},{9,8},{10,9... | collective-permute-start | bytes 1966088 | tf_op jit(solution)/shard_map/ppermute | solution.py:26
  17.3 2.7 %collective-permute-start.10 = (bf16[256,512]{1,0:T(8,128)(2,1)S(1)}, bf16[256,512]{1,0:T(8,128)(2,1)S(1)}, u32[]{:S(2)}, u32[]{:S(2)}) collective-permute-start(bf16[256,512]{1,0:T(8,128)(2,1)S(1)} %slice.32), channel_id=1, source_target_pairs={{0,192},{8,56},{16,208},{24,8},{32,224},{40,24},{48,240},{56,40},{... | collective-permute-start | bytes 786440 | tf_op jit(solution)/shard_map/ppermute | solution.py:53
  21.7 6.2 %collective-permute-done.refs_1_ = bf16[640,512]{1,0:T(8,128)(2,1)S(1)} collective-permute-done((bf16[640,512]{1,0:T(8,128)(2,1)}, bf16[640,512]{1,0:T(8,128)(2,1)S(1)}, u32[]{:S(2)}, u32[]{:S(2)}) %collective-permute-start) | collective-permute-done | bytes 655392 | tf_op jit(solution)/shard_map/ppermute | solution.py:26
  27.9 2.7 %collective-permute-start.3 = (bf16[640,512]{1,0:T(8,128)(2,1)S(1)}, bf16[640,512]{1,0:T(8,128)(2,1)}, u32[]{:S(2)}, u32[]{:S(2)}) collective-permute-start(bf16[640,512]{1,0:T(8,128)(2,1)S(1)} %collective-permute-done.1.refs_2_), channel_id=1, source_target_pairs={{0,7},{1,0},{2,1},{3,2},{4,3},{5,4},{6,5},{7,6},{8,15},{9,8},{10,9... | collective-permute-start | bytes 1966088 | tf_op jit(solution)/shard_map/ppermute | solution.py:26
  32.9 2.5 %collective-permute-start.11 = (bf16[2048,512]{1,0:T(8,128)(2,1)}, bf16[2048,512]{1,0:T(8,128)(2,1)S(1)}, u32[]{:S(2)}, u32[]{:S(2)}) collective-permute-start(bf16[2048,512]{1,0:T(8,128)(2,1)} %constant_dynamic-update-slice_fusion.refs_8_.refs_0_), channel_id=1, source_target_pairs={{0,16},{8,72},{16,32},{24,88},{32,48},{40,104},{48,0},{56,120},{64... | collective-permute-start | bytes 6291464 | tf_op jit(solution)/shard_map/ppermute | solution.py:53
  36.6 7.0 %collective-permute-done.2.refs_3_ = bf16[640,512]{1,0:T(8,128)(2,1)} collective-permute-done((bf16[640,512]{1,0:T(8,128)(2,1)S(1)}, bf16[640,512]{1,0:T(8,128)(2,1)}, u32[]{:S(2)}, u32[]{:S(2)}) %collective-permute-start.2) | collective-permute-done | bytes 655392 | tf_op jit(solution)/shard_map/ppermute | solution.py:26
  43.6 2.7 %collective-permute-start.5 = (bf16[640,512]{1,0:T(8,128)(2,1)}, bf16[640,512]{1,0:T(8,128)(2,1)S(1)}, u32[]{:S(2)}, u32[]{:S(2)}) collective-permute-start(bf16[640,512]{1,0:T(8,128)(2,1)} %collective-permute-done.3.refs_4_), channel_id=1, source_target_pairs={{0,7},{1,0},{2,1},{3,2},{4,3},{5,4},{6,5},{7,6},{8,15},{9,8},{10,9... | collective-permute-start | bytes 1966088 | tf_op jit(solution)/shard_map/ppermute | solution.py:26
  46.3 12.2 %collective-permute-done.4.refs_5_ = bf16[640,512]{1,0:T(8,128)(2,1)S(1)} collective-permute-done((bf16[640,512]{1,0:T(8,128)(2,1)}, bf16[640,512]{1,0:T(8,128)(2,1)S(1)}, u32[]{:S(2)}, u32[]{:S(2)}) %collective-permute-start.4) | collective-permute-done | bytes 655392 | tf_op jit(solution)/shard_map/ppermute | solution.py:26
  58.7 2.5 %collective-permute-start.6 = (bf16[640,512]{1,0:T(8,128)(2,1)S(1)}, bf16[640,512]{1,0:T(8,128)(2,1)S(1)}, u32[]{:S(2)}, u32[]{:S(2)}) collective-permute-start(bf16[640,512]{1,0:T(8,128)(2,1)S(1)} %broadcast_select_fusion), channel_id=1, source_target_pairs={{0,1},{1,2},{2,3},{3,4},{4,5},{5,6},{6,7},{7,0},{8,15},{9,8},{10,9... | collective-permute-start | bytes 1966088 | tf_op jit(solution)/shard_map/ppermute | solution.py:37
  62.6 3.9 %collective-permute-start.13 = (bf16[1024,512]{1,0:T(8,128)(2,1)S(1)}, bf16[1024,512]{1,0:T(8,128)(2,1)S(1)}, u32[]{:S(2)}, u32[]{:S(2)}) collective-permute-start(bf16[1024,512]{1,0:T(8,128)(2,1)S(1)} %slice.33), channel_id=1, source_target_pairs={{0,16},{8,72},{16,32},{24,88},{32,48},{40,104},{48,0},{56,120},{64... | collective-permute-start | bytes 3145736 | tf_op jit(solution)/shard_map/ppermute | solution.py:53
  68.7 6.4 %collective-permute-start.14 = (bf16[1024,512]{1,0:T(8,128)(2,1)S(1)}, bf16[1024,512]{1,0:T(8,128)(2,1)S(1)}, u32[]{:S(2)}, u32[]{:S(2)}) collective-permute-start(bf16[1024,512]{1,0:T(8,128)(2,1)S(1)} %slice.34), channel_id=1, source_target_pairs={{0,48},{8,200},{16,0},{24,216},{32,16},{40,232},{48,32},{56,248},{... | collective-permute-start | bytes 3145736 | tf_op jit(solution)/shard_map/ppermute | solution.py:53
  75.1 4.9 %collective-permute-done.13.refs_11_.refs_3_ = bf16[1024,512]{1,0:T(8,128)(2,1)S(1)} collective-permute-done((bf16[1024,512]{1,0:T(8,128)(2,1)S(1)}, bf16[1024,512]{1,0:T(8,128)(2,1)S(1)}, u32[]{:S(2)}, u32[]{:S(2)}) %collective-permute-start.13) | collective-permute-done | bytes 1048608 | tf_op jit(solution)/shard_map/ppermute | solution.py:53
  79.9 6.9 %collective-permute-done.14.refs_12_.refs_4_ = bf16[1024,512]{1,0:T(8,128)(2,1)S(1)} collective-permute-done((bf16[1024,512]{1,0:T(8,128)(2,1)S(1)}, bf16[1024,512]{1,0:T(8,128)(2,1)S(1)}, u32[]{:S(2)}, u32[]{:S(2)}) %collective-permute-start.14) | collective-permute-done | bytes 1048608 | tf_op jit(solution)/shard_map/ppermute | solution.py:53
  86.8 2.2 %collective-permute-start.19 = (bf16[1024,512]{1,0:T(8,128)(2,1)S(1)}, bf16[1024,512]{1,0:T(8,128)(2,1)S(1)}, u32[]{:S(2)}, u32[]{:S(2)}) collective-permute-start(bf16[1024,512]{1,0:T(8,128)(2,1)S(1)} %collective-permute-done.14.refs_12_.refs_4_), channel_id=1, source_target_pairs={{0,8},{8,0},{16,24},{24,16},{32,40},{40,32},{48,56},{56,48},{64,72... | collective-permute-start | bytes 3145736 | tf_op jit(solution)/shard_map/ppermute | solution.py:42
  91.8 13.7 %project_attend.1 = bf16[512,640]{1,0:T(8,128)(2,1)S(1)} custom-call(s32[5]{0:T(128)S(1)} %copy-done.19, f32[2,4096]{1,0:T(2,128)S(1)} %pad_maximum_fusion.gains, bf16[640,512]{1,0:T(8,128)(2,1)S(1)} %copy-done.14, bf16[640,512]{1,0:T(8,128)(2,1)S(1)} %copy-done.16, bf16[640,512]{1,0:T(8,128)(2,1)S(1)} %copy-done.18, ...), custom_call_target="tpu_custom_call" | custom-call | flops 5000000000 | bytes 31457280 | tf_op jit(solution)/shard_map/project_attend/pallas_call | solution.py:179
  107.3 7.8 %all-to-all-start = ((bf16[32,16,640]{2,1,0:T(8,128)(2,1)}), bf16[32,16,640]{2,1,0:T(8,128)(2,1)}, u32[]{:S(2)}, u32[]{:S(2)}) async-start(bf16[32,16,640]{2,1,0:T(8,128)(2,1)} %bitcast.8), calls=%async_computation | async-start | bytes 1310720 | tf_op jit(solution)/shard_map/all_to_all | solution.py:346
  120.4 6.5 %assemble_out.1.wo = bf16[4096,512]{1,0:T(8,128)(2,1)} custom-call(s32[5]{0:T(128)S(1)} %copy-done.19, bf16[2048,512]{1,0:T(8,128)(2,1)} %constant_dynamic-update-slice_fusion.refs_8_.refs_0_, bf16[2048,512]{1,0:T(8,128)(2,1)S(1)} %collective-permute-done.11.refs_9_.refs_1_, bf16[2048,512]{1,0:T(8,128)(2,1)} %collective-permute-done.12.refs_10_.refs_2_, ...), custom_call_target="tpu_custom_call" | custom-call | bytes 8388608 | tf_op jit(solution)/shard_map/assemble_out/pallas_call | solution.py:215
  128.2 2.2 %copy-done = bf16[4096,512]{1,0:T(8,128)(2,1)S(1)} copy-done((bf16[4096,512]{1,0:T(8,128)(2,1)S(1)}, bf16[4096,512]{1,0:T(8,128)(2,1)}, u32[]{:S(2)}) %copy-start) | copy-done | bytes 4194328
  130.4 3.6 %merge_project.1 = bf16[8,16,640]{2,1,0:T(8,128)(2,1)} custom-call(bf16[512,640]{1,0:T(8,128)(2,1)} %bitcast.5.got, bf16[4096,512]{1,0:T(8,128)(2,1)S(1)} %copy-done), custom_call_target="tpu_custom_call" | custom-call | tf_op jit(solution)/shard_map/merge_project/pallas_call | solution.py:277
  134.0 4.9 %all-to-all-start.1 = ((bf16[8,16,640]{2,1,0:T(8,128)(2,1)}), bf16[8,16,640]{2,1,0:T(8,128)(2,1)S(1)}, u32[]{:S(2)}, u32[]{:S(2)}) async-start(bf16[8,16,640]{2,1,0:T(8,128)(2,1)} %merge_project.1), calls=%async_computation.1 | async-start | bytes 327680 | tf_op jit(solution)/shard_map/all_to_all | solution.py:348
  140.1 8.9 %all-to-all-done.1.got = bf16[8,16,640]{2,1,0:T(8,128)(2,1)S(1)} async-done(((bf16[8,16,640]{2,1,0:T(8,128)(2,1)}), bf16[8,16,640]{2,1,0:T(8,128)(2,1)S(1)}, u32[]{:S(2)}, u32[]{:S(2)}) %all-to-all-start.1) | async-done | bytes 163872 | tf_op jit(solution)/shard_map/all_to_all | solution.py:348
  151.5 6.3 %all-to-all-start.2 = ((bf16[32,16,640]{2,1,0:T(8,128)(2,1)}), bf16[32,16,640]{2,1,0:T(8,128)(2,1)S(1)}, u32[]{:S(2)}, u32[]{:S(2)}) async-start(bf16[32,16,640]{2,1,0:T(8,128)(2,1)} %add_rows.1), calls=%async_computation.2 | async-start | bytes 1310720 | tf_op jit(solution)/shard_map/all_to_all | solution.py:350
  157.8 12.9 %all-to-all-done.2 = bf16[32,16,640]{2,1,0:T(8,128)(2,1)S(1)} async-done(((bf16[32,16,640]{2,1,0:T(8,128)(2,1)}), bf16[32,16,640]{2,1,0:T(8,128)(2,1)S(1)}, u32[]{:S(2)}, u32[]{:S(2)}) %all-to-all-start.2) | async-done | bytes 655392 | tf_op jit(solution)/shard_map/all_to_all | solution.py:350
  (96 shorter events, 35.5 us)
Async XLA Ops:
  4.6 10.6 %collective-permute-start.7 = (bf16[512,512]{1,0:T(8,128)(2,1)}, bf16[512,512]{1,0:T(8,128)(2,1)S(1)}, u32[]{:S(2)}, u32[]{:S(2)}) collective-permute-start(bf16[512,512]{1,0:T(8,128)(2,1)} %get-tuple-element.5), channel_id=1, source_target_pairs={{0,64},{8,24},{16,80},{24,40},{32,96},{40,56},{48,112},{56,8},{64,... | collective-permute-start | bytes 1572872 | tf_op jit(solution)/shard_map/ppermute | solution.py:53
  6.8 10.5 %collective-permute-start.8 = (bf16[512,512]{1,0:T(8,128)(2,1)}, bf16[512,512]{1,0:T(8,128)(2,1)S(1)}, u32[]{:S(2)}, u32[]{:S(2)}) collective-permute-start(bf16[512,512]{1,0:T(8,128)(2,1)} %get-tuple-element.5), channel_id=1, source_target_pairs={{0,192},{8,56},{16,208},{24,8},{32,224},{40,24},{48,240},{56,40},{... | collective-permute-start | bytes 1572872 | tf_op jit(solution)/shard_map/ppermute | solution.py:53
  8.2 19.7 %collective-permute-start = (bf16[640,512]{1,0:T(8,128)(2,1)}, bf16[640,512]{1,0:T(8,128)(2,1)S(1)}, u32[]{:S(2)}, u32[]{:S(2)}) collective-permute-start(bf16[640,512]{1,0:T(8,128)(2,1)} %get-tuple-element.4.refs_0_), channel_id=1, source_target_pairs={{0,1},{1,2},{2,3},{3,4},{4,5},{5,6},{6,7},{7,0},{8,9},{9,10},{10,1... | collective-permute-start | bytes 1966088 | tf_op jit(solution)/shard_map/ppermute | solution.py:26
  9.8 18.0 %collective-permute-start.1 = (bf16[640,512]{1,0:T(8,128)(2,1)}, bf16[640,512]{1,0:T(8,128)(2,1)S(1)}, u32[]{:S(2)}, u32[]{:S(2)}) collective-permute-start(bf16[640,512]{1,0:T(8,128)(2,1)} %get-tuple-element.4.refs_0_), channel_id=1, source_target_pairs={{0,7},{1,0},{2,1},{3,2},{4,3},{5,4},{6,5},{7,6},{8,15},{9,8},{10,9... | collective-permute-start | bytes 1966088 | tf_op jit(solution)/shard_map/ppermute | solution.py:26
  15.3 16.1 %collective-permute-start.9 = (bf16[256,512]{1,0:T(8,128)(2,1)S(1)}, bf16[256,512]{1,0:T(8,128)(2,1)S(1)}, u32[]{:S(2)}, u32[]{:S(2)}) collective-permute-start(bf16[256,512]{1,0:T(8,128)(2,1)S(1)} %slice.31), channel_id=1, source_target_pairs={{0,64},{8,24},{16,80},{24,40},{32,96},{40,56},{48,112},{56,8},{64,... | collective-permute-start | bytes 786440 | tf_op jit(solution)/shard_map/ppermute | solution.py:53
  17.3 14.9 %collective-permute-start.10 = (bf16[256,512]{1,0:T(8,128)(2,1)S(1)}, bf16[256,512]{1,0:T(8,128)(2,1)S(1)}, u32[]{:S(2)}, u32[]{:S(2)}) collective-permute-start(bf16[256,512]{1,0:T(8,128)(2,1)S(1)} %slice.32), channel_id=1, source_target_pairs={{0,192},{8,56},{16,208},{24,8},{32,224},{40,24},{48,240},{56,40},{... | collective-permute-start | bytes 786440 | tf_op jit(solution)/shard_map/ppermute | solution.py:53
  27.9 15.7 %collective-permute-start.2 = (bf16[640,512]{1,0:T(8,128)(2,1)S(1)}, bf16[640,512]{1,0:T(8,128)(2,1)}, u32[]{:S(2)}, u32[]{:S(2)}) collective-permute-start(bf16[640,512]{1,0:T(8,128)(2,1)S(1)} %collective-permute-done.refs_1_), channel_id=1, source_target_pairs={{0,1},{1,2},{2,3},{3,4},{4,5},{5,6},{6,7},{7,0},{8,9},{9,10},{10,1... | collective-permute-start | bytes 1966088 | tf_op jit(solution)/shard_map/ppermute | solution.py:26
  27.9 15.7 %collective-permute-start.3 = (bf16[640,512]{1,0:T(8,128)(2,1)S(1)}, bf16[640,512]{1,0:T(8,128)(2,1)}, u32[]{:S(2)}, u32[]{:S(2)}) collective-permute-start(bf16[640,512]{1,0:T(8,128)(2,1)S(1)} %collective-permute-done.1.refs_2_), channel_id=1, source_target_pairs={{0,7},{1,0},{2,1},{3,2},{4,3},{5,4},{6,5},{7,6},{8,15},{9,8},{10,9... | collective-permute-start | bytes 1966088 | tf_op jit(solution)/shard_map/ppermute | solution.py:26
  32.9 29.6 %collective-permute-start.11 = (bf16[2048,512]{1,0:T(8,128)(2,1)}, bf16[2048,512]{1,0:T(8,128)(2,1)S(1)}, u32[]{:S(2)}, u32[]{:S(2)}) collective-permute-start(bf16[2048,512]{1,0:T(8,128)(2,1)} %constant_dynamic-update-slice_fusion.refs_8_.refs_0_), channel_id=1, source_target_pairs={{0,16},{8,72},{16,32},{24,88},{32,48},{40,104},{48,0},{56,120},{64... | collective-permute-start | bytes 6291464 | tf_op jit(solution)/shard_map/ppermute | solution.py:53
  35.3 31.2 %collective-permute-start.12 = (bf16[2048,512]{1,0:T(8,128)(2,1)}, bf16[2048,512]{1,0:T(8,128)(2,1)}, u32[]{:S(2)}, u32[]{:S(2)}) collective-permute-start(bf16[2048,512]{1,0:T(8,128)(2,1)} %constant_dynamic-update-slice_fusion.refs_8_.refs_0_), channel_id=1, source_target_pairs={{0,48},{8,200},{16,0},{24,216},{32,16},{40,232},{48,32},{56,248},{... | collective-permute-start | bytes 6291464 | tf_op jit(solution)/shard_map/ppermute | solution.py:53
  43.6 14.9 %collective-permute-start.4 = (bf16[640,512]{1,0:T(8,128)(2,1)}, bf16[640,512]{1,0:T(8,128)(2,1)S(1)}, u32[]{:S(2)}, u32[]{:S(2)}) collective-permute-start(bf16[640,512]{1,0:T(8,128)(2,1)} %collective-permute-done.2.refs_3_), channel_id=1, source_target_pairs={{0,1},{1,2},{2,3},{3,4},{4,5},{5,6},{6,7},{7,0},{8,9},{9,10},{10,1... | collective-permute-start | bytes 1966088 | tf_op jit(solution)/shard_map/ppermute | solution.py:26
  43.6 14.9 %collective-permute-start.5 = (bf16[640,512]{1,0:T(8,128)(2,1)}, bf16[640,512]{1,0:T(8,128)(2,1)S(1)}, u32[]{:S(2)}, u32[]{:S(2)}) collective-permute-start(bf16[640,512]{1,0:T(8,128)(2,1)} %collective-permute-done.3.refs_4_), channel_id=1, source_target_pairs={{0,7},{1,0},{2,1},{3,2},{4,3},{5,4},{6,5},{7,6},{8,15},{9,8},{10,9... | collective-permute-start | bytes 1966088 | tf_op jit(solution)/shard_map/ppermute | solution.py:26
  58.7 33.1 %copy-start.14 = (bf16[640,512]{1,0:T(8,128)(2,1)S(1)}, bf16[640,512]{1,0:T(8,128)(2,1)}, u32[]{:S(2)}) copy-start(bf16[640,512]{1,0:T(8,128)(2,1)} %get-tuple-element.4.refs_0_) | copy-start | bytes 1966084
  58.7 10.0 %collective-permute-start.6 = (bf16[640,512]{1,0:T(8,128)(2,1)S(1)}, bf16[640,512]{1,0:T(8,128)(2,1)S(1)}, u32[]{:S(2)}, u32[]{:S(2)}) collective-permute-start(bf16[640,512]{1,0:T(8,128)(2,1)S(1)} %broadcast_select_fusion), channel_id=1, source_target_pairs={{0,1},{1,2},{2,3},{3,4},{4,5},{5,6},{6,7},{7,0},{8,15},{9,8},{10,9... | collective-permute-start | bytes 1966088 | tf_op jit(solution)/shard_map/ppermute | solution.py:37
  61.2 27.9 %collective-permute-start.15 = (bf16[2048,512]{1,0:T(8,128)(2,1)}, bf16[2048,512]{1,0:T(8,128)(2,1)S(1)}, u32[]{:S(2)}, u32[]{:S(2)}) collective-permute-start(bf16[2048,512]{1,0:T(8,128)(2,1)} %constant_dynamic-update-slice_fusion.refs_8_.refs_0_), channel_id=1, source_target_pairs={{0,8},{8,0},{16,24},{24,16},{32,40},{40,32},{48,56},{56,48},{64,72... | collective-permute-start | bytes 6291464 | tf_op jit(solution)/shard_map/ppermute | solution.py:42
  62.6 17.3 %collective-permute-start.13 = (bf16[1024,512]{1,0:T(8,128)(2,1)S(1)}, bf16[1024,512]{1,0:T(8,128)(2,1)S(1)}, u32[]{:S(2)}, u32[]{:S(2)}) collective-permute-start(bf16[1024,512]{1,0:T(8,128)(2,1)S(1)} %slice.33), channel_id=1, source_target_pairs={{0,16},{8,72},{16,32},{24,88},{32,48},{40,104},{48,0},{56,120},{64... | collective-permute-start | bytes 3145736 | tf_op jit(solution)/shard_map/ppermute | solution.py:53
  66.5 22.6 %collective-permute-start.16 = (bf16[2048,512]{1,0:T(8,128)(2,1)S(1)}, bf16[2048,512]{1,0:T(8,128)(2,1)S(1)}, u32[]{:S(2)}, u32[]{:S(2)}) collective-permute-start(bf16[2048,512]{1,0:T(8,128)(2,1)S(1)} %collective-permute-done.11.refs_9_.refs_1_), channel_id=1, source_target_pairs={{0,8},{8,0},{16,24},{24,16},{32,40},{40,32},{48,56},{56,48},{64,72... | collective-permute-start | bytes 6291464 | tf_op jit(solution)/shard_map/ppermute | solution.py:42
  67.8 21.3 %collective-permute-start.17 = (bf16[2048,512]{1,0:T(8,128)(2,1)}, bf16[2048,512]{1,0:T(8,128)(2,1)S(1)}, u32[]{:S(2)}, u32[]{:S(2)}) collective-permute-start(bf16[2048,512]{1,0:T(8,128)(2,1)} %collective-permute-done.12.refs_10_.refs_2_), channel_id=1, source_target_pairs={{0,8},{8,0},{16,24},{24,16},{32,40},{40,32},{48,56},{56,48},{64,72... | collective-permute-start | bytes 6291464 | tf_op jit(solution)/shard_map/ppermute | solution.py:42
  68.7 18.1 %collective-permute-start.14 = (bf16[1024,512]{1,0:T(8,128)(2,1)S(1)}, bf16[1024,512]{1,0:T(8,128)(2,1)S(1)}, u32[]{:S(2)}, u32[]{:S(2)}) collective-permute-start(bf16[1024,512]{1,0:T(8,128)(2,1)S(1)} %slice.34), channel_id=1, source_target_pairs={{0,48},{8,200},{16,0},{24,216},{32,16},{40,232},{48,32},{56,248},{... | collective-permute-start | bytes 3145736 | tf_op jit(solution)/shard_map/ppermute | solution.py:53
  79.9 9.2 %collective-permute-start.18 = (bf16[1024,512]{1,0:T(8,128)(2,1)S(1)}, bf16[1024,512]{1,0:T(8,128)(2,1)S(1)}, u32[]{:S(2)}, u32[]{:S(2)}) collective-permute-start(bf16[1024,512]{1,0:T(8,128)(2,1)S(1)} %collective-permute-done.13.refs_11_.refs_3_), channel_id=1, source_target_pairs={{0,8},{8,0},{16,24},{24,16},{32,40},{40,32},{48,56},{56,48},{64,72... | collective-permute-start | bytes 3145736 | tf_op jit(solution)/shard_map/ppermute | solution.py:42
  86.8 4.5 %collective-permute-start.19 = (bf16[1024,512]{1,0:T(8,128)(2,1)S(1)}, bf16[1024,512]{1,0:T(8,128)(2,1)S(1)}, u32[]{:S(2)}, u32[]{:S(2)}) collective-permute-start(bf16[1024,512]{1,0:T(8,128)(2,1)S(1)} %collective-permute-done.14.refs_12_.refs_4_), channel_id=1, source_target_pairs={{0,8},{8,0},{16,24},{24,16},{32,40},{40,32},{48,56},{56,48},{64,72... | collective-permute-start | bytes 3145736 | tf_op jit(solution)/shard_map/ppermute | solution.py:42
  107.3 20.8 %all-to-all-start = ((bf16[32,16,640]{2,1,0:T(8,128)(2,1)}), bf16[32,16,640]{2,1,0:T(8,128)(2,1)}, u32[]{:S(2)}, u32[]{:S(2)}) async-start(bf16[32,16,640]{2,1,0:T(8,128)(2,1)} %bitcast.8), calls=%async_computation | async-start | bytes 1310720 | tf_op jit(solution)/shard_map/all_to_all | solution.py:346
  134.0 15.1 %all-to-all-start.1 = ((bf16[8,16,640]{2,1,0:T(8,128)(2,1)}), bf16[8,16,640]{2,1,0:T(8,128)(2,1)S(1)}, u32[]{:S(2)}, u32[]{:S(2)}) async-start(bf16[8,16,640]{2,1,0:T(8,128)(2,1)} %merge_project.1), calls=%async_computation.1 | async-start | bytes 327680 | tf_op jit(solution)/shard_map/all_to_all | solution.py:348
  151.5 19.3 %all-to-all-start.2 = ((bf16[32,16,640]{2,1,0:T(8,128)(2,1)}), bf16[32,16,640]{2,1,0:T(8,128)(2,1)S(1)}, u32[]{:S(2)}, u32[]{:S(2)}) async-start(bf16[32,16,640]{2,1,0:T(8,128)(2,1)} %add_rows.1), calls=%async_computation.2 | async-start | bytes 1310720 | tf_op jit(solution)/shard_map/all_to_all | solution.py:350
  (24 other events, 290.1 us)

commit v5 on v3

--- a/solution.py
+++ b/solution.py
@@ -72,10 +72,12 @@
     theirs3 = along_tp_by_core(theirs2)
     mine4 = along_tp_by_core(mine3)
     passed2, go = other_core(theirs2), other_core(g2)
-    ga, mine3, passed1 = together((ga, mine3, passed1))
+    ga, mine3 = together((ga, mine3))
     half = g.shape[0] // 2
     gc, gd = in_plane(ga[:half], 1, True), in_plane(gb[half:], -1, True)
-    theirs3, ga2, gb2, mine4, passed2 = together((theirs3, ga, gb, mine4, passed2))
+    theirs3, ga2, gb2, mine4, passed1, passed2 = together(
+        (theirs3, ga, gb, mine4, passed1, passed2)
+    )
     passed3, gao, gbo = other_core(theirs3), other_core(ga2), other_core(gb2)
     gc, gd, mine4 = together((gc, gd, mine4))
     held = [tokens, mine1, mine2, mine3, mine4, passed1, passed2, passed3]
@@ -195,7 +197,7 @@
             pltpu.VMEM((640, 128), F32),
             pltpu.SemaphoreType.DMA((4,)),
         ],
-        compiler_params=pltpu.CompilerParams(vmem_limit_bytes=54 * 2**20),
+        compiler_params=pltpu.CompilerParams(vmem_limit_bytes=58 * 2**20),
         cost_estimate=pl.CostEstimate(
             flops=5 * 10**9, bytes_accessed=30 * 2**20, transcendentals=2**19
         ),

time: 167 us -> 165 us (0.988)
  starting transfers between devices: 58.8 us -> 55.8 us
  waiting for transfers between devices: 66.3 us -> 68.2 us
    ppermute x9, starting transfers between devices: 15.6 us -> 10.8 us  [other_core(): return lax.ppermute(v, 'sec', [(i, i ^ 1) for i in range(s)])]
    ppermute x8, waiting for transfers between devices: 12.8 us -> 16.7 us  [in_plane(): return lax.ppermute(v, 'sec', pairs)]
    ppermute x7, waiting for transfers between devices: 19.3 us -> 17.3 us  [along_tp_by_core(): return lax.ppermute(v, ('sec', 'tp'), pairs)]
where the time goes in v5:
time: 165 us; the launch traced here: 164 us
  waiting for transfers between devices  68.2 us (41%)
  starting transfers between devices  55.8 us (34%)
  Pallas kernels  28.6 us (17%)
  local copies, waits for them, and re-layouts  8.32 us (5%)
  other arithmetic  2.18 us (1%)
    ppermute x7, waiting for transfers between devices, along_tp_by_core(): return lax.ppermute(v, ('sec', 'tp'), pairs)  17.3 us
    ppermute x8, waiting for transfers between devices, in_plane(): return lax.ppermute(v, 'sec', pairs)  16.7 us
    ppermute x7, starting transfers between devices, along_tp_by_core(): return lax.ppermute(v, ('sec', 'tp'), pairs)  15.9 us
    pallas_call x1, Pallas kernels, attend(): pl.pallas_call(attend_kernel, in_specs=[pl.BlockSpec(memory_space=pltpu.S...  14.4 us
    all_to_all x1, waiting for transfers between devices, on_device(): finished = lax.all_to_all(add_rows(terms, rows), 'sec', 0, 0, tiled=True)  13.1 us
    ppermute x8, starting transfers between devices, in_plane(): return lax.ppermute(v, 'sec', pairs)  12.2 us
    ppermute x9, starting transfers between devices, other_core(): return lax.ppermute(v, 'sec', [(i, i ^ 1) for i in range(s)])  10.8 us
    all_to_all x1, waiting for transfers between devices, on_device(): terms = lax.all_to_all(terms, 'tp', 0, 0, tiled=True)  8.91 us
  transfers between devices with their start and end apart: 27, of which 13 were waited for; matrix products, arithmetic and copies ran while one was open for 2% of the time, Pallas kernels for 3%

profile of v5, /device:TPU:1, one launch (start us, length us, event | category | flops | bytes accessed | tf_op | source)
XLA Modules:
  0.0 164.1 jit_solution(7961296301277833807)
XLA Ops:
  4.7 3.2 %collective-permute-start.5 = (bf16[640,512]{1,0:T(8,128)(2,1)}, bf16[640,512]{1,0:T(8,128)(2,1)S(1)}, u32[]{:S(2)}, u32[]{:S(2)}) collective-permute-start(bf16[640,512]{1,0:T(8,128)(2,1)} %get-tuple-element.25.refs_0_), channel_id=1, source_target_pairs={{0,8},{8,0},{16,24},{24,16},{32,40},{40,32},{48,56},{56,48},{64,72... | collective-permute-start | bytes 1966088 | tf_op jit(solution)/shard_map/ppermute | solution.py:42
  7.9 3.8 %collective-permute-start.2 = (bf16[640,512]{1,0:T(8,128)(2,1)}, bf16[640,512]{1,0:T(8,128)(2,1)S(1)}, u32[]{:S(2)}, u32[]{:S(2)}) collective-permute-start(bf16[640,512]{1,0:T(8,128)(2,1)} %get-tuple-element.25.refs_0_), channel_id=1, source_target_pairs={{0,1},{1,2},{2,3},{3,4},{4,5},{5,6},{6,7},{7,0},{8,15},{9,8},{10,9... | collective-permute-start | bytes 1966088 | tf_op jit(solution)/shard_map/ppermute | solution.py:37
  15.2 6.3 %collective-permute-done = bf16[512,512]{1,0:T(8,128)(2,1)S(1)} collective-permute-done((bf16[512,512]{1,0:T(8,128)(2,1)}, bf16[512,512]{1,0:T(8,128)(2,1)S(1)}, u32[]{:S(2)}, u32[]{:S(2)}) %collective-permute-start) | collective-permute-done | bytes 524320 | tf_op jit(solution)/shard_map/ppermute | solution.py:53
  26.7 2.8 %collective-permute-done.3 = bf16[256,512]{1,0:T(8,128)(2,1)S(1)} collective-permute-done((bf16[256,512]{1,0:T(8,128)(2,1)S(1)}, bf16[256,512]{1,0:T(8,128)(2,1)S(1)}, u32[]{:S(2)}, u32[]{:S(2)}) %collective-permute-start.3) | collective-permute-done | bytes 262176 | tf_op jit(solution)/shard_map/ppermute | solution.py:53
  31.0 2.6 %collective-permute-done.7.refs_2_ = bf16[640,512]{1,0:T(8,128)(2,1)S(1)} collective-permute-done((bf16[640,512]{1,0:T(8,128)(2,1)S(1)}, bf16[640,512]{1,0:T(8,128)(2,1)S(1)}, u32[]{:S(2)}, u32[]{:S(2)}) %collective-permute-start.7) | collective-permute-done | bytes 655392 | tf_op jit(solution)/shard_map/ppermute | solution.py:37
  33.5 2.5 %collective-permute-start.11 = (bf16[2048,512]{1,0:T(8,128)(2,1)S(1)}, bf16[2048,512]{1,0:T(8,128)(2,1)S(1)}, u32[]{:S(2)}, u32[]{:S(2)}) collective-permute-start(bf16[2048,512]{1,0:T(8,128)(2,1)S(1)} %constant_dynamic-update-slice_fusion.refs_8_.refs_0_), channel_id=1, source_target_pairs={{0,48},{8,200},{16,0},{24,216},{32,16},{40,232},{48,32},{56,248},{... | collective-permute-start | bytes 6291464 | tf_op jit(solution)/shard_map/ppermute | solution.py:53
  36.0 3.4 %collective-permute-start.13 = (bf16[640,512]{1,0:T(8,128)(2,1)S(1)}, bf16[640,512]{1,0:T(8,128)(2,1)S(1)}, u32[]{:S(2)}, u32[]{:S(2)}) collective-permute-start(bf16[640,512]{1,0:T(8,128)(2,1)S(1)} %collective-permute-done.6), channel_id=1, source_target_pairs={{0,1},{1,2},{2,3},{3,4},{4,5},{5,6},{6,7},{7,0},{8,15},{9,8},{10,9... | collective-permute-start | bytes 1966088 | tf_op jit(solution)/shard_map/ppermute | solution.py:37
  39.5 7.5 %collective-permute-done.13 = bf16[640,512]{1,0:T(8,128)(2,1)S(1)} collective-permute-done((bf16[640,512]{1,0:T(8,128)(2,1)S(1)}, bf16[640,512]{1,0:T(8,128)(2,1)S(1)}, u32[]{:S(2)}, u32[]{:S(2)}) %collective-permute-start.13) | collective-permute-done | bytes 655392 | tf_op jit(solution)/shard_map/ppermute | solution.py:37
  47.0 3.4 %collective-permute-start.14 = (bf16[640,512]{1,0:T(8,128)(2,1)S(1)}, bf16[640,512]{1,0:T(8,128)(2,1)S(1)}, u32[]{:S(2)}, u32[]{:S(2)}) collective-permute-start(bf16[640,512]{1,0:T(8,128)(2,1)S(1)} %collective-permute-done.13), channel_id=1, source_target_pairs={{0,1},{1,2},{2,3},{3,4},{4,5},{5,6},{6,7},{7,0},{8,15},{9,8},{10,9... | collective-permute-start | bytes 1966088 | tf_op jit(solution)/shard_map/ppermute | solution.py:37
  50.4 3.6 %collective-permute-done.9.refs_3_ = bf16[640,512]{1,0:T(8,128)(2,1)S(1)} collective-permute-done((bf16[640,512]{1,0:T(8,128)(2,1)S(1)}, bf16[640,512]{1,0:T(8,128)(2,1)S(1)}, u32[]{:S(2)}, u32[]{:S(2)}) %collective-permute-start.9) | collective-permute-done | bytes 655392 | tf_op jit(solution)/shard_map/ppermute | solution.py:37
  54.0 3.4 %collective-permute-start.15 = (bf16[640,512]{1,0:T(8,128)(2,1)S(1)}, bf16[640,512]{1,0:T(8,128)(2,1)S(1)}, u32[]{:S(2)}, u32[]{:S(2)}) collective-permute-start(bf16[640,512]{1,0:T(8,128)(2,1)S(1)} %collective-permute-done.9.refs_3_), channel_id=1, source_target_pairs={{0,1},{1,2},{2,3},{3,4},{4,5},{5,6},{6,7},{7,0},{8,15},{9,8},{10,9... | collective-permute-start | bytes 1966088 | tf_op jit(solution)/shard_map/ppermute | solution.py:37
  64.4 3.7 %collective-permute-done.15.refs_4_ = bf16[640,512]{1,0:T(8,128)(2,1)S(1)} collective-permute-done((bf16[640,512]{1,0:T(8,128)(2,1)S(1)}, bf16[640,512]{1,0:T(8,128)(2,1)S(1)}, u32[]{:S(2)}, u32[]{:S(2)}) %collective-permute-start.15) | collective-permute-done | bytes 655392 | tf_op jit(solution)/shard_map/ppermute | solution.py:37
  68.0 2.8 %collective-permute-start.20 = (bf16[2048,512]{1,0:T(8,128)(2,1)S(1)}, bf16[2048,512]{1,0:T(8,128)(2,1)S(1)}, u32[]{:S(2)}, u32[]{:S(2)}) collective-permute-start(bf16[2048,512]{1,0:T(8,128)(2,1)S(1)} %collective-permute-done.8.refs_9_.refs_1_), channel_id=1, source_target_pairs={{0,8},{8,0},{16,24},{24,16},{32,40},{40,32},{48,56},{56,48},{64,72... | collective-permute-start | bytes 6291464 | tf_op jit(solution)/shard_map/ppermute | solution.py:42
  71.0 5.9 %collective-permute-done.10.refs_11_.refs_3_ = bf16[1024,512]{1,0:T(8,128)(2,1)S(1)} collective-permute-done((bf16[1024,512]{1,0:T(8,128)(2,1)S(1)}, bf16[1024,512]{1,0:T(8,128)(2,1)S(1)}, u32[]{:S(2)}, u32[]{:S(2)}) %collective-permute-start.10) | collective-permute-done | bytes 1048608 | tf_op jit(solution)/shard_map/ppermute | solution.py:53
  79.0 4.2 %collective-permute-done.18.refs_7_ = bf16[640,512]{1,0:T(8,128)(2,1)S(1)} collective-permute-done((bf16[640,512]{1,0:T(8,128)(2,1)S(1)}, bf16[640,512]{1,0:T(8,128)(2,1)S(1)}, u32[]{:S(2)}, u32[]{:S(2)}) %collective-permute-start.18) | collective-permute-done | bytes 655392 | tf_op jit(solution)/shard_map/ppermute | solution.py:42
  86.6 14.4 %project_attend.1 = bf16[512,640]{1,0:T(8,128)(2,1)} custom-call(s32[5]{0:T(128)} %pad_add_fusion.info, f32[2,4096]{1,0:T(2,128)} %get-tuple-element.24.gains, bf16[640,512]{1,0:T(8,128)(2,1)} %get-tuple-element.25.refs_0_, bf16[640,512]{1,0:T(8,128)(2,1)} %copy-done.11, bf16[640,512]{1,0:T(8,128)(2,1)} %copy-done.12, bf16[640,512]{1,0:T(8,128)(2,1)} %copy-done.13, ...), custom_call_target="tpu_custom_call" | custom-call | flops 5000000000 | bytes 31457280 | tf_op jit(solution)/shard_map/project_attend/pallas_call | solution.py:186
  101.0 7.4 %all-to-all-start = ((bf16[32,16,640]{2,1,0:T(8,128)(2,1)}), bf16[32,16,640]{2,1,0:T(8,128)(2,1)S(1)}, u32[]{:S(2)}, u32[]{:S(2)}) async-start(bf16[32,16,640]{2,1,0:T(8,128)(2,1)} %bitcast.8), calls=%async_computation | async-start | bytes 1310720 | tf_op jit(solution)/shard_map/all_to_all | solution.py:364
  108.4 5.0 %assemble_out.1.wo = bf16[4096,512]{1,0:T(8,128)(2,1)} custom-call(s32[5]{0:T(128)} %pad_add_fusion.info, bf16[2048,512]{1,0:T(8,128)(2,1)} %copy-done.2, bf16[2048,512]{1,0:T(8,128)(2,1)} %copy-done, bf16[2048,512]{1,0:T(8,128)(2,1)} %copy-done.1, bf16[1024,512]{1,0:T(8,128)(2,1)} %copy-done.6, bf16[1024,512]{1,0:T(8,128)(2,1)} %copy-done.7, ...), custom_call_target="tpu_custom_call" | custom-call | bytes 8388608 | tf_op jit(solution)/shard_map/assemble_out/pallas_call | solution.py:222
  113.4 8.0 %all-to-all-done = bf16[32,16,640]{2,1,0:T(8,128)(2,1)S(1)} async-done(((bf16[32,16,640]{2,1,0:T(8,128)(2,1)}), bf16[32,16,640]{2,1,0:T(8,128)(2,1)S(1)}, u32[]{:S(2)}, u32[]{:S(2)}) %all-to-all-start) | async-done | bytes 655392 | tf_op jit(solution)/shard_map/all_to_all | solution.py:364
  122.2 4.9 %merge_project.1 = bf16[8,16,640]{2,1,0:T(8,128)(2,1)} custom-call(bf16[512,640]{1,0:T(8,128)(2,1)} %bitcast.9, bf16[4096,512]{1,0:T(8,128)(2,1)} %assemble_out.1.wo), custom_call_target="tpu_custom_call" | custom-call | tf_op jit(solution)/shard_map/merge_project/pallas_call | solution.py:284
  127.2 5.6 %all-to-all-start.1 = ((bf16[8,16,640]{2,1,0:T(8,128)(2,1)}), bf16[8,16,640]{2,1,0:T(8,128)(2,1)S(1)}, u32[]{:S(2)}, u32[]{:S(2)}) async-start(bf16[8,16,640]{2,1,0:T(8,128)(2,1)} %merge_project.1), calls=%async_computation.1 | async-start | bytes 327680 | tf_op jit(solution)/shard_map/all_to_all | solution.py:366
  134.0 8.9 %all-to-all-done.1.got = bf16[8,16,640]{2,1,0:T(8,128)(2,1)S(1)} async-done(((bf16[8,16,640]{2,1,0:T(8,128)(2,1)}), bf16[8,16,640]{2,1,0:T(8,128)(2,1)S(1)}, u32[]{:S(2)}, u32[]{:S(2)}) %all-to-all-start.1) | async-done | bytes 163872 | tf_op jit(solution)/shard_map/all_to_all | solution.py:366
  145.4 4.1 %all-to-all-start.2 = ((bf16[32,16,640]{2,1,0:T(8,128)(2,1)}), bf16[32,16,640]{2,1,0:T(8,128)(2,1)S(1)}, u32[]{:S(2)}, u32[]{:S(2)}) async-start(bf16[32,16,640]{2,1,0:T(8,128)(2,1)} %add_rows.1), calls=%async_computation.2 | async-start | bytes 1310720 | tf_op jit(solution)/shard_map/all_to_all | solution.py:368
  149.5 13.1 %all-to-all-done.2 = bf16[32,16,640]{2,1,0:T(8,128)(2,1)S(1)} async-done(((bf16[32,16,640]{2,1,0:T(8,128)(2,1)}), bf16[32,16,640]{2,1,0:T(8,128)(2,1)S(1)}, u32[]{:S(2)}, u32[]{:S(2)}) %all-to-all-start.2) | async-done | bytes 655392 | tf_op jit(solution)/shard_map/all_to_all | solution.py:368
  (90 shorter events, 32.7 us)
Async XLA Ops:
  4.7 9.8 %collective-permute-start.5 = (bf16[640,512]{1,0:T(8,128)(2,1)}, bf16[640,512]{1,0:T(8,128)(2,1)S(1)}, u32[]{:S(2)}, u32[]{:S(2)}) collective-permute-start(bf16[640,512]{1,0:T(8,128)(2,1)} %get-tuple-element.25.refs_0_), channel_id=1, source_target_pairs={{0,8},{8,0},{16,24},{24,16},{32,40},{40,32},{48,56},{56,48},{64,72... | collective-permute-start | bytes 1966088 | tf_op jit(solution)/shard_map/ppermute | solution.py:42
  7.9 13.7 %collective-permute-start.2 = (bf16[640,512]{1,0:T(8,128)(2,1)}, bf16[640,512]{1,0:T(8,128)(2,1)S(1)}, u32[]{:S(2)}, u32[]{:S(2)}) collective-permute-start(bf16[640,512]{1,0:T(8,128)(2,1)} %get-tuple-element.25.refs_0_), channel_id=1, source_target_pairs={{0,1},{1,2},{2,3},{3,4},{4,5},{5,6},{6,7},{7,0},{8,15},{9,8},{10,9... | collective-permute-start | bytes 1966088 | tf_op jit(solution)/shard_map/ppermute | solution.py:37
  11.7 9.8 %collective-permute-start = (bf16[512,512]{1,0:T(8,128)(2,1)}, bf16[512,512]{1,0:T(8,128)(2,1)S(1)}, u32[]{:S(2)}, u32[]{:S(2)}) collective-permute-start(bf16[512,512]{1,0:T(8,128)(2,1)} %get-tuple-element.26), channel_id=1, source_target_pairs={{0,64},{8,24},{16,80},{24,40},{32,96},{40,56},{48,112},{56,8},{64,... | collective-permute-start | bytes 1572872 | tf_op jit(solution)/shard_map/ppermute | solution.py:53
  13.0 8.5 %collective-permute-start.1 = (bf16[512,512]{1,0:T(8,128)(2,1)}, bf16[512,512]{1,0:T(8,128)(2,1)S(1)}, u32[]{:S(2)}, u32[]{:S(2)}) collective-permute-start(bf16[512,512]{1,0:T(8,128)(2,1)} %get-tuple-element.26), channel_id=1, source_target_pairs={{0,192},{8,56},{16,208},{24,8},{32,224},{40,24},{48,240},{56,40},{... | collective-permute-start | bytes 1572872 | tf_op jit(solution)/shard_map/ppermute | solution.py:53
  14.5 15.1 %collective-permute-start.6 = (bf16[640,512]{1,0:T(8,128)(2,1)S(1)}, bf16[640,512]{1,0:T(8,128)(2,1)S(1)}, u32[]{:S(2)}, u32[]{:S(2)}) collective-permute-start(bf16[640,512]{1,0:T(8,128)(2,1)S(1)} %collective-permute-done.5), channel_id=1, source_target_pairs={{0,1},{1,2},{2,3},{3,4},{4,5},{5,6},{6,7},{7,0},{8,15},{9,8},{10,9... | collective-permute-start | bytes 1966088 | tf_op jit(solution)/shard_map/ppermute | solution.py:37
  21.6 11.9 %collective-permute-start.7 = (bf16[640,512]{1,0:T(8,128)(2,1)S(1)}, bf16[640,512]{1,0:T(8,128)(2,1)S(1)}, u32[]{:S(2)}, u32[]{:S(2)}) collective-permute-start(bf16[640,512]{1,0:T(8,128)(2,1)S(1)} %collective-permute-done.2.refs_1_), channel_id=1, source_target_pairs={{0,1},{1,2},{2,3},{3,4},{4,5},{5,6},{6,7},{7,0},{8,15},{9,8},{10,9... | collective-permute-start | bytes 1966088 | tf_op jit(solution)/shard_map/ppermute | solution.py:37
  22.6 6.9 %collective-permute-start.3 = (bf16[256,512]{1,0:T(8,128)(2,1)S(1)}, bf16[256,512]{1,0:T(8,128)(2,1)S(1)}, u32[]{:S(2)}, u32[]{:S(2)}) collective-permute-start(bf16[256,512]{1,0:T(8,128)(2,1)S(1)} %slice.25), channel_id=1, source_target_pairs={{0,64},{8,24},{16,80},{24,40},{32,96},{40,56},{48,112},{56,8},{64,... | collective-permute-start | bytes 786440 | tf_op jit(solution)/shard_map/ppermute | solution.py:53
  29.7 27.7 %collective-permute-start.8 = (bf16[2048,512]{1,0:T(8,128)(2,1)S(1)}, bf16[2048,512]{1,0:T(8,128)(2,1)S(1)}, u32[]{:S(2)}, u32[]{:S(2)}) collective-permute-start(bf16[2048,512]{1,0:T(8,128)(2,1)S(1)} %constant_dynamic-update-slice_fusion.refs_8_.refs_0_), channel_id=1, source_target_pairs={{0,16},{8,72},{16,32},{24,88},{32,48},{40,104},{48,0},{56,120},{64... | collective-permute-start | bytes 6291464 | tf_op jit(solution)/shard_map/ppermute | solution.py:53
  33.5 25.5 %collective-permute-start.11 = (bf16[2048,512]{1,0:T(8,128)(2,1)S(1)}, bf16[2048,512]{1,0:T(8,128)(2,1)S(1)}, u32[]{:S(2)}, u32[]{:S(2)}) collective-permute-start(bf16[2048,512]{1,0:T(8,128)(2,1)S(1)} %constant_dynamic-update-slice_fusion.refs_8_.refs_0_), channel_id=1, source_target_pairs={{0,48},{8,200},{16,0},{24,216},{32,16},{40,232},{48,32},{56,248},{... | collective-permute-start | bytes 6291464 | tf_op jit(solution)/shard_map/ppermute | solution.py:53
  36.0 10.9 %collective-permute-start.13 = (bf16[640,512]{1,0:T(8,128)(2,1)S(1)}, bf16[640,512]{1,0:T(8,128)(2,1)S(1)}, u32[]{:S(2)}, u32[]{:S(2)}) collective-permute-start(bf16[640,512]{1,0:T(8,128)(2,1)S(1)} %collective-permute-done.6), channel_id=1, source_target_pairs={{0,1},{1,2},{2,3},{3,4},{4,5},{5,6},{6,7},{7,0},{8,15},{9,8},{10,9... | collective-permute-start | bytes 1966088 | tf_op jit(solution)/shard_map/ppermute | solution.py:37
  39.4 14.6 %collective-permute-start.9 = (bf16[640,512]{1,0:T(8,128)(2,1)S(1)}, bf16[640,512]{1,0:T(8,128)(2,1)S(1)}, u32[]{:S(2)}, u32[]{:S(2)}) collective-permute-start(bf16[640,512]{1,0:T(8,128)(2,1)S(1)} %collective-permute-done.7.refs_2_), channel_id=1, source_target_pairs={{0,1},{1,2},{2,3},{3,4},{4,5},{5,6},{6,7},{7,0},{8,15},{9,8},{10,9... | collective-permute-start | bytes 1966088 | tf_op jit(solution)/shard_map/ppermute | solution.py:37
  39.5 22.1 %collective-permute-start.16 = (bf16[640,512]{1,0:T(8,128)(2,1)S(1)}, bf16[640,512]{1,0:T(8,128)(2,1)S(1)}, u32[]{:S(2)}, u32[]{:S(2)}) collective-permute-start(bf16[640,512]{1,0:T(8,128)(2,1)S(1)} %collective-permute-done.6), channel_id=1, source_target_pairs={{0,8},{8,0},{16,24},{24,16},{32,40},{40,32},{48,56},{56,48},{64,72... | collective-permute-start | bytes 1966088 | tf_op jit(solution)/shard_map/ppermute | solution.py:42
  47.0 15.9 %collective-permute-start.14 = (bf16[640,512]{1,0:T(8,128)(2,1)S(1)}, bf16[640,512]{1,0:T(8,128)(2,1)S(1)}, u32[]{:S(2)}, u32[]{:S(2)}) collective-permute-start(bf16[640,512]{1,0:T(8,128)(2,1)S(1)} %collective-permute-done.13), channel_id=1, source_target_pairs={{0,1},{1,2},{2,3},{3,4},{4,5},{5,6},{6,7},{7,0},{8,15},{9,8},{10,9... | collective-permute-start | bytes 1966088 | tf_op jit(solution)/shard_map/ppermute | solution.py:37
  54.0 14.0 %collective-permute-start.15 = (bf16[640,512]{1,0:T(8,128)(2,1)S(1)}, bf16[640,512]{1,0:T(8,128)(2,1)S(1)}, u32[]{:S(2)}, u32[]{:S(2)}) collective-permute-start(bf16[640,512]{1,0:T(8,128)(2,1)S(1)} %collective-permute-done.9.refs_3_), channel_id=1, source_target_pairs={{0,1},{1,2},{2,3},{3,4},{4,5},{5,6},{6,7},{7,0},{8,15},{9,8},{10,9... | collective-permute-start | bytes 1966088 | tf_op jit(solution)/shard_map/ppermute | solution.py:37
  57.4 10.6 %collective-permute-start.17 = (bf16[640,512]{1,0:T(8,128)(2,1)S(1)}, bf16[640,512]{1,0:T(8,128)(2,1)S(1)}, u32[]{:S(2)}, u32[]{:S(2)}) collective-permute-start(bf16[640,512]{1,0:T(8,128)(2,1)S(1)} %collective-permute-done.13), channel_id=1, source_target_pairs={{0,8},{8,0},{16,24},{24,16},{32,40},{40,32},{48,56},{56,48},{64,72... | collective-permute-start | bytes 1966088 | tf_op jit(solution)/shard_map/ppermute | solution.py:42
  59.0 19.5 %collective-permute-start.19 = (bf16[2048,512]{1,0:T(8,128)(2,1)S(1)}, bf16[2048,512]{1,0:T(8,128)(2,1)S(1)}, u32[]{:S(2)}, u32[]{:S(2)}) collective-permute-start(bf16[2048,512]{1,0:T(8,128)(2,1)S(1)} %constant_dynamic-update-slice_fusion.refs_8_.refs_0_), channel_id=1, source_target_pairs={{0,8},{8,0},{16,24},{24,16},{32,40},{40,32},{48,56},{56,48},{64,72... | collective-permute-start | bytes 6291464 | tf_op jit(solution)/shard_map/ppermute | solution.py:42
  61.6 15.2 %collective-permute-start.10 = (bf16[1024,512]{1,0:T(8,128)(2,1)S(1)}, bf16[1024,512]{1,0:T(8,128)(2,1)S(1)}, u32[]{:S(2)}, u32[]{:S(2)}) collective-permute-start(bf16[1024,512]{1,0:T(8,128)(2,1)S(1)} %slice.27), channel_id=1, source_target_pairs={{0,16},{8,72},{16,32},{24,88},{32,48},{40,104},{48,0},{56,120},{64... | collective-permute-start | bytes 3145736 | tf_op jit(solution)/shard_map/ppermute | solution.py:53
  62.9 13.9 %collective-permute-start.12 = (bf16[1024,512]{1,0:T(8,128)(2,1)S(1)}, bf16[1024,512]{1,0:T(8,128)(2,1)S(1)}, u32[]{:S(2)}, u32[]{:S(2)}) collective-permute-start(bf16[1024,512]{1,0:T(8,128)(2,1)S(1)} %slice.31), channel_id=1, source_target_pairs={{0,48},{8,200},{16,0},{24,216},{32,16},{40,232},{48,32},{56,248},{... | collective-permute-start | bytes 3145736 | tf_op jit(solution)/shard_map/ppermute | solution.py:53
  68.0 15.2 %collective-permute-start.20 = (bf16[2048,512]{1,0:T(8,128)(2,1)S(1)}, bf16[2048,512]{1,0:T(8,128)(2,1)S(1)}, u32[]{:S(2)}, u32[]{:S(2)}) collective-permute-start(bf16[2048,512]{1,0:T(8,128)(2,1)S(1)} %collective-permute-done.8.refs_9_.refs_1_), channel_id=1, source_target_pairs={{0,8},{8,0},{16,24},{24,16},{32,40},{40,32},{48,56},{56,48},{64,72... | collective-permute-start | bytes 6291464 | tf_op jit(solution)/shard_map/ppermute | solution.py:42
  70.9 12.4 %collective-permute-start.21 = (bf16[2048,512]{1,0:T(8,128)(2,1)S(1)}, bf16[2048,512]{1,0:T(8,128)(2,1)S(1)}, u32[]{:S(2)}, u32[]{:S(2)}) collective-permute-start(bf16[2048,512]{1,0:T(8,128)(2,1)S(1)} %collective-permute-done.11.refs_10_.refs_2_), channel_id=1, source_target_pairs={{0,8},{8,0},{16,24},{24,16},{32,40},{40,32},{48,56},{56,48},{64,72... | collective-permute-start | bytes 6291464 | tf_op jit(solution)/shard_map/ppermute | solution.py:42
  76.8 6.4 %collective-permute-start.22 = (bf16[1024,512]{1,0:T(8,128)(2,1)S(1)}, bf16[1024,512]{1,0:T(8,128)(2,1)S(1)}, u32[]{:S(2)}, u32[]{:S(2)}) collective-permute-start(bf16[1024,512]{1,0:T(8,128)(2,1)S(1)} %collective-permute-done.10.refs_11_.refs_3_), channel_id=1, source_target_pairs={{0,8},{8,0},{16,24},{24,16},{32,40},{40,32},{48,56},{56,48},{64,72... | collective-permute-start | bytes 3145736 | tf_op jit(solution)/shard_map/ppermute | solution.py:42
  101.0 20.3 %all-to-all-start = ((bf16[32,16,640]{2,1,0:T(8,128)(2,1)}), bf16[32,16,640]{2,1,0:T(8,128)(2,1)S(1)}, u32[]{:S(2)}, u32[]{:S(2)}) async-start(bf16[32,16,640]{2,1,0:T(8,128)(2,1)} %bitcast.8), calls=%async_computation | async-start | bytes 1310720 | tf_op jit(solution)/shard_map/all_to_all | solution.py:364
  127.2 15.8 %all-to-all-start.1 = ((bf16[8,16,640]{2,1,0:T(8,128)(2,1)}), bf16[8,16,640]{2,1,0:T(8,128)(2,1)S(1)}, u32[]{:S(2)}, u32[]{:S(2)}) async-start(bf16[8,16,640]{2,1,0:T(8,128)(2,1)} %merge_project.1), calls=%async_computation.1 | async-start | bytes 327680 | tf_op jit(solution)/shard_map/all_to_all | solution.py:366
  145.4 17.1 %all-to-all-start.2 = ((bf16[32,16,640]{2,1,0:T(8,128)(2,1)}), bf16[32,16,640]{2,1,0:T(8,128)(2,1)S(1)}, u32[]{:S(2)}, u32[]{:S(2)}) async-start(bf16[32,16,640]{2,1,0:T(8,128)(2,1)} %add_rows.1), calls=%async_computation.2 | async-start | bytes 1310720 | tf_op jit(solution)/shard_map/all_to_all | solution.py:368
  (22 other events, 279.4 us)

commit v6 on v5

--- a/solution.py
+++ b/solution.py
@@ -231,7 +231,10 @@
     )(info, *w_parts)
 
 
-def merge_kernel(got, wo, out):
+def merge_kernel(got, rows, out, wo, sems):
+    for z in range(8):
+        at = pl.ds(512 * z, 512)
+        pltpu.make_async_copy(rows.at[at], wo.at[at], sems.at[z]).start()
     st = got[:, 512:640].astype(F32)
     both = st + pltpu.roll(st, 120, 1)
     sum_a = pltpu.roll(both, 112, 1).reshape(32, 16, 128)
@@ -270,6 +273,8 @@
     row = lax.broadcasted_iota(jnp.int32, (16, 128), 0)
     extra = jnp.where(row == 0, pool_hi, jnp.where(row == 1, pool_lo, 0.0)).astype(BF16)
     for z in range(8):
+        at = pl.ds(512 * z, 512)
+        pltpu.make_async_copy(rows.at[at], wo.at[at], sems.at[z]).wait()
         term = lax.dot_general(
             context,
             wo[512 * z : 512 * (z + 1), :],
@@ -283,7 +288,13 @@
 def merge(got, wo):
     return pl.pallas_call(
         merge_kernel,
+        in_specs=[
+            pl.BlockSpec(memory_space=pltpu.VMEM),
+            pl.BlockSpec(memory_space=pl.ANY),
+        ],
+        out_specs=pl.BlockSpec(memory_space=pltpu.VMEM),
         out_shape=jax.ShapeDtypeStruct((8, 16, 640), BF16),
+        scratch_shapes=[pltpu.VMEM((4096, 512), BF16), pltpu.SemaphoreType.DMA((8,))],
         compiler_params=pltpu.CompilerParams(vmem_limit_bytes=58 * 2**20),
         name="merge_project",
     )(got, wo)

time: 165 us -> 165 us (level)
  no operation moved by 1% of the time
where the time goes in v6:
time: 165 us; the launch traced here: 164 us
  waiting for transfers between devices  68.2 us (41%)
  starting transfers between devices  55.8 us (34%)
  Pallas kernels  28.6 us (17%)
  local copies, waits for them, and re-layouts  8.32 us (5%)
  other arithmetic  2.18 us (1%)
    ppermute x7, waiting for transfers between devices, along_tp_by_core(): return lax.ppermute(v, ('sec', 'tp'), pairs)  17.3 us
    ppermute x8, waiting for transfers between devices, in_plane(): return lax.ppermute(v, 'sec', pairs)  16.7 us
    ppermute x7, starting transfers between devices, along_tp_by_core(): return lax.ppermute(v, ('sec', 'tp'), pairs)  15.9 us
    pallas_call x1, Pallas kernels, attend(): pl.pallas_call(attend_kernel, in_specs=[pl.BlockSpec(memory_space=pltpu.S...  14.4 us
    all_to_all x1, waiting for transfers between devices, on_device(): finished = lax.all_to_all(add_rows(terms, rows), 'sec', 0, 0, tiled=True)  13.1 us
    ppermute x8, starting transfers between devices, in_plane(): return lax.ppermute(v, 'sec', pairs)  12.2 us
    ppermute x9, starting transfers between devices, other_core(): return lax.ppermute(v, 'sec', [(i, i ^ 1) for i in range(s)])  10.8 us
    all_to_all x1, waiting for transfers between devices, on_device(): terms = lax.all_to_all(terms, 'tp', 0, 0, tiled=True)  8.91 us
  transfers between devices with their start and end apart: 27, of which 13 were waited for; matrix products, arithmetic and copies ran while one was open for 2% of the time, Pallas kernels for 3%

profile of v6, /device:TPU:1, one launch (start us, length us, event | category | flops | bytes accessed | tf_op | source)
XLA Modules:
  0.0 164.1 jit_solution(4540749625506623883)
XLA Ops:
  4.7 3.2 %collective-permute-start.5 = (bf16[640,512]{1,0:T(8,128)(2,1)}, bf16[640,512]{1,0:T(8,128)(2,1)S(1)}, u32[]{:S(2)}, u32[]{:S(2)}) collective-permute-start(bf16[640,512]{1,0:T(8,128)(2,1)} %get-tuple-element.25.refs_0_), channel_id=1, source_target_pairs={{0,8},{8,0},{16,24},{24,16},{32,40},{40,32},{48,56},{56,48},{64,72... | collective-permute-start | bytes 1966088 | tf_op jit(solution)/shard_map/ppermute | solution.py:42
  7.9 3.8 %collective-permute-start.2 = (bf16[640,512]{1,0:T(8,128)(2,1)}, bf16[640,512]{1,0:T(8,128)(2,1)S(1)}, u32[]{:S(2)}, u32[]{:S(2)}) collective-permute-start(bf16[640,512]{1,0:T(8,128)(2,1)} %get-tuple-element.25.refs_0_), channel_id=1, source_target_pairs={{0,1},{1,2},{2,3},{3,4},{4,5},{5,6},{6,7},{7,0},{8,15},{9,8},{10,9... | collective-permute-start | bytes 1966088 | tf_op jit(solution)/shard_map/ppermute | solution.py:37
  15.2 6.3 %collective-permute-done = bf16[512,512]{1,0:T(8,128)(2,1)S(1)} collective-permute-done((bf16[512,512]{1,0:T(8,128)(2,1)}, bf16[512,512]{1,0:T(8,128)(2,1)S(1)}, u32[]{:S(2)}, u32[]{:S(2)}) %collective-permute-start) | collective-permute-done | bytes 524320 | tf_op jit(solution)/shard_map/ppermute | solution.py:53
  26.7 2.8 %collective-permute-done.3 = bf16[256,512]{1,0:T(8,128)(2,1)S(1)} collective-permute-done((bf16[256,512]{1,0:T(8,128)(2,1)S(1)}, bf16[256,512]{1,0:T(8,128)(2,1)S(1)}, u32[]{:S(2)}, u32[]{:S(2)}) %collective-permute-start.3) | collective-permute-done | bytes 262176 | tf_op jit(solution)/shard_map/ppermute | solution.py:53
  31.0 2.6 %collective-permute-done.7.refs_2_ = bf16[640,512]{1,0:T(8,128)(2,1)S(1)} collective-permute-done((bf16[640,512]{1,0:T(8,128)(2,1)S(1)}, bf16[640,512]{1,0:T(8,128)(2,1)S(1)}, u32[]{:S(2)}, u32[]{:S(2)}) %collective-permute-start.7) | collective-permute-done | bytes 655392 | tf_op jit(solution)/shard_map/ppermute | solution.py:37
  33.5 2.5 %collective-permute-start.11 = (bf16[2048,512]{1,0:T(8,128)(2,1)S(1)}, bf16[2048,512]{1,0:T(8,128)(2,1)S(1)}, u32[]{:S(2)}, u32[]{:S(2)}) collective-permute-start(bf16[2048,512]{1,0:T(8,128)(2,1)S(1)} %constant_dynamic-update-slice_fusion.refs_8_.refs_0_), channel_id=1, source_target_pairs={{0,48},{8,200},{16,0},{24,216},{32,16},{40,232},{48,32},{56,248},{... | collective-permute-start | bytes 6291464 | tf_op jit(solution)/shard_map/ppermute | solution.py:53
  36.0 3.4 %collective-permute-start.13 = (bf16[640,512]{1,0:T(8,128)(2,1)S(1)}, bf16[640,512]{1,0:T(8,128)(2,1)S(1)}, u32[]{:S(2)}, u32[]{:S(2)}) collective-permute-start(bf16[640,512]{1,0:T(8,128)(2,1)S(1)} %collective-permute-done.6), channel_id=1, source_target_pairs={{0,1},{1,2},{2,3},{3,4},{4,5},{5,6},{6,7},{7,0},{8,15},{9,8},{10,9... | collective-permute-start | bytes 1966088 | tf_op jit(solution)/shard_map/ppermute | solution.py:37
  39.5 7.5 %collective-permute-done.13 = bf16[640,512]{1,0:T(8,128)(2,1)S(1)} collective-permute-done((bf16[640,512]{1,0:T(8,128)(2,1)S(1)}, bf16[640,512]{1,0:T(8,128)(2,1)S(1)}, u32[]{:S(2)}, u32[]{:S(2)}) %collective-permute-start.13) | collective-permute-done | bytes 655392 | tf_op jit(solution)/shard_map/ppermute | solution.py:37
  47.0 3.4 %collective-permute-start.14 = (bf16[640,512]{1,0:T(8,128)(2,1)S(1)}, bf16[640,512]{1,0:T(8,128)(2,1)S(1)}, u32[]{:S(2)}, u32[]{:S(2)}) collective-permute-start(bf16[640,512]{1,0:T(8,128)(2,1)S(1)} %collective-permute-done.13), channel_id=1, source_target_pairs={{0,1},{1,2},{2,3},{3,4},{4,5},{5,6},{6,7},{7,0},{8,15},{9,8},{10,9... | collective-permute-start | bytes 1966088 | tf_op jit(solution)/shard_map/ppermute | solution.py:37
  50.4 3.6 %collective-permute-done.9.refs_3_ = bf16[640,512]{1,0:T(8,128)(2,1)S(1)} collective-permute-done((bf16[640,512]{1,0:T(8,128)(2,1)S(1)}, bf16[640,512]{1,0:T(8,128)(2,1)S(1)}, u32[]{:S(2)}, u32[]{:S(2)}) %collective-permute-start.9) | collective-permute-done | bytes 655392 | tf_op jit(solution)/shard_map/ppermute | solution.py:37
  54.0 3.4 %collective-permute-start.15 = (bf16[640,512]{1,0:T(8,128)(2,1)S(1)}, bf16[640,512]{1,0:T(8,128)(2,1)S(1)}, u32[]{:S(2)}, u32[]{:S(2)}) collective-permute-start(bf16[640,512]{1,0:T(8,128)(2,1)S(1)} %collective-permute-done.9.refs_3_), channel_id=1, source_target_pairs={{0,1},{1,2},{2,3},{3,4},{4,5},{5,6},{6,7},{7,0},{8,15},{9,8},{10,9... | collective-permute-start | bytes 1966088 | tf_op jit(solution)/shard_map/ppermute | solution.py:37
  64.4 3.7 %collective-permute-done.15.refs_4_ = bf16[640,512]{1,0:T(8,128)(2,1)S(1)} collective-permute-done((bf16[640,512]{1,0:T(8,128)(2,1)S(1)}, bf16[640,512]{1,0:T(8,128)(2,1)S(1)}, u32[]{:S(2)}, u32[]{:S(2)}) %collective-permute-start.15) | collective-permute-done | bytes 655392 | tf_op jit(solution)/shard_map/ppermute | solution.py:37
  68.0 2.8 %collective-permute-start.20 = (bf16[2048,512]{1,0:T(8,128)(2,1)S(1)}, bf16[2048,512]{1,0:T(8,128)(2,1)S(1)}, u32[]{:S(2)}, u32[]{:S(2)}) collective-permute-start(bf16[2048,512]{1,0:T(8,128)(2,1)S(1)} %collective-permute-done.8.refs_9_.refs_1_), channel_id=1, source_target_pairs={{0,8},{8,0},{16,24},{24,16},{32,40},{40,32},{48,56},{56,48},{64,72... | collective-permute-start | bytes 6291464 | tf_op jit(solution)/shard_map/ppermute | solution.py:42
  71.0 5.9 %collective-permute-done.10.refs_11_.refs_3_ = bf16[1024,512]{1,0:T(8,128)(2,1)S(1)} collective-permute-done((bf16[1024,512]{1,0:T(8,128)(2,1)S(1)}, bf16[1024,512]{1,0:T(8,128)(2,1)S(1)}, u32[]{:S(2)}, u32[]{:S(2)}) %collective-permute-start.10) | collective-permute-done | bytes 1048608 | tf_op jit(solution)/shard_map/ppermute | solution.py:53
  79.0 4.2 %collective-permute-done.18.refs_7_ = bf16[640,512]{1,0:T(8,128)(2,1)S(1)} collective-permute-done((bf16[640,512]{1,0:T(8,128)(2,1)S(1)}, bf16[640,512]{1,0:T(8,128)(2,1)S(1)}, u32[]{:S(2)}, u32[]{:S(2)}) %collective-permute-start.18) | collective-permute-done | bytes 655392 | tf_op jit(solution)/shard_map/ppermute | solution.py:42
  86.6 14.4 %project_attend.1 = bf16[512,640]{1,0:T(8,128)(2,1)} custom-call(s32[5]{0:T(128)} %pad_add_fusion.info, f32[2,4096]{1,0:T(2,128)} %get-tuple-element.24.gains, bf16[640,512]{1,0:T(8,128)(2,1)} %get-tuple-element.25.refs_0_, bf16[640,512]{1,0:T(8,128)(2,1)} %copy-done.11, bf16[640,512]{1,0:T(8,128)(2,1)} %copy-done.12, bf16[640,512]{1,0:T(8,128)(2,1)} %copy-done.13, ...), custom_call_target="tpu_custom_call" | custom-call | flops 5000000000 | bytes 31457280 | tf_op jit(solution)/shard_map/project_attend/pallas_call | solution.py:186
  101.0 7.4 %all-to-all-start = ((bf16[32,16,640]{2,1,0:T(8,128)(2,1)}), bf16[32,16,640]{2,1,0:T(8,128)(2,1)S(1)}, u32[]{:S(2)}, u32[]{:S(2)}) async-start(bf16[32,16,640]{2,1,0:T(8,128)(2,1)} %bitcast.8), calls=%async_computation | async-start | bytes 1310720 | tf_op jit(solution)/shard_map/all_to_all | solution.py:375
  108.4 5.0 %assemble_out.1.rows = bf16[4096,512]{1,0:T(8,128)(2,1)} custom-call(s32[5]{0:T(128)} %pad_add_fusion.info, bf16[2048,512]{1,0:T(8,128)(2,1)} %copy-done.2, bf16[2048,512]{1,0:T(8,128)(2,1)} %copy-done, bf16[2048,512]{1,0:T(8,128)(2,1)} %copy-done.1, bf16[1024,512]{1,0:T(8,128)(2,1)} %copy-done.6, bf16[1024,512]{1,0:T(8,128)(2,1)} %copy-done.7, ...), custom_call_target="tpu_custom_call" | custom-call | bytes 8388608 | tf_op jit(solution)/shard_map/assemble_out/pallas_call | solution.py:222
  113.4 8.0 %all-to-all-done = bf16[32,16,640]{2,1,0:T(8,128)(2,1)S(1)} async-done(((bf16[32,16,640]{2,1,0:T(8,128)(2,1)}), bf16[32,16,640]{2,1,0:T(8,128)(2,1)S(1)}, u32[]{:S(2)}, u32[]{:S(2)}) %all-to-all-start) | async-done | bytes 655392 | tf_op jit(solution)/shard_map/all_to_all | solution.py:375
  122.2 4.9 %merge_project.1 = bf16[8,16,640]{2,1,0:T(8,128)(2,1)} custom-call(bf16[512,640]{1,0:T(8,128)(2,1)} %bitcast.9, bf16[4096,512]{1,0:T(8,128)(2,1)} %assemble_out.1.rows), custom_call_target="tpu_custom_call" | custom-call | tf_op jit(solution)/shard_map/merge_project/pallas_call | solution.py:289
  127.1 5.6 %all-to-all-start.1 = ((bf16[8,16,640]{2,1,0:T(8,128)(2,1)}), bf16[8,16,640]{2,1,0:T(8,128)(2,1)S(1)}, u32[]{:S(2)}, u32[]{:S(2)}) async-start(bf16[8,16,640]{2,1,0:T(8,128)(2,1)} %merge_project.1), calls=%async_computation.1 | async-start | bytes 327680 | tf_op jit(solution)/shard_map/all_to_all | solution.py:377
  134.0 8.9 %all-to-all-done.1.got = bf16[8,16,640]{2,1,0:T(8,128)(2,1)S(1)} async-done(((bf16[8,16,640]{2,1,0:T(8,128)(2,1)}), bf16[8,16,640]{2,1,0:T(8,128)(2,1)S(1)}, u32[]{:S(2)}, u32[]{:S(2)}) %all-to-all-start.1) | async-done | bytes 163872 | tf_op jit(solution)/shard_map/all_to_all | solution.py:377
  145.4 4.1 %all-to-all-start.2 = ((bf16[32,16,640]{2,1,0:T(8,128)(2,1)}), bf16[32,16,640]{2,1,0:T(8,128)(2,1)S(1)}, u32[]{:S(2)}, u32[]{:S(2)}) async-start(bf16[32,16,640]{2,1,0:T(8,128)(2,1)} %add_rows.1), calls=%async_computation.2 | async-start | bytes 1310720 | tf_op jit(solution)/shard_map/all_to_all | solution.py:379
  149.5 13.1 %all-to-all-done.2 = bf16[32,16,640]{2,1,0:T(8,128)(2,1)S(1)} async-done(((bf16[32,16,640]{2,1,0:T(8,128)(2,1)}), bf16[32,16,640]{2,1,0:T(8,128)(2,1)S(1)}, u32[]{:S(2)}, u32[]{:S(2)}) %all-to-all-start.2) | async-done | bytes 655392 | tf_op jit(solution)/shard_map/all_to_all | solution.py:379
  (90 shorter events, 32.7 us)
Async XLA Ops:
  4.7 9.8 %collective-permute-start.5 = (bf16[640,512]{1,0:T(8,128)(2,1)}, bf16[640,512]{1,0:T(8,128)(2,1)S(1)}, u32[]{:S(2)}, u32[]{:S(2)}) collective-permute-start(bf16[640,512]{1,0:T(8,128)(2,1)} %get-tuple-element.25.refs_0_), channel_id=1, source_target_pairs={{0,8},{8,0},{16,24},{24,16},{32,40},{40,32},{48,56},{56,48},{64,72... | collective-permute-start | bytes 1966088 | tf_op jit(solution)/shard_map/ppermute | solution.py:42
  7.9 13.7 %collective-permute-start.2 = (bf16[640,512]{1,0:T(8,128)(2,1)}, bf16[640,512]{1,0:T(8,128)(2,1)S(1)}, u32[]{:S(2)}, u32[]{:S(2)}) collective-permute-start(bf16[640,512]{1,0:T(8,128)(2,1)} %get-tuple-element.25.refs_0_), channel_id=1, source_target_pairs={{0,1},{1,2},{2,3},{3,4},{4,5},{5,6},{6,7},{7,0},{8,15},{9,8},{10,9... | collective-permute-start | bytes 1966088 | tf_op jit(solution)/shard_map/ppermute | solution.py:37
  11.7 9.8 %collective-permute-start = (bf16[512,512]{1,0:T(8,128)(2,1)}, bf16[512,512]{1,0:T(8,128)(2,1)S(1)}, u32[]{:S(2)}, u32[]{:S(2)}) collective-permute-start(bf16[512,512]{1,0:T(8,128)(2,1)} %get-tuple-element.26), channel_id=1, source_target_pairs={{0,64},{8,24},{16,80},{24,40},{32,96},{40,56},{48,112},{56,8},{64,... | collective-permute-start | bytes 1572872 | tf_op jit(solution)/shard_map/ppermute | solution.py:53
  13.0 8.5 %collective-permute-start.1 = (bf16[512,512]{1,0:T(8,128)(2,1)}, bf16[512,512]{1,0:T(8,128)(2,1)S(1)}, u32[]{:S(2)}, u32[]{:S(2)}) collective-permute-start(bf16[512,512]{1,0:T(8,128)(2,1)} %get-tuple-element.26), channel_id=1, source_target_pairs={{0,192},{8,56},{16,208},{24,8},{32,224},{40,24},{48,240},{56,40},{... | collective-permute-start | bytes 1572872 | tf_op jit(solution)/shard_map/ppermute | solution.py:53
  14.5 15.1 %collective-permute-start.6 = (bf16[640,512]{1,0:T(8,128)(2,1)S(1)}, bf16[640,512]{1,0:T(8,128)(2,1)S(1)}, u32[]{:S(2)}, u32[]{:S(2)}) collective-permute-start(bf16[640,512]{1,0:T(8,128)(2,1)S(1)} %collective-permute-done.5), channel_id=1, source_target_pairs={{0,1},{1,2},{2,3},{3,4},{4,5},{5,6},{6,7},{7,0},{8,15},{9,8},{10,9... | collective-permute-start | bytes 1966088 | tf_op jit(solution)/shard_map/ppermute | solution.py:37
  21.6 11.9 %collective-permute-start.7 = (bf16[640,512]{1,0:T(8,128)(2,1)S(1)}, bf16[640,512]{1,0:T(8,128)(2,1)S(1)}, u32[]{:S(2)}, u32[]{:S(2)}) collective-permute-start(bf16[640,512]{1,0:T(8,128)(2,1)S(1)} %collective-permute-done.2.refs_1_), channel_id=1, source_target_pairs={{0,1},{1,2},{2,3},{3,4},{4,5},{5,6},{6,7},{7,0},{8,15},{9,8},{10,9... | collective-permute-start | bytes 1966088 | tf_op jit(solution)/shard_map/ppermute | solution.py:37
  22.6 6.9 %collective-permute-start.3 = (bf16[256,512]{1,0:T(8,128)(2,1)S(1)}, bf16[256,512]{1,0:T(8,128)(2,1)S(1)}, u32[]{:S(2)}, u32[]{:S(2)}) collective-permute-start(bf16[256,512]{1,0:T(8,128)(2,1)S(1)} %slice.25), channel_id=1, source_target_pairs={{0,64},{8,24},{16,80},{24,40},{32,96},{40,56},{48,112},{56,8},{64,... | collective-permute-start | bytes 786440 | tf_op jit(solution)/shard_map/ppermute | solution.py:53
  29.7 27.7 %collective-permute-start.8 = (bf16[2048,512]{1,0:T(8,128)(2,1)S(1)}, bf16[2048,512]{1,0:T(8,128)(2,1)S(1)}, u32[]{:S(2)}, u32[]{:S(2)}) collective-permute-start(bf16[2048,512]{1,0:T(8,128)(2,1)S(1)} %constant_dynamic-update-slice_fusion.refs_8_.refs_0_), channel_id=1, source_target_pairs={{0,16},{8,72},{16,32},{24,88},{32,48},{40,104},{48,0},{56,120},{64... | collective-permute-start | bytes 6291464 | tf_op jit(solution)/shard_map/ppermute | solution.py:53
  33.5 25.5 %collective-permute-start.11 = (bf16[2048,512]{1,0:T(8,128)(2,1)S(1)}, bf16[2048,512]{1,0:T(8,128)(2,1)S(1)}, u32[]{:S(2)}, u32[]{:S(2)}) collective-permute-start(bf16[2048,512]{1,0:T(8,128)(2,1)S(1)} %constant_dynamic-update-slice_fusion.refs_8_.refs_0_), channel_id=1, source_target_pairs={{0,48},{8,200},{16,0},{24,216},{32,16},{40,232},{48,32},{56,248},{... | collective-permute-start | bytes 6291464 | tf_op jit(solution)/shard_map/ppermute | solution.py:53
  36.0 10.9 %collective-permute-start.13 = (bf16[640,512]{1,0:T(8,128)(2,1)S(1)}, bf16[640,512]{1,0:T(8,128)(2,1)S(1)}, u32[]{:S(2)}, u32[]{:S(2)}) collective-permute-start(bf16[640,512]{1,0:T(8,128)(2,1)S(1)} %collective-permute-done.6), channel_id=1, source_target_pairs={{0,1},{1,2},{2,3},{3,4},{4,5},{5,6},{6,7},{7,0},{8,15},{9,8},{10,9... | collective-permute-start | bytes 1966088 | tf_op jit(solution)/shard_map/ppermute | solution.py:37
  39.4 14.6 %collective-permute-start.9 = (bf16[640,512]{1,0:T(8,128)(2,1)S(1)}, bf16[640,512]{1,0:T(8,128)(2,1)S(1)}, u32[]{:S(2)}, u32[]{:S(2)}) collective-permute-start(bf16[640,512]{1,0:T(8,128)(2,1)S(1)} %collective-permute-done.7.refs_2_), channel_id=1, source_target_pairs={{0,1},{1,2},{2,3},{3,4},{4,5},{5,6},{6,7},{7,0},{8,15},{9,8},{10,9... | collective-permute-start | bytes 1966088 | tf_op jit(solution)/shard_map/ppermute | solution.py:37
  39.5 22.1 %collective-permute-start.16 = (bf16[640,512]{1,0:T(8,128)(2,1)S(1)}, bf16[640,512]{1,0:T(8,128)(2,1)S(1)}, u32[]{:S(2)}, u32[]{:S(2)}) collective-permute-start(bf16[640,512]{1,0:T(8,128)(2,1)S(1)} %collective-permute-done.6), channel_id=1, source_target_pairs={{0,8},{8,0},{16,24},{24,16},{32,40},{40,32},{48,56},{56,48},{64,72... | collective-permute-start | bytes 1966088 | tf_op jit(solution)/shard_map/ppermute | solution.py:42
  47.0 15.9 %collective-permute-start.14 = (bf16[640,512]{1,0:T(8,128)(2,1)S(1)}, bf16[640,512]{1,0:T(8,128)(2,1)S(1)}, u32[]{:S(2)}, u32[]{:S(2)}) collective-permute-start(bf16[640,512]{1,0:T(8,128)(2,1)S(1)} %collective-permute-done.13), channel_id=1, source_target_pairs={{0,1},{1,2},{2,3},{3,4},{4,5},{5,6},{6,7},{7,0},{8,15},{9,8},{10,9... | collective-permute-start | bytes 1966088 | tf_op jit(solution)/shard_map/ppermute | solution.py:37
  54.0 14.0 %collective-permute-start.15 = (bf16[640,512]{1,0:T(8,128)(2,1)S(1)}, bf16[640,512]{1,0:T(8,128)(2,1)S(1)}, u32[]{:S(2)}, u32[]{:S(2)}) collective-permute-start(bf16[640,512]{1,0:T(8,128)(2,1)S(1)} %collective-permute-done.9.refs_3_), channel_id=1, source_target_pairs={{0,1},{1,2},{2,3},{3,4},{4,5},{5,6},{6,7},{7,0},{8,15},{9,8},{10,9... | collective-permute-start | bytes 1966088 | tf_op jit(solution)/shard_map/ppermute | solution.py:37
  57.4 10.6 %collective-permute-start.17 = (bf16[640,512]{1,0:T(8,128)(2,1)S(1)}, bf16[640,512]{1,0:T(8,128)(2,1)S(1)}, u32[]{:S(2)}, u32[]{:S(2)}) collective-permute-start(bf16[640,512]{1,0:T(8,128)(2,1)S(1)} %collective-permute-done.13), channel_id=1, source_target_pairs={{0,8},{8,0},{16,24},{24,16},{32,40},{40,32},{48,56},{56,48},{64,72... | collective-permute-start | bytes 1966088 | tf_op jit(solution)/shard_map/ppermute | solution.py:42
  59.0 19.5 %collective-permute-start.19 = (bf16[2048,512]{1,0:T(8,128)(2,1)S(1)}, bf16[2048,512]{1,0:T(8,128)(2,1)S(1)}, u32[]{:S(2)}, u32[]{:S(2)}) collective-permute-start(bf16[2048,512]{1,0:T(8,128)(2,1)S(1)} %constant_dynamic-update-slice_fusion.refs_8_.refs_0_), channel_id=1, source_target_pairs={{0,8},{8,0},{16,24},{24,16},{32,40},{40,32},{48,56},{56,48},{64,72... | collective-permute-start | bytes 6291464 | tf_op jit(solution)/shard_map/ppermute | solution.py:42
  61.6 15.2 %collective-permute-start.10 = (bf16[1024,512]{1,0:T(8,128)(2,1)S(1)}, bf16[1024,512]{1,0:T(8,128)(2,1)S(1)}, u32[]{:S(2)}, u32[]{:S(2)}) collective-permute-start(bf16[1024,512]{1,0:T(8,128)(2,1)S(1)} %slice.27), channel_id=1, source_target_pairs={{0,16},{8,72},{16,32},{24,88},{32,48},{40,104},{48,0},{56,120},{64... | collective-permute-start | bytes 3145736 | tf_op jit(solution)/shard_map/ppermute | solution.py:53
  62.9 13.9 %collective-permute-start.12 = (bf16[1024,512]{1,0:T(8,128)(2,1)S(1)}, bf16[1024,512]{1,0:T(8,128)(2,1)S(1)}, u32[]{:S(2)}, u32[]{:S(2)}) collective-permute-start(bf16[1024,512]{1,0:T(8,128)(2,1)S(1)} %slice.31), channel_id=1, source_target_pairs={{0,48},{8,200},{16,0},{24,216},{32,16},{40,232},{48,32},{56,248},{... | collective-permute-start | bytes 3145736 | tf_op jit(solution)/shard_map/ppermute | solution.py:53
  68.0 15.2 %collective-permute-start.20 = (bf16[2048,512]{1,0:T(8,128)(2,1)S(1)}, bf16[2048,512]{1,0:T(8,128)(2,1)S(1)}, u32[]{:S(2)}, u32[]{:S(2)}) collective-permute-start(bf16[2048,512]{1,0:T(8,128)(2,1)S(1)} %collective-permute-done.8.refs_9_.refs_1_), channel_id=1, source_target_pairs={{0,8},{8,0},{16,24},{24,16},{32,40},{40,32},{48,56},{56,48},{64,72... | collective-permute-start | bytes 6291464 | tf_op jit(solution)/shard_map/ppermute | solution.py:42
  70.9 12.4 %collective-permute-start.21 = (bf16[2048,512]{1,0:T(8,128)(2,1)S(1)}, bf16[2048,512]{1,0:T(8,128)(2,1)S(1)}, u32[]{:S(2)}, u32[]{:S(2)}) collective-permute-start(bf16[2048,512]{1,0:T(8,128)(2,1)S(1)} %collective-permute-done.11.refs_10_.refs_2_), channel_id=1, source_target_pairs={{0,8},{8,0},{16,24},{24,16},{32,40},{40,32},{48,56},{56,48},{64,72... | collective-permute-start | bytes 6291464 | tf_op jit(solution)/shard_map/ppermute | solution.py:42
  76.8 6.4 %collective-permute-start.22 = (bf16[1024,512]{1,0:T(8,128)(2,1)S(1)}, bf16[1024,512]{1,0:T(8,128)(2,1)S(1)}, u32[]{:S(2)}, u32[]{:S(2)}) collective-permute-start(bf16[1024,512]{1,0:T(8,128)(2,1)S(1)} %collective-permute-done.10.refs_11_.refs_3_), channel_id=1, source_target_pairs={{0,8},{8,0},{16,24},{24,16},{32,40},{40,32},{48,56},{56,48},{64,72... | collective-permute-start | bytes 3145736 | tf_op jit(solution)/shard_map/ppermute | solution.py:42
  101.0 20.3 %all-to-all-start = ((bf16[32,16,640]{2,1,0:T(8,128)(2,1)}), bf16[32,16,640]{2,1,0:T(8,128)(2,1)S(1)}, u32[]{:S(2)}, u32[]{:S(2)}) async-start(bf16[32,16,640]{2,1,0:T(8,128)(2,1)} %bitcast.8), calls=%async_computation | async-start | bytes 1310720 | tf_op jit(solution)/shard_map/all_to_all | solution.py:375
  127.1 15.8 %all-to-all-start.1 = ((bf16[8,16,640]{2,1,0:T(8,128)(2,1)}), bf16[8,16,640]{2,1,0:T(8,128)(2,1)S(1)}, u32[]{:S(2)}, u32[]{:S(2)}) async-start(bf16[8,16,640]{2,1,0:T(8,128)(2,1)} %merge_project.1), calls=%async_computation.1 | async-start | bytes 327680 | tf_op jit(solution)/shard_map/all_to_all | solution.py:377
  145.4 17.1 %all-to-all-start.2 = ((bf16[32,16,640]{2,1,0:T(8,128)(2,1)}), bf16[32,16,640]{2,1,0:T(8,128)(2,1)S(1)}, u32[]{:S(2)}, u32[]{:S(2)}) async-start(bf16[32,16,640]{2,1,0:T(8,128)(2,1)} %add_rows.1), calls=%async_computation.2 | async-start | bytes 1310720 | tf_op jit(solution)/shard_map/all_to_all | solution.py:379
  (22 other events, 279.4 us)
